TPU v7x, 32 devices: a whole 2x2x4 slice. The times are simulated.
32 devices in a mesh: gx: 4 (over y, x), gy: 8 (over z, core).
Axes of the slice: x: 2, y: 2, z: 4, core: 2. Of those that a mesh axis runs over, the one named last changes fastest.
Arguments:
- right_side: float32 [32, 64, 256], P('gx', 'gy'), may hold values from -6 to 6
- coefficient: float32 [32, 64, 256], P('gx', 'gy'), may hold values from 0.5 to 4
Outputs:
- solution_field: float32 [32, 64, 256], P('gx', 'gy')
All inputs are finite; a program needn't handle non-finite values.
Results may differ from a plain program's by a relative error of at most 0.000078.
Values sent between devices are 32-bit elements; how exact they have to be, the bound alone decides.
No kernel may reach another device: no remote copies, remote signals or barrier semaphores. Data moves between devices by JAX's collectives and lax.ppermute only.
A program may use at most 64 MiB of HBM per device.

v0:
```python
import jax
import jax.numpy as jnp
from jax import lax
from jax.sharding import PartitionSpec as P

LEVELS = 3
SMOOTH = 2
COARSE_STEPS = 6


SMOOTH_LOW = 0.5
SMOOTH_HIGH = 2.0
COARSE_LOW = 0.05
COARSE_HIGH = 2.0


def with_halo(value, sides, width):
    for axis, dim in sides:
        count, length = (lax.axis_size(axis), value.shape[dim])
        up = [(i, (i + 1) % count) for i in range(count - 1)]
        down = [(j, i) for i, j in up]
        last = lax.slice_in_dim(value, length - width, length, axis=dim)
        leading = lax.slice_in_dim(value, 0, width, axis=dim)
        before = lax.ppermute(last, axis, up)
        after = lax.ppermute(leading, axis, down)
        value = jnp.concatenate([before, value, after], axis=dim)
    return value


def chebyshev(low_end, high_end, sweeps):
    middle = 0.5 * (high_end + low_end)
    half_span = 0.5 * (high_end - low_end)
    sig_ratio = middle / half_span
    rho_now = 1.0 / sig_ratio
    coeff_pairs = []
    for sweep_num in range(1, sweeps):
        rho_next = 1.0 / (2.0 * sig_ratio - rho_now)
        coeff_pairs.append((rho_next * rho_now, 2.0 * rho_next / half_span))
        rho_now = rho_next
    return (1.0 / middle, coeff_pairs)


def neighbours(padded):
    return [
        padded[2:, 1:-1, 1:-1],
        padded[:-2, 1:-1, 1:-1],
        padded[1:-1, 2:, 1:-1],
        padded[1:-1, :-2, 1:-1],
        padded[1:-1, 1:-1, 2:],
        padded[1:-1, 1:-1, :-2],
    ]


def face_weights(padded):
    centre = padded[1:-1, 1:-1, 1:-1]
    weights = [0.5 * (centre + beside_cell) for beside_cell in neighbours(padded)]
    diagonal = weights[0] + weights[1] + weights[2] + weights[3] + weights[4] + weights[5]
    return (weights, diagonal)


def apply_operator(padded, weights, diagonal):
    beside_list = neighbours(padded)
    summed = weights[0] * beside_list[0]
    for face_num in range(1, 6):
        summed = summed + weights[face_num] * beside_list[face_num]
    return diagonal * padded[1:-1, 1:-1, 1:-1] - summed


def restrict_sum(field):
    field = field[0::2] + field[1::2]
    field = field[:, 0::2] + field[:, 1::2]
    return field[:, :, 0::2] + field[:, :, 1::2]


def pad_depth(field):
    return jnp.pad(field, ((0, 0), (0, 0), (1, 1)))


def trim_sides(field, width):
    return field[width : field.shape[0] - width, width : field.shape[1] - width]


def inside_mask(brick_rows, brick_cols, width):
    first = (
        lax.axis_index("gx") * brick_rows
        + jnp.arange(brick_rows + 2 * width, dtype=jnp.int32)
        - width
    )
    second = (
        lax.axis_index("gy") * brick_cols
        + jnp.arange(brick_cols + 2 * width, dtype=jnp.int32)
        - width
    )
    good_rows = (first >= 0) & (first < brick_rows * lax.axis_size("gx"))
    good_cols = (second >= 0) & (second < brick_cols * lax.axis_size("gy"))
    return (good_rows[:, None] & good_cols[None, :])[:, :, None]


def prolong_axis(padded, axis_num):
    length = padded.shape[axis_num] - 2
    centre = lax.slice_in_dim(padded, 1, length + 1, axis=axis_num)
    before = lax.slice_in_dim(padded, 0, length, axis=axis_num)
    following = lax.slice_in_dim(padded, 2, length + 2, axis=axis_num)
    even_part = 0.75 * centre + 0.25 * before
    odd_part = 0.75 * centre + 0.25 * following
    joined = jnp.stack([even_part, odd_part], axis=axis_num + 1)
    new_shape = list(centre.shape)
    new_shape[axis_num] = 2 * length
    return joined.reshape(new_shape)


def depth_weights(coarse_len):
    row_ids = jnp.arange(coarse_len + 2, dtype=jnp.int32)[:, None]
    col_ids = jnp.arange(2 * coarse_len, dtype=jnp.int32)[None, :]
    home_row = col_ids // 2 + 1
    near_row = jnp.where(col_ids % 2 == 0, home_row - 1, home_row + 1)
    return jnp.where(row_ids == home_row, 0.75, 0.0).astype(jnp.float32) + jnp.where(
        row_ids == near_row, 0.25, 0.0
    ).astype(jnp.float32)


def prolong_local(padded):
    padded = prolong_axis(padded, 0)
    padded = prolong_axis(padded, 1)
    coarse_len = padded.shape[2] - 2
    flattened = padded.reshape(-1, coarse_len + 2)
    fine_vals = jnp.dot(
        flattened,
        depth_weights(coarse_len),
        precision=lax.Precision.HIGHEST,
        preferred_element_type=jnp.float32,
    )
    return fine_vals.reshape(padded.shape[0], padded.shape[1], 2 * coarse_len)


def residual_each(iterate, source, weights, diagonal):
    padded = pad_depth(with_halo(iterate, (("gx", 0), ("gy", 1)), 1))
    return source - apply_operator(padded, weights, diagonal)


def smooth_deep(start_ext, source_ext, weights_ext, diagonal_ext, inverse_ext, inside_masks):
    inv_mid, coeff_pairs = chebyshev(SMOOTH_LOW, SMOOTH_HIGH, SMOOTH)
    if start_ext is None:
        residue = source_ext
    else:
        residue = source_ext - apply_operator(pad_depth(start_ext), weights_ext, diagonal_ext)
    step_dir = residue * inverse_ext * inv_mid
    iterate = step_dir if start_ext is None else trim_sides(start_ext, 1) + step_dir
    iterate = jnp.where(inside_masks[0], iterate, 0.0)
    keep_part, push_part = coeff_pairs[0]
    weights_now = [trim_sides(weight_one, 1) for weight_one in weights_ext]
    residue = trim_sides(source_ext, 1) - apply_operator(
        pad_depth(iterate), weights_now, trim_sides(diagonal_ext, 1)
    )
    step_dir = keep_part * trim_sides(step_dir, 1) + push_part * (
        residue * trim_sides(inverse_ext, 1)
    )
    iterate = jnp.where(inside_masks[1], trim_sides(iterate, 1) + step_dir, 0.0)
    return iterate


def smooth_whole(source, coeffs):
    weights, diagonal = face_weights(jnp.pad(coeffs, 1))
    inverse = 1.0 / diagonal
    inv_mid, coeff_pairs = chebyshev(COARSE_LOW, COARSE_HIGH, COARSE_STEPS)
    step_dir = source * inverse * inv_mid
    iterate = step_dir
    for keep_part, push_part in coeff_pairs:
        residue = source - apply_operator(jnp.pad(iterate, 1), weights, diagonal)
        step_dir = keep_part * step_dir + push_part * (residue * inverse)
        iterate = iterate + step_dir
    residue = source - apply_operator(jnp.pad(iterate, 1), weights, diagonal)
    ones_image = apply_operator(jnp.pad(jnp.ones_like(source), 1), weights, diagonal)
    return iterate + jnp.sum(residue) / jnp.sum(ones_image)


def assemble(pieces, brick_rows, brick_cols, brick_depth):
    along_x = lax.axis_size("gx")
    along_y = lax.axis_size("gy")
    blocks = pieces.reshape(along_x, along_y, brick_rows, brick_cols, brick_depth)
    return blocks.transpose(0, 2, 1, 3, 4).reshape(
        along_x * brick_rows, along_y * brick_cols, brick_depth
    )


def coarse_solve(source, coeffs):
    brick_rows, brick_cols, brick_depth = source.shape
    pieces = (
        lax.all_gather(source[None], ("gx", "gy"), axis=0, tiled=True),
        lax.all_gather(coeffs[None], ("gx", "gy"), axis=0, tiled=True),
    )
    whole_source = assemble(pieces[0], brick_rows, brick_cols, brick_depth)
    whole_coeffs = assemble(pieces[1], brick_rows, brick_cols, brick_depth)
    iterate = smooth_whole(whole_source, whole_coeffs)
    return lax.dynamic_slice(
        iterate,
        (lax.axis_index("gx") * brick_rows, lax.axis_index("gy") * brick_cols, 0),
        (brick_rows, brick_cols, brick_depth),
    )


def body(right_side, coefficient):
    source = right_side
    coeffs = coefficient
    stored = []
    for level_num in range(LEVELS - 1):
        brick_rows, brick_cols, brick_depth = source.shape
        coeff_ext = pad_depth(with_halo(coeffs, (("gx", 0), ("gy", 1)), SMOOTH))
        source_ext = with_halo(source, (("gx", 0), ("gy", 1)), SMOOTH - 1)
        weights_ext, diagonal_ext = face_weights(coeff_ext)
        inside_masks = [
            inside_mask(brick_rows, brick_cols, SMOOTH - 1 - sweep_num)
            for sweep_num in range(SMOOTH)
        ]
        inverse_ext = jnp.where(
            inside_masks[0], 1.0 / jnp.where(inside_masks[0], diagonal_ext, 1.0), 0.0
        )
        iterate = smooth_deep(
            None, source_ext, weights_ext, diagonal_ext, inverse_ext, inside_masks
        )
        weights = [trim_sides(weight_one, SMOOTH - 1) for weight_one in weights_ext]
        diagonal = trim_sides(diagonal_ext, SMOOTH - 1)
        inverse = trim_sides(inverse_ext, SMOOTH - 1)
        extended = (source_ext, weights_ext, diagonal_ext, inverse_ext, inside_masks)
        residue = residual_each(iterate, source, weights, diagonal)
        stored.append((iterate, source, weights, diagonal, inverse, extended))
        source = 0.5 * restrict_sum(residue)
        coeffs = 0.125 * restrict_sum(coeffs)
    coarse = coarse_solve(source, coeffs)
    for iterate, source, weights, diagonal, inverse, extended in reversed(stored):
        padded = pad_depth(with_halo(coarse, (("gx", 0), ("gy", 1)), 1))
        iterate = iterate + prolong_local(padded)
        start_ext = with_halo(iterate, (("gx", 0), ("gy", 1)), SMOOTH)
        source_ext, weights_ext, diagonal_ext, inverse_ext, inside_masks = extended
        coarse = smooth_deep(
            start_ext, source_ext, weights_ext, diagonal_ext, inverse_ext, inside_masks
        )
    return coarse


def solution(mesh):
    placed = (P("gx", "gy", None), P("gx", "gy", None))
    return jax.shard_map(
        body, mesh=mesh, in_specs=placed, out_specs=P("gx", "gy", None), check_vma=False
    )
```

profile of v0, /device:TPU:0, one launch (start us, length us, event | category | flops | bytes accessed | tf_op | source)
XLA Modules:
  0.0 233.8 jit_solution(7657790477419757659)
XLA Ops:
  0.8 4.8 %collective-permute-start.4 = (f32[2,8,256]{2,1,0:T(8,128)S(1)}, f32[2,8,256]{2,1,0:T(8,128)S(1)}, u32[]{:S(2)}, u32[]{:S(2)}) collective-permute-start(f32[2,8,256]{2,1,0:T(8,128)S(1)} %get-tuple-element.62), channel_id=1, source_target_pairs={{0,8},{8,16},{16,24},{1,9},{9,17},{17,25},{2,10},{10,18},{18,26},{... | collective-permute-start | bytes 49160 | tf_op jit(solution)/shard_map/ppermute | solution.py:24
  6.9 4.5 %collective-permute-start = (f32[1,8,256]{2,1,0:T(8,128)S(1)}, f32[1,8,256]{2,1,0:T(8,128)S(1)}, u32[]{:S(2)}, u32[]{:S(2)}) collective-permute-start(f32[1,8,256]{2,1,0:T(8,128)S(1)} %get-tuple-element.60), channel_id=1, source_target_pairs={{0,8},{8,16},{16,24},{1,9},{9,17},{17,25},{2,10},{10,18},{18,26},{... | collective-permute-start | bytes 24584 | tf_op jit(solution)/shard_map/ppermute | solution.py:24
  14.4 4.9 %collective-permute-start.16 = (f32[2,4,128]{2,1,0:T(4,128)S(1)}, f32[2,4,128]{2,1,0:T(4,128)S(1)}, u32[]{:S(2)}, u32[]{:S(2)}) collective-permute-start(f32[2,4,128]{2,1,0:T(4,128)S(1)} %get-tuple-element.87), channel_id=1, source_target_pairs={{0,8},{8,16},{16,24},{1,9},{9,17},{17,25},{2,10},{10,18},{18,26},{... | collective-permute-start | bytes 12296 | tf_op jit(solution)/shard_map/ppermute | solution.py:24
  24.9 4.8 %collective-permute-start.2 = (f32[10,1,256]{2,1,0:T(1,128)S(1)}, f32[10,1,256]{2,1,0:T(1,128)S(1)}, u32[]{:S(2)}, u32[]{:S(2)}) collective-permute-start(f32[10,1,256]{2,1,0:T(1,128)S(1)} %get-tuple-element.53), channel_id=1, source_target_pairs={{0,1},{1,2},{2,3},{3,4},{4,5},{5,6},{6,7},{8,9},{9,10},{10,11},{11... | collective-permute-start | bytes 30728 | tf_op jit(solution)/shard_map/ppermute | solution.py:24
  35.6 6.1 %collective-permute-start.9 = (f32[1,8,256]{2,1,0:T(8,128)S(1)}, f32[1,8,256]{2,1,0:T(8,128)S(1)}, u32[]{:S(2)}, u32[]{:S(2)}) collective-permute-start(f32[1,8,256]{2,1,0:T(8,128)S(1)} %get-tuple-element.57), channel_id=1, source_target_pairs={{0,8},{8,16},{16,24},{1,9},{9,17},{17,25},{2,10},{10,18},{18,26},{... | collective-permute-start | bytes 24584 | tf_op jit(solution)/shard_map/ppermute | solution.py:24
  44.4 4.1 %collective-permute-start.11 = (f32[10,1,256]{2,1,0:T(1,128)S(1)}, f32[10,1,256]{2,1,0:T(1,128)S(1)}, u32[]{:S(2)}, u32[]{:S(2)}) collective-permute-start(f32[10,1,256]{2,1,0:T(1,128)S(1)} %get-tuple-element.51), channel_id=1, source_target_pairs={{0,1},{1,2},{2,3},{3,4},{4,5},{5,6},{6,7},{8,9},{9,10},{10,11},{11... | collective-permute-start | bytes 30728 | tf_op jit(solution)/shard_map/ppermute | solution.py:24
  48.5 3.6 %collective-permute-start.18 = (f32[8,2,128]{2,1,0:T(2,128)S(1)}, f32[8,2,128]{2,1,0:T(2,128)S(1)}, u32[]{:S(2)}, u32[]{:S(2)}) collective-permute-start(f32[8,2,128]{2,1,0:T(2,128)S(1)} %get-tuple-element.69), channel_id=1, source_target_pairs={{0,1},{1,2},{2,3},{3,4},{4,5},{5,6},{6,7},{8,9},{9,10},{10,11},{11... | collective-permute-start | bytes 24584 | tf_op jit(solution)/shard_map/ppermute | solution.py:24
  54.6 4.8 %collective-permute-start.12 = (f32[1,4,128]{2,1,0:T(4,128)S(1)}, f32[1,4,128]{2,1,0:T(4,128)S(1)}, u32[]{:S(2)}, u32[]{:S(2)}) collective-permute-start(f32[1,4,128]{2,1,0:T(4,128)S(1)} %get-tuple-element.90), channel_id=1, source_target_pairs={{0,8},{8,16},{16,24},{1,9},{9,17},{17,25},{2,10},{10,18},{18,26},{... | collective-permute-start | bytes 6152 | tf_op jit(solution)/shard_map/ppermute | solution.py:24
  60.8 5.0 %collective-permute-done.13 = f32[1,4,128]{2,1,0:T(4,128)S(1)} collective-permute-done((f32[1,4,128]{2,1,0:T(4,128)S(1)}, f32[1,4,128]{2,1,0:T(4,128)S(1)}, u32[]{:S(2)}, u32[]{:S(2)}) %collective-permute-start.13) | collective-permute-done | bytes 2080 | tf_op jit(solution)/shard_map/ppermute | solution.py:25
  69.2 3.4 %collective-permute-done.15 = f32[6,1,128]{2,1,0:T(1,128)S(1)} collective-permute-done((f32[6,1,128]{2,1,0:T(1,128)S(1)}, f32[6,1,128]{2,1,0:T(1,128)S(1)}, u32[]{:S(2)}, u32[]{:S(2)}) %collective-permute-start.15) | collective-permute-done | bytes 3104 | tf_op jit(solution)/shard_map/ppermute | solution.py:25
  74.1 5.4 %collective-permute-start.21 = (f32[1,4,128]{2,1,0:T(4,128)S(1)}, f32[1,4,128]{2,1,0:T(4,128)S(1)}, u32[]{:S(2)}, u32[]{:S(2)}) collective-permute-start(f32[1,4,128]{2,1,0:T(4,128)S(1)} %get-tuple-element.88), channel_id=1, source_target_pairs={{0,8},{8,16},{16,24},{1,9},{9,17},{17,25},{2,10},{10,18},{18,26},{... | collective-permute-start | bytes 6152 | tf_op jit(solution)/shard_map/ppermute | solution.py:24
  82.2 4.0 %collective-permute-start.23 = (f32[6,1,128]{2,1,0:T(1,128)S(1)}, f32[6,1,128]{2,1,0:T(1,128)S(1)}, u32[]{:S(2)}, u32[]{:S(2)}) collective-permute-start(f32[6,1,128]{2,1,0:T(1,128)S(1)} %get-tuple-element.73), channel_id=1, source_target_pairs={{0,1},{1,2},{2,3},{3,4},{4,5},{5,6},{6,7},{8,9},{9,10},{10,11},{11... | collective-permute-start | bytes 9224 | tf_op jit(solution)/shard_map/ppermute | solution.py:24
  86.2 42.5 %all-gather.1 = f32[64,2,64]{2,1,0:T(2,128)S(1)} all-gather(f32[2,2,64]{2,1,0:T(2,128)S(1)} %add_multiply_fusion.2), channel_id=3, replica_groups=mesh['gx'=4,'gy'=8] {'gx','gy'}, dimensions={0}, use_global_device_ids=true | all-gather | bytes 33792 | tf_op jit(solution)/shard_map/all_gather | solution.py:190
  129.4 36.9 %all-gather = f32[64,2,64]{2,1,0:T(2,128)S(1)} all-gather(f32[2,2,64]{2,1,0:T(2,128)S(1)} %add_multiply_fusion.3), channel_id=2, replica_groups=mesh['gx'=4,'gy'=8] {'gx','gy'}, dimensions={0}, use_global_device_ids=true | all-gather | bytes 33792 | tf_op jit(solution)/shard_map/all_gather | solution.py:189
  171.9 5.4 %collective-permute-done.25 = f32[1,2,64]{2,1,0:T(2,128)S(1)} collective-permute-done((f32[1,2,64]{2,1,0:T(2,128)S(1)}, f32[1,2,64]{2,1,0:T(2,128)S(1)}, u32[]{:S(2)}, u32[]{:S(2)}) %collective-permute-start.25) | collective-permute-done | bytes 544 | tf_op jit(solution)/shard_map/ppermute | solution.py:25
  180.0 3.6 %collective-permute-done.27 = f32[4,1,64]{2,1,0:T(1,128)S(1)} collective-permute-done((f32[4,1,64]{2,1,0:T(1,128)S(1)}, f32[4,1,64]{2,1,0:T(1,128)S(1)}, u32[]{:S(2)}, u32[]{:S(2)}) %collective-permute-start.27) | collective-permute-done | bytes 1056 | tf_op jit(solution)/shard_map/ppermute | solution.py:25
  184.0 4.8 %collective-permute-start.28 = (f32[2,4,128]{2,1,0:T(4,128)S(1)}, f32[2,4,128]{2,1,0:T(4,128)S(1)}, u32[]{:S(2)}, u32[]{:S(2)}) collective-permute-start(f32[2,4,128]{2,1,0:T(4,128)S(1)} %get-tuple-element.79), channel_id=1, source_target_pairs={{0,8},{8,16},{16,24},{1,9},{9,17},{17,25},{2,10},{10,18},{18,26},{... | collective-permute-start | bytes 12296 | tf_op jit(solution)/shard_map/ppermute | solution.py:24
  190.1 4.2 %collective-permute-done.29 = f32[2,4,128]{2,1,0:T(4,128)S(1)} collective-permute-done((f32[2,4,128]{2,1,0:T(4,128)S(1)}, f32[2,4,128]{2,1,0:T(4,128)S(1)}, u32[]{:S(2)}, u32[]{:S(2)}) %collective-permute-start.29) | collective-permute-done | bytes 4128 | tf_op jit(solution)/shard_map/ppermute | solution.py:25
  194.3 2.8 %collective-permute-start.30 = (f32[8,2,128]{2,1,0:T(2,128)S(1)}, f32[8,2,128]{2,1,0:T(2,128)S(1)}, u32[]{:S(2)}, u32[]{:S(2)}) collective-permute-start(f32[8,2,128]{2,1,0:T(2,128)S(1)} %get-tuple-element.67), channel_id=1, source_target_pairs={{0,1},{1,2},{2,3},{3,4},{4,5},{5,6},{6,7},{8,9},{9,10},{10,11},{11... | collective-permute-start | bytes 24584 | tf_op jit(solution)/shard_map/ppermute | solution.py:24
  201.4 2.8 %collective-permute-start.32 = (f32[1,4,128]{2,1,0:T(4,128)S(1)}, f32[1,4,128]{2,1,0:T(4,128)S(1)}, u32[]{:S(2)}, u32[]{:S(2)}) collective-permute-start(f32[1,4,128]{2,1,0:T(4,128)S(1)} %get-tuple-element.77), channel_id=1, source_target_pairs={{0,8},{8,16},{16,24},{1,9},{9,17},{17,25},{2,10},{10,18},{18,26},{... | collective-permute-start | bytes 6152 | tf_op jit(solution)/shard_map/ppermute | solution.py:24
  205.6 4.2 %collective-permute-done.33 = f32[1,4,128]{2,1,0:T(4,128)S(1)} collective-permute-done((f32[1,4,128]{2,1,0:T(4,128)S(1)}, f32[1,4,128]{2,1,0:T(4,128)S(1)}, u32[]{:S(2)}, u32[]{:S(2)}) %collective-permute-start.33) | collective-permute-done | bytes 2080 | tf_op jit(solution)/shard_map/ppermute | solution.py:25
  209.8 2.9 %collective-permute-start.34 = (f32[6,1,128]{2,1,0:T(1,128)S(1)}, f32[6,1,128]{2,1,0:T(1,128)S(1)}, u32[]{:S(2)}, u32[]{:S(2)}) collective-permute-start(f32[6,1,128]{2,1,0:T(1,128)S(1)} %get-tuple-element.71), channel_id=1, source_target_pairs={{0,1},{1,2},{2,3},{3,4},{4,5},{5,6},{6,7},{8,9},{9,10},{10,11},{11... | collective-permute-start | bytes 9224 | tf_op jit(solution)/shard_map/ppermute | solution.py:24
  221.6 4.2 %collective-permute-done.37 = f32[2,8,256]{2,1,0:T(8,128)S(1)} collective-permute-done((f32[2,8,256]{2,1,0:T(8,128)S(1)}, f32[2,8,256]{2,1,0:T(8,128)S(1)}, u32[]{:S(2)}, u32[]{:S(2)}) %collective-permute-start.37) | collective-permute-done | bytes 16416 | tf_op jit(solution)/shard_map/ppermute | solution.py:25
  225.8 2.8 %collective-permute-start.38 = (f32[12,2,256]{2,1,0:T(2,128)S(1)}, f32[12,2,256]{2,1,0:T(2,128)S(1)}, u32[]{:S(2)}, u32[]{:S(2)}) collective-permute-start(f32[12,2,256]{2,1,0:T(2,128)S(1)} %get-tuple-element.47), channel_id=1, source_target_pairs={{0,1},{1,2},{2,3},{3,4},{4,5},{5,6},{6,7},{8,9},{9,10},{10,11},{11... | collective-permute-start | bytes 73736 | tf_op jit(solution)/shard_map/ppermute | solution.py:24
  (175 shorter events, 58.4 us)
Async XLA Ops:
  0.8 20.6 %collective-permute-start.4 = (f32[2,8,256]{2,1,0:T(8,128)S(1)}, f32[2,8,256]{2,1,0:T(8,128)S(1)}, u32[]{:S(2)}, u32[]{:S(2)}) collective-permute-start(f32[2,8,256]{2,1,0:T(8,128)S(1)} %get-tuple-element.62), channel_id=1, source_target_pairs={{0,8},{8,16},{16,24},{1,9},{9,17},{17,25},{2,10},{10,18},{18,26},{... | collective-permute-start | bytes 49160 | tf_op jit(solution)/shard_map/ppermute | solution.py:24
  5.6 16.6 %collective-permute-start.5 = (f32[2,8,256]{2,1,0:T(8,128)S(1)}, f32[2,8,256]{2,1,0:T(8,128)S(1)}, u32[]{:S(2)}, u32[]{:S(2)}) collective-permute-start(f32[2,8,256]{2,1,0:T(8,128)S(1)} %get-tuple-element.61), channel_id=1, source_target_pairs={{8,0},{16,8},{24,16},{9,1},{17,9},{25,17},{10,2},{18,10},{26,18},{... | collective-permute-start | bytes 49160 | tf_op jit(solution)/shard_map/ppermute | solution.py:25
  6.9 13.1 %collective-permute-start = (f32[1,8,256]{2,1,0:T(8,128)S(1)}, f32[1,8,256]{2,1,0:T(8,128)S(1)}, u32[]{:S(2)}, u32[]{:S(2)}) collective-permute-start(f32[1,8,256]{2,1,0:T(8,128)S(1)} %get-tuple-element.60), channel_id=1, source_target_pairs={{0,8},{8,16},{16,24},{1,9},{9,17},{17,25},{2,10},{10,18},{18,26},{... | collective-permute-start | bytes 24584 | tf_op jit(solution)/shard_map/ppermute | solution.py:24
  11.5 9.9 %collective-permute-start.1 = (f32[1,8,256]{2,1,0:T(8,128)S(1)}, f32[1,8,256]{2,1,0:T(8,128)S(1)}, u32[]{:S(2)}, u32[]{:S(2)}) collective-permute-start(f32[1,8,256]{2,1,0:T(8,128)S(1)} %get-tuple-element.59), channel_id=1, source_target_pairs={{8,0},{16,8},{24,16},{9,1},{17,9},{25,17},{10,2},{18,10},{26,18},{... | collective-permute-start | bytes 24584 | tf_op jit(solution)/shard_map/ppermute | solution.py:25
  14.4 27.3 %collective-permute-start.16 = (f32[2,4,128]{2,1,0:T(4,128)S(1)}, f32[2,4,128]{2,1,0:T(4,128)S(1)}, u32[]{:S(2)}, u32[]{:S(2)}) collective-permute-start(f32[2,4,128]{2,1,0:T(4,128)S(1)} %get-tuple-element.87), channel_id=1, source_target_pairs={{0,8},{8,16},{16,24},{1,9},{9,17},{17,25},{2,10},{10,18},{18,26},{... | collective-permute-start | bytes 12296 | tf_op jit(solution)/shard_map/ppermute | solution.py:24
  20.1 21.7 %collective-permute-start.17 = (f32[2,4,128]{2,1,0:T(4,128)S(1)}, f32[2,4,128]{2,1,0:T(4,128)S(1)}, u32[]{:S(2)}, u32[]{:S(2)}) collective-permute-start(f32[2,4,128]{2,1,0:T(4,128)S(1)} %get-tuple-element.86), channel_id=1, source_target_pairs={{8,0},{16,8},{24,16},{9,1},{17,9},{25,17},{10,2},{18,10},{26,18},{... | collective-permute-start | bytes 12296 | tf_op jit(solution)/shard_map/ppermute | solution.py:25
  22.3 7.5 %collective-permute-start.6 = (f32[12,2,256]{2,1,0:T(2,128)S(1)}, f32[12,2,256]{2,1,0:T(2,128)S(1)}, u32[]{:S(2)}, u32[]{:S(2)}) collective-permute-start(f32[12,2,256]{2,1,0:T(2,128)S(1)} %get-tuple-element.49), channel_id=1, source_target_pairs={{0,1},{1,2},{2,3},{3,4},{4,5},{5,6},{6,7},{8,9},{9,10},{10,11},{11... | collective-permute-start | bytes 73736 | tf_op jit(solution)/shard_map/ppermute | solution.py:24
  23.6 7.5 %collective-permute-start.7 = (f32[12,2,256]{2,1,0:T(2,128)S(1)}, f32[12,2,256]{2,1,0:T(2,128)S(1)}, u32[]{:S(2)}, u32[]{:S(2)}) collective-permute-start(f32[12,2,256]{2,1,0:T(2,128)S(1)} %get-tuple-element.50), channel_id=1, source_target_pairs={{1,0},{2,1},{3,2},{4,3},{5,4},{6,5},{7,6},{9,8},{10,9},{11,10},{12... | collective-permute-start | bytes 73736 | tf_op jit(solution)/shard_map/ppermute | solution.py:25
  24.9 6.4 %collective-permute-start.2 = (f32[10,1,256]{2,1,0:T(1,128)S(1)}, f32[10,1,256]{2,1,0:T(1,128)S(1)}, u32[]{:S(2)}, u32[]{:S(2)}) collective-permute-start(f32[10,1,256]{2,1,0:T(1,128)S(1)} %get-tuple-element.53), channel_id=1, source_target_pairs={{0,1},{1,2},{2,3},{3,4},{4,5},{5,6},{6,7},{8,9},{9,10},{10,11},{11... | collective-permute-start | bytes 30728 | tf_op jit(solution)/shard_map/ppermute | solution.py:24
  34.3 7.4 %collective-permute-start.8 = (f32[1,8,256]{2,1,0:T(8,128)S(1)}, f32[1,8,256]{2,1,0:T(8,128)S(1)}, u32[]{:S(2)}, u32[]{:S(2)}) collective-permute-start(f32[1,8,256]{2,1,0:T(8,128)S(1)} %get-tuple-element.58), channel_id=1, source_target_pairs={{8,0},{16,8},{24,16},{9,1},{17,9},{25,17},{10,2},{18,10},{26,18},{... | collective-permute-start | bytes 24584 | tf_op jit(solution)/shard_map/ppermute | solution.py:25
  35.6 7.4 %collective-permute-start.9 = (f32[1,8,256]{2,1,0:T(8,128)S(1)}, f32[1,8,256]{2,1,0:T(8,128)S(1)}, u32[]{:S(2)}, u32[]{:S(2)}) collective-permute-start(f32[1,8,256]{2,1,0:T(8,128)S(1)} %get-tuple-element.57), channel_id=1, source_target_pairs={{0,8},{8,16},{16,24},{1,9},{9,17},{17,25},{2,10},{10,18},{18,26},{... | collective-permute-start | bytes 24584 | tf_op jit(solution)/shard_map/ppermute | solution.py:24
  43.1 10.4 %collective-permute-start.10 = (f32[10,1,256]{2,1,0:T(1,128)S(1)}, f32[10,1,256]{2,1,0:T(1,128)S(1)}, u32[]{:S(2)}, u32[]{:S(2)}) collective-permute-start(f32[10,1,256]{2,1,0:T(1,128)S(1)} %get-tuple-element.52), channel_id=1, source_target_pairs={{1,0},{2,1},{3,2},{4,3},{5,4},{6,5},{7,6},{9,8},{10,9},{11,10},{12... | collective-permute-start | bytes 30728 | tf_op jit(solution)/shard_map/ppermute | solution.py:25
  44.4 9.1 %collective-permute-start.11 = (f32[10,1,256]{2,1,0:T(1,128)S(1)}, f32[10,1,256]{2,1,0:T(1,128)S(1)}, u32[]{:S(2)}, u32[]{:S(2)}) collective-permute-start(f32[10,1,256]{2,1,0:T(1,128)S(1)} %get-tuple-element.51), channel_id=1, source_target_pairs={{0,1},{1,2},{2,3},{3,4},{4,5},{5,6},{6,7},{8,9},{9,10},{10,11},{11... | collective-permute-start | bytes 30728 | tf_op jit(solution)/shard_map/ppermute | solution.py:24
  48.5 12.2 %collective-permute-start.18 = (f32[8,2,128]{2,1,0:T(2,128)S(1)}, f32[8,2,128]{2,1,0:T(2,128)S(1)}, u32[]{:S(2)}, u32[]{:S(2)}) collective-permute-start(f32[8,2,128]{2,1,0:T(2,128)S(1)} %get-tuple-element.69), channel_id=1, source_target_pairs={{0,1},{1,2},{2,3},{3,4},{4,5},{5,6},{6,7},{8,9},{9,10},{10,11},{11... | collective-permute-start | bytes 24584 | tf_op jit(solution)/shard_map/ppermute | solution.py:24
  52.1 8.6 %collective-permute-start.19 = (f32[8,2,128]{2,1,0:T(2,128)S(1)}, f32[8,2,128]{2,1,0:T(2,128)S(1)}, u32[]{:S(2)}, u32[]{:S(2)}) collective-permute-start(f32[8,2,128]{2,1,0:T(2,128)S(1)} %get-tuple-element.70), channel_id=1, source_target_pairs={{1,0},{2,1},{3,2},{4,3},{5,4},{6,5},{7,6},{9,8},{10,9},{11,10},{12... | collective-permute-start | bytes 24584 | tf_op jit(solution)/shard_map/ppermute | solution.py:25
  54.6 6.2 %collective-permute-start.12 = (f32[1,4,128]{2,1,0:T(4,128)S(1)}, f32[1,4,128]{2,1,0:T(4,128)S(1)}, u32[]{:S(2)}, u32[]{:S(2)}) collective-permute-start(f32[1,4,128]{2,1,0:T(4,128)S(1)} %get-tuple-element.90), channel_id=1, source_target_pairs={{0,8},{8,16},{16,24},{1,9},{9,17},{17,25},{2,10},{10,18},{18,26},{... | collective-permute-start | bytes 6152 | tf_op jit(solution)/shard_map/ppermute | solution.py:24
  59.4 6.4 %collective-permute-start.13 = (f32[1,4,128]{2,1,0:T(4,128)S(1)}, f32[1,4,128]{2,1,0:T(4,128)S(1)}, u32[]{:S(2)}, u32[]{:S(2)}) collective-permute-start(f32[1,4,128]{2,1,0:T(4,128)S(1)} %get-tuple-element.91), channel_id=1, source_target_pairs={{8,0},{16,8},{24,16},{9,1},{17,9},{25,17},{10,2},{18,10},{26,18},{... | collective-permute-start | bytes 6152 | tf_op jit(solution)/shard_map/ppermute | solution.py:25
  72.8 6.8 %collective-permute-start.20 = (f32[1,4,128]{2,1,0:T(4,128)S(1)}, f32[1,4,128]{2,1,0:T(4,128)S(1)}, u32[]{:S(2)}, u32[]{:S(2)}) collective-permute-start(f32[1,4,128]{2,1,0:T(4,128)S(1)} %get-tuple-element.89), channel_id=1, source_target_pairs={{8,0},{16,8},{24,16},{9,1},{17,9},{25,17},{10,2},{18,10},{26,18},{... | collective-permute-start | bytes 6152 | tf_op jit(solution)/shard_map/ppermute | solution.py:25
  74.1 6.7 %collective-permute-start.21 = (f32[1,4,128]{2,1,0:T(4,128)S(1)}, f32[1,4,128]{2,1,0:T(4,128)S(1)}, u32[]{:S(2)}, u32[]{:S(2)}) collective-permute-start(f32[1,4,128]{2,1,0:T(4,128)S(1)} %get-tuple-element.88), channel_id=1, source_target_pairs={{0,8},{8,16},{16,24},{1,9},{9,17},{17,25},{2,10},{10,18},{18,26},{... | collective-permute-start | bytes 6152 | tf_op jit(solution)/shard_map/ppermute | solution.py:24
  80.9 47.9 %collective-permute-start.22 = (f32[6,1,128]{2,1,0:T(1,128)S(1)}, f32[6,1,128]{2,1,0:T(1,128)S(1)}, u32[]{:S(2)}, u32[]{:S(2)}) collective-permute-start(f32[6,1,128]{2,1,0:T(1,128)S(1)} %get-tuple-element.74), channel_id=1, source_target_pairs={{1,0},{2,1},{3,2},{4,3},{5,4},{6,5},{7,6},{9,8},{10,9},{11,10},{12... | collective-permute-start | bytes 9224 | tf_op jit(solution)/shard_map/ppermute | solution.py:25
  82.2 46.6 %collective-permute-start.23 = (f32[6,1,128]{2,1,0:T(1,128)S(1)}, f32[6,1,128]{2,1,0:T(1,128)S(1)}, u32[]{:S(2)}, u32[]{:S(2)}) collective-permute-start(f32[6,1,128]{2,1,0:T(1,128)S(1)} %get-tuple-element.73), channel_id=1, source_target_pairs={{0,1},{1,2},{2,3},{3,4},{4,5},{5,6},{6,7},{8,9},{9,10},{10,11},{11... | collective-permute-start | bytes 9224 | tf_op jit(solution)/shard_map/ppermute | solution.py:24
  170.6 6.7 %collective-permute-start.25 = (f32[1,2,64]{2,1,0:T(2,128)S(1)}, f32[1,2,64]{2,1,0:T(2,128)S(1)}, u32[]{:S(2)}, u32[]{:S(2)}) collective-permute-start(f32[1,2,64]{2,1,0:T(2,128)S(1)} %get-tuple-element.95), channel_id=1, source_target_pairs={{8,0},{16,8},{24,16},{9,1},{17,9},{25,17},{10,2},{18,10},{26,18},{... | collective-permute-start | bytes 1544 | tf_op jit(solution)/shard_map/ppermute | solution.py:25
  184.0 6.1 %collective-permute-start.28 = (f32[2,4,128]{2,1,0:T(4,128)S(1)}, f32[2,4,128]{2,1,0:T(4,128)S(1)}, u32[]{:S(2)}, u32[]{:S(2)}) collective-permute-start(f32[2,4,128]{2,1,0:T(4,128)S(1)} %get-tuple-element.79), channel_id=1, source_target_pairs={{0,8},{8,16},{16,24},{1,9},{9,17},{17,25},{2,10},{10,18},{18,26},{... | collective-permute-start | bytes 12296 | tf_op jit(solution)/shard_map/ppermute | solution.py:24
  220.1 5.6 %collective-permute-start.37 = (f32[2,8,256]{2,1,0:T(8,128)S(1)}, f32[2,8,256]{2,1,0:T(8,128)S(1)}, u32[]{:S(2)}, u32[]{:S(2)}) collective-permute-start(f32[2,8,256]{2,1,0:T(8,128)S(1)} %get-tuple-element.56), channel_id=1, source_target_pairs={{8,0},{16,8},{24,16},{9,1},{17,9},{25,17},{10,2},{18,10},{26,18},{... | collective-permute-start | bytes 49160 | tf_op jit(solution)/shard_map/ppermute | solution.py:25
  (18 other events, 74.5 us)
where the time goes:
time: 237 us; the launch traced here: 234 us
  starting transfers between devices  98 us (41%)
  blocking collectives  79.4 us (34%)
  waiting for transfers between devices  43.7 us (18%)
  other arithmetic  5.64 us (2%)
  local copies, waits for them, and re-layouts  4.15 us (2%)
  between operations  2.39 us (1%)
    ppermute x20, starting transfers between devices, with_halo(): before = lax.ppermute(last, axis, up)  72.1 us
    all_gather x1, blocking collectives, coarse_solve(): lax.all_gather(coeffs[None], ('gx', 'gy'), axis=0, tiled=True)  42.5 us
    ppermute x20, waiting for transfers between devices, with_halo(): after = lax.ppermute(leading, axis, down)  41 us
    all_gather x1, blocking collectives, coarse_solve(): lax.all_gather(source[None], ('gx', 'gy'), axis=0, tiled=True)  36.9 us
    ppermute x20, starting transfers between devices, with_halo(): after = lax.ppermute(leading, axis, down)  25.8 us
  transfers between devices with their start and end apart: 40, of which 14 were waited for; matrix products, arithmetic and copies ran while one was open for 2% of the time, Pallas kernels for 0%

commit v1 on v0

v1 whole, which is shorter than its diff:
```python
import functools

import jax
import jax.numpy as jnp
from jax import lax
from jax.experimental import pallas as pl
from jax.experimental.pallas import tpu as pltpu
from jax.sharding import PartitionSpec as P

SMOOTH = 2
COARSE_STEPS = 6
SMOOTH_LOW = 0.5
SMOOTH_HIGH = 2.0
COARSE_LOW = 0.05
COARSE_HIGH = 2.0

DEEP_F = 2 * SMOOTH - 1
DEEP_C = 2 * SMOOTH
SUB = 8
PAD = 4
WRITTEN_OUT = 512

VMEM = pl.BlockSpec(memory_space=pltpu.VMEM)
F32 = jnp.float32


def chebyshev(low_end, high_end, sweeps):
    middle = 0.5 * (high_end + low_end)
    half_span = 0.5 * (high_end - low_end)
    sig_ratio = middle / half_span
    rho_now = 1.0 / sig_ratio
    coeff_pairs = []
    for sweep_num in range(1, sweeps):
        rho_next = 1.0 / (2.0 * sig_ratio - rho_now)
        coeff_pairs.append((rho_next * rho_now, 2.0 * rho_next / half_span))
        rho_now = rho_next
    return (1.0 / middle, coeff_pairs)


def each(count, registers, step):
    if count * registers <= WRITTEN_OUT:
        for i in range(count):
            step(i)
    else:

        def one(i, carry):
            step(i)
            return carry

        lax.fori_loop(0, count, one, 0)


def turn(value, amount, axis):
    return pltpu.roll(value, amount % value.shape[axis], axis)


def iota(shape, axis):
    return lax.broadcasted_iota(jnp.int32, shape, axis)


def beside(v, below, above, w_below, w_above, w_cols, w_depth, stride=1):
    out = w_above * above + w_below * below
    out = out + w_cols * turn(v, -1, 0)
    out = out + w_depth * turn(v, -stride, 1)
    return out + turn(w_cols * v, 1, 0) + turn(w_depth * v, stride, 1)


def exact_dot(a, b):
    return jnp.dot(a, b, precision=lax.Precision.HIGHEST, preferred_element_type=F32)


def call(kernel, out_shapes, scratch, args, limit):
    return pl.pallas_call(
        kernel,
        out_shape=[jax.ShapeDtypeStruct(s, F32) for s in out_shapes],
        in_specs=[VMEM] * len(args),
        out_specs=[VMEM] * len(out_shapes),
        scratch_shapes=[pltpu.VMEM(s, F32) for s in scratch],
        compiler_params=pltpu.CompilerParams(vmem_limit_bytes=limit),
    )(*args)


def pack_rows(f_ref, c_ref, a_ref, b_ref):
    rows = f_ref.shape[0]
    odd = lax.rem(lax.axis_index("gx"), 2)
    for ref, at_end in ((a_ref, 1 - odd), (b_ref, odd)):
        ref[0:DEEP_F] = f_ref[pl.ds(at_end * (rows - DEEP_F), DEEP_F)]
        ref[DEEP_F:] = c_ref[pl.ds(at_end * (rows - DEEP_C), DEEP_C)]


def row_sources(along_x, rows, f_ref, c_ref, a_ref, b_ref):
    gx = lax.axis_index("gx")
    odd = lax.rem(gx, 2) == 1
    has_before = (gx > 0).astype(F32)
    has_after = (gx < along_x - 1).astype(F32)

    def before(i):
        return jnp.where(odd, a_ref[i], b_ref[i]) * has_before

    def after(i):
        return jnp.where(odd, b_ref[i], a_ref[i]) * has_after

    def f_row(i):
        if i < 0:
            return before(DEEP_F + i)
        return f_ref[i] if i < rows else after(i - rows)

    def c_row(i):
        if i < 0:
            return before(DEEP_F + DEEP_C + i)
        return c_ref[i] if i < rows else after(DEEP_F + i - rows)

    return f_row, c_row


def pack_cols(along_x, f_ref, c_ref, a_ref, b_ref, z_ref, k_ref):
    rows = f_ref.shape[0]
    f_row, c_row = row_sources(along_x, rows, f_ref, c_ref, a_ref, b_ref)
    odd = lax.rem(lax.axis_index("gy"), 2) == 1
    low_half = iota(f_ref.shape[1:], 0) < DEEP_C
    for t in range(rows + 2 * DEEP_F):
        f, c = f_row(t - DEEP_F), c_row(t - DEEP_F)
        first = jnp.where(low_half, c, turn(f, DEEP_C, 0))
        last = jnp.where(low_half, turn(c, DEEP_C, 0), f)
        z_ref[t] = jnp.where(odd, last, first)
        k_ref[t] = jnp.where(odd, first, last)


def fine_down(
    along_x, along_y, copies,
    f_ref, c_ref, a_ref, b_ref, z_ref, k_ref,
    send_ref, u_ref, fx_ref, wx_ref, wy_ref, wz_ref, diag_ref, inv_ref,
    cx_ref, v_ref, r_ref,
):
    rows, cols, depth = f_ref.shape
    f_row, c_row = row_sources(along_x, rows, f_ref, c_ref, a_ref, b_ref)
    gx, gy = lax.axis_index("gx"), lax.axis_index("gy")
    odd = lax.rem(gy, 2) == 1
    has_left = (gy > 0).astype(F32)
    has_right = (gy < along_y - 1).astype(F32)
    low_half = iota((cols, depth), 0) < DEEP_C
    wide = (cols + 2 * DEEP_C, depth)
    lane = iota(wide, 1)
    col = iota(wide, 0)
    col_inside = ((col >= DEEP_C) | (gy > 0)) & (
        (col < DEEP_C + cols) | (gy < along_y - 1)
    )
    inv_mid, ((keep, push),) = chebyshev(SMOOTH_LOW, SMOOTH_HIGH, SMOOTH)

    for t in range(rows + 2 * DEEP_C):
        row = t - DEEP_C
        c = c_row(row)
        turned = turn(c, DEEP_C, 0)
        s = row + DEEP_F
        if 0 <= s < rows + 2 * DEEP_F:
            left = jnp.where(odd, k_ref[s], z_ref[s]) * has_left
            right = jnp.where(odd, z_ref[s], k_ref[s]) * has_right
            f = f_row(row)
            fx_ref[s, 0:cols] = turn(jnp.where(low_half, f, left), DEEP_C, 0)
            fx_ref[s, cols:] = jnp.where(low_half, turn(f, DEEP_C, 0), right)
        else:
            left = right = jnp.zeros_like(c)
        cx_ref[t, 0:cols] = jnp.where(low_half, left, turned)
        cx_ref[t, cols:] = jnp.where(low_half, turned, turn(right, DEEP_C, 0))

    tall = rows + 2 * DEEP_F
    wx_ref[0] = 0.5 * (cx_ref[0] + cx_ref[1])
    for s in range(tall):
        c = cx_ref[s + 1]
        half = 0.5 * c
        above = half + 0.5 * cx_ref[s + 2]
        wx_ref[s + 1] = above
        w_cols = half + turn(half, -1, 0)
        w_depth = jnp.where(lane == depth - 1, 0.0, half + turn(half, -1, 1))
        edge = jnp.where((lane == 0) | (lane == depth - 1), half, 0.0)
        diag = wx_ref[s] + above + w_cols + turn(w_cols, 1, 0)
        diag = diag + w_depth + turn(w_depth, 1, 1) + edge
        inside = col_inside
        if s < DEEP_F:
            inside = inside & (gx > 0)
        if s >= rows + DEEP_F:
            inside = inside & (gx < along_x - 1)
        inv = jnp.where(inside, 1.0 / diag, 0.0)
        wy_ref[s] = w_cols
        wz_ref[s] = w_depth
        diag_ref[s] = diag
        inv_ref[s] = inv
        v_ref[s] = fx_ref[s] * inv * inv_mid

    def residual(x_ref, shift, s):
        x = x_ref[s - shift]
        total = beside(
            x, x_ref[s - shift - 1], x_ref[s - shift + 1],
            wx_ref[s], wx_ref[s + 1], wy_ref[s], wz_ref[s],
        )
        return x, fx_ref[s] - (diag_ref[s] * x - total)

    for s in range(1, tall - 1):
        v, r = residual(v_ref, 0, s)
        u_ref[s - 1] = v + (keep * v + push * (r * inv_ref[s]))
    for i in range(rows):
        _, r_ref[i] = residual(u_ref, 1, i + DEEP_F)

    half_rows = rows // 2
    summed = [r_ref[2 * i] + r_ref[2 * i + 1] for i in range(half_rows)]
    summed += [c_ref[2 * i] + c_ref[2 * i + 1] for i in range(half_rows)]
    summed = jnp.concatenate(summed, axis=0)
    pairs = (depth, depth // 2)
    thin = exact_dot(summed, (iota(pairs, 0) // 2 == iota(pairs, 1)).astype(F32))
    choice = (SUB * half_rows, summed.shape[0])
    line, source = iota(choice, 0), iota(choice, 1)
    block, place = line // SUB, line % SUB
    half_cols = cols // 2
    f_half = (place >= half_cols) == odd
    place = place % half_cols
    f_from = wide[0] * block + DEEP_C + 2 * place
    c_from = wide[0] * half_rows + cols * block + 2 * place
    from_f = (source == f_from) | (source == f_from + 1)
    from_c = (source == c_from) | (source == c_from + 1)
    picker = jnp.where(f_half, jnp.where(from_f, 0.5, 0.0), jnp.where(from_c, 0.125, 0.0))
    tile = exact_dot(picker, thin).reshape(half_rows, SUB, depth // 2)

    def put(i):
        send_ref[pl.ds(i * half_rows, half_rows)] = tile

    each(copies, half_rows, put)


def coarse_and_up(
    along_x, along_y,
    own_ref, other_ref, u0_ref, fx_ref, wx0_ref, wy0_ref, wz0_ref, diag0_ref, inv0_ref,
    out_ref,
    f_ref, c_ref, wx_ref, wy_ref, wz_ref, diag_ref, inv_ref, v_ref,
    f2_ref, c2_ref, wx2_ref, wy2_ref, wz2_ref, diag2_ref, inv2_ref, d2_ref, e2_ref, e3_ref,
    py_ref, vw_ref, dw_ref, vx_ref, e1_ref, yy_ref, v0_ref, d0_ref, x0_ref, o_ref,
):
    gx, gy = lax.axis_index("gx"), lax.axis_index("gy")
    odd = lax.rem(gy, 2) == 1
    brick1 = own_ref.shape[0] // (along_x * (along_y // 2))
    rows1, cols1, depth1 = f_ref.shape[0] - 2 * PAD, f_ref.shape[1], f_ref.shape[2]
    across = cols1 // SUB
    registers1 = across * (depth1 // 128)
    shape1 = (cols1, depth1)
    zero1 = jnp.zeros(shape1, F32)
    inv_mid, ((keep, push),) = chebyshev(SMOOTH_LOW, SMOOTH_HIGH, SMOOTH)

    mine = (iota((SUB, depth1), 0) < SUB // 2) != odd
    c_ref[PAD - 1] = zero1
    c_ref[PAD + rows1] = zero1

    def place(k):
        x, z = k // across, k % across
        for i in range(brick1):
            own, other = own_ref[k * brick1 + i], other_ref[k * brick1 + i]
            row = PAD + x * brick1 + i
            at = z * SUB if isinstance(z, int) else pl.multiple_of(z * SUB, SUB)
            f_ref[row, pl.ds(at, SUB)] = jnp.where(mine, own, other)
            c_ref[row, pl.ds(at, SUB)] = turn(jnp.where(mine, other, own), SUB // 2, 0)

    each(along_x * across, brick1, place)

    wx_ref[PAD] = 0.5 * c_ref[PAD]

    def weigh(c, below, above, shape, stride):
        col, lane = iota(shape, 0), iota(shape, 1)
        half = 0.5 * c
        w_above = half + 0.5 * above
        w_cols = jnp.where(col == shape[0] - 1, 0.0, half + turn(half, -1, 0))
        w_depth = jnp.where(lane >= shape[1] - stride, 0.0, half + turn(half, -stride, 1))
        edge = jnp.where((col == 0) | (col == shape[0] - 1), half, 0.0)
        edge = edge + jnp.where((lane < stride) | (lane >= shape[1] - stride), half, 0.0)
        diag = half + 0.5 * below + w_above + w_cols + turn(w_cols, 1, 0)
        diag = diag + w_depth + turn(w_depth, stride, 1) + edge
        return w_above, w_cols, w_depth, diag

    def weigh1(i):
        row = PAD + i
        w_above, w_cols, w_depth, diag = weigh(
            c_ref[row], c_ref[row - 1], c_ref[row + 1], shape1, 1
        )
        inv = 1.0 / diag
        wx_ref[row + 1] = w_above
        wy_ref[row] = w_cols
        wz_ref[row] = w_depth
        diag_ref[row] = diag
        inv_ref[row] = inv
        v_ref[row] = f_ref[row] * inv * inv_mid

    v_ref[PAD - 1] = zero1
    v_ref[PAD + rows1] = zero1
    each(rows1, registers1, weigh1)

    rows2, cols2 = rows1 // 2, cols1 // 2
    shape2 = (cols2, depth1)
    registers2 = max(registers1 // 2, 1)
    zero2 = jnp.zeros(shape2, F32)
    lane2, col2 = iota(shape2, 1), iota(shape2, 0)
    even2 = lane2 % 2 == 0

    def fold(ref, row):
        half = ref[row, pl.ds(0, cols2, stride=2), :] + ref[row, pl.ds(1, cols2, stride=2), :]
        return half + jnp.where(even2, turn(half, -1, 1), turn(half, 1, 1))

    def restrict_c(k):
        row = PAD + 2 * k
        c2_ref[k + 1] = 0.125 * (fold(c_ref, row) + fold(c_ref, row + 1))

    each(rows2, 2 * registers1, restrict_c)
    u_ref = c_ref

    def residual1(x_ref, at, row):
        x = x_ref[at]
        total = beside(
            x, x_ref[at - 1], x_ref[at + 1],
            wx_ref[row], wx_ref[row + 1], wy_ref[row], wz_ref[row],
        )
        return x, f_ref[row] - (diag_ref[row] * x - total)

    def second1(i):
        row = PAD + i
        v, r = residual1(v_ref, row, row)
        u_ref[row] = v + (keep * v + push * (r * inv_ref[row]))

    each(rows1, registers1, second1)

    def restrict(k):
        row = PAD + 2 * k
        _, first = residual1(u_ref, row, row)
        _, second = residual1(u_ref, row + 1, row + 1)
        v_ref[k] = first + second
        f2_ref[k] = 0.5 * fold(v_ref, k)

    each(rows2, 2 * registers1, restrict)
    c2_ref[0] = zero2
    c2_ref[rows2 + 1] = zero2
    wx2_ref[0] = 0.5 * c2_ref[1]
    for ref in (e2_ref, e3_ref):
        ref[0] = zero2
        ref[rows2 + 1] = zero2
    inv_mid2, pairs2 = chebyshev(COARSE_LOW, COARSE_HIGH, COARSE_STEPS)

    def weigh2(k):
        w_above, w_cols, w_depth, diag = weigh(
            c2_ref[k + 1], c2_ref[k], c2_ref[k + 2], shape2, 2
        )
        inv = 1.0 / diag
        wx2_ref[k + 1] = w_above
        wy2_ref[k] = w_cols
        wz2_ref[k] = w_depth
        diag2_ref[k] = diag
        inv2_ref[k] = inv
        d = f2_ref[k] * inv * inv_mid2
        d2_ref[k] = d
        e2_ref[k + 1] = d

    each(rows2, registers2, weigh2)

    def residual2(e_ref, k):
        e = e_ref[k + 1]
        total = beside(
            e, e_ref[k], e_ref[k + 2], wx2_ref[k], wx2_ref[k + 1], wy2_ref[k], wz2_ref[k], 2
        )
        return e, f2_ref[k] - (diag2_ref[k] * e - total)

    now_ref, next_ref = e2_ref, e3_ref
    for keep2, push2 in pairs2:

        def step2(k):
            e, r = residual2(now_ref, k)
            d = keep2 * d2_ref[k] + push2 * (r * inv2_ref[k])
            d2_ref[k] = d
            next_ref[k + 1] = e + d

        each(rows2, registers2, step2)
        now_ref, next_ref = next_ref, now_ref

    def gather_sums(k, sums):
        _, r = residual2(now_ref, k)
        total = wx2_ref[k] * (k > 0) + wx2_ref[k + 1] * (k < rows2 - 1)
        total = total + wy2_ref[k] + turn(wy2_ref[k], 1, 0)
        total = total + wz2_ref[k] + turn(wz2_ref[k], 2, 1)
        return sums[0] + r, sums[1] + (diag2_ref[k] - total)

    sums = (zero2, zero2)
    if rows2 * registers2 <= WRITTEN_OUT:
        for k in range(rows2):
            sums = gather_sums(k, sums)
    else:
        sums = lax.fori_loop(0, rows2, gather_sums, sums)
    top = jnp.sum(sums[0], axis=(0, 1), keepdims=True)
    bottom = jnp.sum(sums[1], axis=(0, 1), keepdims=True)
    mean = top / bottom

    span = brick1 + 2 * PAD
    start = gx * brick1 - PAD
    coarse_span = span // 2 + 2
    for k in range(coarse_span):
        row = lax.div(gx * brick1, 2) - PAD // 2 - 1 + k
        good = (row >= 0) & (row < rows2)
        e = now_ref[jnp.clip(row, 0, rows2 - 1) + 1] + mean
        e = jnp.where(good, e, 0.0)
        back = jnp.where(lane2 < 2, 0.0, turn(e, 2, 1))
        ahead = jnp.where(lane2 >= depth1 - 2, 0.0, turn(e, -2, 1))
        e = 0.75 * e + 0.25 * jnp.where(even2, back, ahead)
        back = jnp.where(col2 == 0, 0.0, turn(e, 1, 0))
        ahead = jnp.where(col2 == cols2 - 1, 0.0, turn(e, -1, 0))
        py_ref[k, pl.ds(0, cols2, stride=2), :] = 0.75 * e + 0.25 * back
        py_ref[k, pl.ds(1, cols2, stride=2), :] = 0.75 * e + 0.25 * ahead

    def inside1(m):
        return (start + m >= 0) & (start + m < rows1)

    for m in range(span):
        near = m // 2 + 1
        far = near - 1 if m % 2 == 0 else near + 1
        total = u_ref[PAD + start + m] + (0.75 * py_ref[near] + 0.25 * py_ref[far])
        vw_ref[m] = jnp.where(inside1(m), total, 0.0)
    for m in range(1, span - 1):
        row = PAD + start + m
        v, r = residual1(vw_ref, m, row)
        d = r * inv_ref[row] * inv_mid
        dw_ref[m] = d
        vx_ref[m] = jnp.where(inside1(m), v + d, 0.0)
    margin = SUB
    e1_ref[:, 0:margin, :] = jnp.zeros((span - 4, margin, depth1), F32)
    e1_ref[:, margin + cols1 :, :] = jnp.zeros((span - 4, margin, depth1), F32)
    for m in range(2, span - 2):
        row = PAD + start + m
        v, r = residual1(vx_ref, m, row)
        e = v + (keep * dw_ref[m] + push * (r * inv_ref[row]))
        e1_ref[m - 2, margin : margin + cols1, :] = jnp.where(inside1(m), e, 0.0)

    rows, cols, depth = out_ref.shape
    wide = (cols + 2 * DEEP_C, depth)
    half_wide = wide[0] // 2
    first_col = margin + gy * (cols // 2) - DEEP_C // 2
    for k in range(span - 4):
        e = e1_ref[k, pl.ds(first_col, half_wide), :]
        at = k * wide[0]
        yy_ref[pl.ds(at, half_wide, stride=2), :] = 0.75 * e + 0.25 * turn(e, 1, 0)
        yy_ref[pl.ds(at + 1, half_wide, stride=2), :] = 0.75 * e + 0.25 * turn(e, -1, 0)
    spread = (depth1, depth)
    from_cell, to_cell = iota(spread, 0), iota(spread, 1)
    home = to_cell // 2
    near_cell = jnp.where(to_cell % 2 == 0, home - 1, home + 1)
    weights = jnp.where(from_cell == home, 0.75, 0.0) + jnp.where(from_cell == near_cell, 0.25, 0.0)
    carried = exact_dot(yy_ref[...], weights).reshape(span - 4, wide[0], depth)
    col = iota(wide, 0)
    col_inside = ((col >= DEEP_C) | (gy > 0)) & (
        (col < DEEP_C + cols) | (gy < along_y - 1)
    )
    for s in range(1, rows + 2 * DEEP_F - 1):
        row = s - DEEP_F
        near = row // 2 + 2
        far = near - 1 if row % 2 == 0 else near + 1
        inside = col_inside
        if row < 0:
            inside = inside & (gx > 0)
        if row >= rows:
            inside = inside & (gx < along_x - 1)
        total = u0_ref[s - 1] + (0.75 * carried[near] + 0.25 * carried[far])
        v0_ref[s] = jnp.where(inside, total, 0.0)

    def residual0(x_ref, s):
        x = x_ref[s]
        total = beside(
            x, x_ref[s - 1], x_ref[s + 1],
            wx0_ref[s], wx0_ref[s + 1], wy0_ref[s], wz0_ref[s],
        )
        return x, fx_ref[s] - (diag0_ref[s] * x - total)

    for s in range(2, rows + 2 * DEEP_F - 2):
        v, r = residual0(v0_ref, s)
        d = r * inv0_ref[s] * inv_mid
        d0_ref[s] = d
        x0_ref[s] = v + d
    for i in range(rows):
        s = i + DEEP_F
        v, r = residual0(x0_ref, s)
        o_ref[i] = v + (keep * d0_ref[s] + push * (r * inv0_ref[s]))
    for i in range(rows):
        out_ref[i] = o_ref[i, DEEP_C : DEEP_C + cols, :]


def pairs_from(first, count):
    swaps = []
    for i in range(first, first + count, 2):
        a, b = i % count, (i + 1) % count
        swaps += [(a, b), (b, a)]
    return swaps


def body(right_side, coefficient):
    along_x, along_y = lax.axis_size("gx"), lax.axis_size("gy")
    rows, cols, depth = right_side.shape
    assert cols == 2 * DEEP_C and rows % 4 == 0 and depth % 256 == 0
    assert along_x % 2 == 0 and along_y % 2 == 0
    small = 16 << 20
    strip = (DEEP_F + DEEP_C, cols, depth)
    a, b = call(pack_rows, [strip] * 2, [], (right_side, coefficient), small)
    a = lax.ppermute(a, "gx", pairs_from(0, along_x))
    b = lax.ppermute(b, "gx", pairs_from(1, along_x))

    tall = rows + 2 * DEEP_F
    z, k = call(
        functools.partial(pack_cols, along_x),
        [(tall, cols, depth)] * 2,
        [],
        (right_side, coefficient, a, b),
        small,
    )
    z = lax.ppermute(z, "gy", pairs_from(1, along_y))
    k = lax.ppermute(k, "gy", pairs_from(0, along_y))

    wide = (cols + 2 * DEEP_C, depth)
    half = (rows // 2, SUB, depth // 2)
    copies = along_x * along_y // 2
    send, *state = call(
        functools.partial(fine_down, along_x, along_y, copies),
        [(copies * half[0],) + half[1:], (tall - 2,) + wide, (tall,) + wide, (tall + 1,) + wide]
        + [(tall,) + wide] * 4,
        [(tall + 2,) + wide, (tall,) + wide, (rows,) + wide],
        (right_side, coefficient, a, b, z, k),
        small + 2 * 4 * copies * half[0] * half[1] * half[2],
    )
    flat = along_x * along_y
    groups = [[i for i in range(flat) if i % 2 == core] for core in range(2)]
    own = lax.all_to_all(send, ("gx", "gy"), 0, 0, axis_index_groups=groups, tiled=True)
    other = lax.ppermute(own, "gy", pairs_from(0, along_y))

    rows1, cols1, depth1 = along_x * half[0], along_y * (cols // 2), half[2]
    whole1 = (rows1 + 2 * PAD + 1, cols1, depth1)
    rows2, cols2 = rows1 // 2, cols1 // 2
    whole2 = (rows2 + 2, cols2, depth1)
    span = half[0] + 2 * PAD
    line = (cols1, depth1)
    scratch = [(rows1 + 2 * PAD,) + line] + [whole1] * 7 + [whole2] * 10
    scratch += [(span // 2 + 2,) + line] + [(span,) + line] * 3
    scratch += [(span - 4, cols1 + 2 * SUB, depth1), ((span - 4) * wide[0], depth1)]
    scratch += [(tall,) + wide] * 3 + [(rows,) + wide]
    size = sum(4 * s[0] * s[1] * (s[2] if len(s) == 3 else 1) for s in scratch)
    size += 2 * 4 * own.size + 4 * 8 * tall * wide[0] * wide[1]
    (out,) = call(
        functools.partial(coarse_and_up, along_x, along_y),
        [right_side.shape],
        scratch,
        (own, other, *state),
        size + (12 << 20),
    )
    return out


def solution(mesh):
    placed = (P("gx", "gy", None), P("gx", "gy", None))
    return jax.shard_map(
        body, mesh=mesh, in_specs=placed, out_specs=P("gx", "gy", None), check_vma=False
    )
```

time: 237 us -> 37.4 us (0.16); the launches traced: 234 us -> 37.2 us
  starting transfers between devices: 98 us -> 6.77 us
  blocking collectives: 79.4 us -> 14.7 us
  waiting for transfers between devices: 43.7 us -> 9.89 us
  other arithmetic: 5.64 us -> 0 us
  Pallas kernels: 0 us -> 4.14 us
  local copies, waits for them, and re-layouts: 4.15 us -> 1.69 us
    ppermute x40 -> x5, starting transfers between devices: 98 us -> 6.77 us  [the longest x1 3 us: body(): a = lax.ppermute(a, 'gx', pairs_from(0, along_x))]
    all_gather x2 -> x0, blocking collectives: 79.4 us -> none  [the longest x1 42.5 us: coarse_solve(): lax.all_gather(coeffs[None], ('gx', 'gy'), axis=0, tiled=True)]
    ppermute x40 -> x5, waiting for transfers between devices: 43.7 us -> 9.89 us  [the longest x1 4.77 us: body(): z = lax.ppermute(z, 'gy', pairs_from(1, along_y))]
    all_to_all x0 -> x1, blocking collectives: none -> 14.7 us  [body(): lax.all_to_all(send, ('gx', 'gy'), 0, 0, axis_index_groups=groups, tiled=...]
    pallas_call x0 -> x4, Pallas kernels: none -> 4.14 us  [call(): pl.pallas_call(kernel, out_shape=[jax.ShapeDtypeStruct(s, F32) for s in o...]
    slice x31 -> x0, local copies, waits for them, and re-layouts: 3.11 us -> none  [the longest x8 2.06 us: restrict_sum(): return field[:, :, 0::2] + field[:, :, 1::2]]
  transfers between devices with their start and end apart: 40 -> 5, of which waited for: 14 -> 4; matrix products, arithmetic and copies ran while one was open for 2% -> 0% of each run, Pallas kernels for 0% -> 0%
where the time goes in v1:
time: 37.4 us; the launch traced here: 37.2 us
  blocking collectives  14.7 us (39%)
  waiting for transfers between devices  9.89 us (26%)
  starting transfers between devices  6.77 us (18%)
  Pallas kernels  4.14 us (11%)
  local copies, waits for them, and re-layouts  1.69 us (5%)
    all_to_all x1, blocking collectives, body(): lax.all_to_all(send, ('gx', 'gy'), 0, 0, axis_index_groups=groups, tiled=...  14.7 us
    ppermute x1, waiting for transfers between devices, body(): z = lax.ppermute(z, 'gy', pairs_from(1, along_y))  4.77 us
    pallas_call x4, Pallas kernels, call(): pl.pallas_call(kernel, out_shape=[jax.ShapeDtypeStruct(s, F32) for s in o...  4.14 us
    ppermute x1, starting transfers between devices, body(): a = lax.ppermute(a, 'gx', pairs_from(0, along_x))  3 us
    ppermute x1, waiting for transfers between devices, body(): b = lax.ppermute(b, 'gx', pairs_from(1, along_x))  2.85 us
    ppermute x1, starting transfers between devices, body(): z = lax.ppermute(z, 'gy', pairs_from(1, along_y))  2.27 us
    unnamed x8, local copies, waits for them, and re-layouts  1.69 us
    ppermute x1, waiting for transfers between devices, body(): other = lax.ppermute(own, 'gy', pairs_from(0, along_y))  1.53 us
  transfers between devices with their start and end apart: 5, of which 4 were waited for; matrix products, arithmetic and copies ran while one was open for 0% of the time, Pallas kernels for 0%

profile of v1, /device:TPU:0, one launch (start us, length us, event | category | flops | bytes accessed | tf_op | source)
XLA Modules:
  0.0 37.2 jit_solution(7753714196159975585)
XLA Ops:
  0.0 0.0 copy-start
  0.0 0.8 %copy-done = f32[8,8,256]{2,1,0:T(8,128)S(1)} copy-done((f32[8,8,256]{2,1,0:T(8,128)S(1)}, f32[8,8,256]{2,1,0:T(8,128)}, u32[]{:S(2)}) %copy-start) | copy-done | bytes 65560
  0.8 0.0 copy-start.2
  0.8 0.8 %copy-done.2 = f32[8,8,256]{2,1,0:T(8,128)S(1)} copy-done((f32[8,8,256]{2,1,0:T(8,128)S(1)}, f32[8,8,256]{2,1,0:T(8,128)}, u32[]{:S(2)}) %copy-start.2) | copy-done | bytes 65560
  1.7 3.0 %collective-permute-start = (f32[7,8,256]{2,1,0:T(8,128)S(1)}, f32[7,8,256]{2,1,0:T(8,128)S(1)}, u32[]{:S(2)}, u32[]{:S(2)}) collective-permute-start(f32[7,8,256]{2,1,0:T(8,128)S(1)} %get-tuple-element.17), channel_id=1, source_target_pairs={{0,8},{8,0},{16,24},{24,16},{1,9},{9,1},{17,25},{25,17},{2,10},{10... | collective-permute-start | bytes 172040 | tf_op jit(solution)/shard_map/ppermute | solution.py:501
  4.7 0.0 copy-start.1
  4.7 0.0 copy-start.3
  4.7 1.5 %collective-permute-start.1 = (f32[7,8,256]{2,1,0:T(8,128)S(1)}, f32[7,8,256]{2,1,0:T(8,128)S(1)}, u32[]{:S(2)}, u32[]{:S(2)}) collective-permute-start(f32[7,8,256]{2,1,0:T(8,128)S(1)} %get-tuple-element.18), channel_id=1, source_target_pairs={{8,16},{16,8},{24,0},{0,24},{9,17},{17,9},{25,1},{1,25},{10,18},{1... | collective-permute-start | bytes 172040 | tf_op jit(solution)/shard_map/ppermute | solution.py:502
  6.2 0.7 %collective-permute-done.a_ref = f32[7,8,256]{2,1,0:T(8,128)S(1)} collective-permute-done((f32[7,8,256]{2,1,0:T(8,128)S(1)}, f32[7,8,256]{2,1,0:T(8,128)S(1)}, u32[]{:S(2)}, u32[]{:S(2)}) %collective-permute-start) | collective-permute-done | bytes 57376 | tf_op jit(solution)/shard_map/ppermute | solution.py:501
  6.9 2.9 %collective-permute-done.1.b_ref = f32[7,8,256]{2,1,0:T(8,128)S(1)} collective-permute-done((f32[7,8,256]{2,1,0:T(8,128)S(1)}, f32[7,8,256]{2,1,0:T(8,128)S(1)}, u32[]{:S(2)}, u32[]{:S(2)}) %collective-permute-start.1) | collective-permute-done | bytes 57376 | tf_op jit(solution)/shard_map/ppermute | solution.py:502
  9.8 2.3 %collective-permute-start.2 = (f32[14,8,256]{2,1,0:T(8,128)S(1)}, f32[14,8,256]{2,1,0:T(8,128)S(1)}, u32[]{:S(2)}, u32[]{:S(2)}) collective-permute-start(f32[14,8,256]{2,1,0:T(8,128)S(1)} %get-tuple-element.19), channel_id=1, source_target_pairs={{1,2},{2,1},{3,4},{4,3},{5,6},{6,5},{7,0},{0,7},{9,10},{10,9},{11,... | collective-permute-start | bytes 344072 | tf_op jit(solution)/shard_map/ppermute | solution.py:512
  12.1 0.0 collective-permute-start.3
  12.1 4.8 %collective-permute-done.2.z_ref = f32[14,8,256]{2,1,0:T(8,128)S(1)} collective-permute-done((f32[14,8,256]{2,1,0:T(8,128)S(1)}, f32[14,8,256]{2,1,0:T(8,128)S(1)}, u32[]{:S(2)}, u32[]{:S(2)}) %collective-permute-start.2) | collective-permute-done | bytes 114720 | tf_op jit(solution)/shard_map/ppermute | solution.py:512
  16.9 0.0 collective-permute-done.3.k_ref
  16.9 0.0 copy-done.1
  16.9 0.0 copy-done.3
  16.9 1.0 %shard_map.30 = (f32[64,8,128]{2,1,0:T(8,128)S(1)}, f32[12,16,256]{2,1,0:T(8,128)S(1)}, f32[14,16,256]{2,1,0:T(8,128)S(1)}, f32[15,16,256]{2,1,0:T(8,128)S(1)}, ...) custom-call(f32[8,8,256]{2,1,0:T(8,128)S(1)} %copy-done.1, ...), custom_call_target="tpu_custom_call" | custom-call | tf_op jit(solution)/shard_map/pallas_call | solution.py:73
  17.9 14.7 %all_to_all.5.own_ref = f32[64,8,128]{2,1,0:T(8,128)S(1)} all-to-all(f32[64,8,128]{2,1,0:T(8,128)S(1)} %get-tuple-element.21), channel_id=1, replica_groups={{0,2,4,6,8,10,12,14,16,18,20,22,24,26,28,30},{1,3,5,7,9,11,13,15,17,19,..., dimensions={0} | all-to-all | bytes 524288 | tf_op jit(solution)/shard_map/all_to_all | solution.py:528
  32.6 0.0 collective-permute-start.4
  32.6 1.5 %collective-permute-done.4.other_ref = f32[64,8,128]{2,1,0:T(8,128)S(1)} collective-permute-done((f32[64,8,128]{2,1,0:T(8,128)S(1)}, f32[64,8,128]{2,1,0:T(8,128)S(1)}, u32[]{:S(2)}, u32[]{:S(2)}) %collective-permute-start.4) | collective-permute-done | bytes 262176 | tf_op jit(solution)/shard_map/ppermute | solution.py:529
  34.1 3.1 %shard_map.31 = f32[8,8,256]{2,1,0:T(8,128)} custom-call(f32[64,8,128]{2,1,0:T(8,128)S(1)} %all_to_all.5.own_ref, f32[64,8,128]{2,1,0:T(8,128)S(1)} %collective-permute-done.4.other_ref, f32[12,16,256]{2,1,0:T(8,128)S(1)} %get-tuple-element.22.u0_ref, f32[14,16,256]{2,1,0:T(8,128)S(1)} %get-tuple-element.23.fx_ref, ...), custom_call_target="tpu_custom_call" | custom-call | tf_op jit(solution)/shard_map/pallas_call | solution.py:73
  (2 shorter events, 0.0 us)
Async XLA Ops:
  0.0 0.8 %copy-start = (f32[8,8,256]{2,1,0:T(8,128)S(1)}, f32[8,8,256]{2,1,0:T(8,128)}, u32[]{:S(2)}) copy-start(f32[8,8,256]{2,1,0:T(8,128)} %f_ref.5) | copy-start | bytes 196612
  0.8 0.8 %copy-start.2 = (f32[8,8,256]{2,1,0:T(8,128)S(1)}, f32[8,8,256]{2,1,0:T(8,128)}, u32[]{:S(2)}) copy-start(f32[8,8,256]{2,1,0:T(8,128)} %c_ref.5) | copy-start | bytes 196612
  1.7 5.2 %collective-permute-start = (f32[7,8,256]{2,1,0:T(8,128)S(1)}, f32[7,8,256]{2,1,0:T(8,128)S(1)}, u32[]{:S(2)}, u32[]{:S(2)}) collective-permute-start(f32[7,8,256]{2,1,0:T(8,128)S(1)} %get-tuple-element.17), channel_id=1, source_target_pairs={{0,8},{8,0},{16,24},{24,16},{1,9},{9,1},{17,25},{25,17},{2,10},{10... | collective-permute-start | bytes 172040 | tf_op jit(solution)/shard_map/ppermute | solution.py:501
  4.7 12.2 %copy-start.1 = (f32[8,8,256]{2,1,0:T(8,128)S(1)}, f32[8,8,256]{2,1,0:T(8,128)}, u32[]{:S(2)}) copy-start(f32[8,8,256]{2,1,0:T(8,128)} %f_ref.5) | copy-start | bytes 196612
  4.7 12.2 %copy-start.3 = (f32[8,8,256]{2,1,0:T(8,128)S(1)}, f32[8,8,256]{2,1,0:T(8,128)}, u32[]{:S(2)}) copy-start(f32[8,8,256]{2,1,0:T(8,128)} %c_ref.5) | copy-start | bytes 196612
  4.7 5.1 %collective-permute-start.1 = (f32[7,8,256]{2,1,0:T(8,128)S(1)}, f32[7,8,256]{2,1,0:T(8,128)S(1)}, u32[]{:S(2)}, u32[]{:S(2)}) collective-permute-start(f32[7,8,256]{2,1,0:T(8,128)S(1)} %get-tuple-element.18), channel_id=1, source_target_pairs={{8,16},{16,8},{24,0},{0,24},{9,17},{17,9},{25,1},{1,25},{10,18},{1... | collective-permute-start | bytes 172040 | tf_op jit(solution)/shard_map/ppermute | solution.py:502
  9.8 7.0 %collective-permute-start.2 = (f32[14,8,256]{2,1,0:T(8,128)S(1)}, f32[14,8,256]{2,1,0:T(8,128)S(1)}, u32[]{:S(2)}, u32[]{:S(2)}) collective-permute-start(f32[14,8,256]{2,1,0:T(8,128)S(1)} %get-tuple-element.19), channel_id=1, source_target_pairs={{1,2},{2,1},{3,4},{4,3},{5,6},{6,5},{7,0},{0,7},{9,10},{10,9},{11,... | collective-permute-start | bytes 344072 | tf_op jit(solution)/shard_map/ppermute | solution.py:512
  12.1 4.8 %collective-permute-start.3 = (f32[14,8,256]{2,1,0:T(8,128)S(1)}, f32[14,8,256]{2,1,0:T(8,128)S(1)}, u32[]{:S(2)}, u32[]{:S(2)}) collective-permute-start(f32[14,8,256]{2,1,0:T(8,128)S(1)} %get-tuple-element.20), channel_id=1, source_target_pairs={{0,1},{1,0},{2,3},{3,2},{4,5},{5,4},{6,7},{7,6},{8,9},{9,8},{10,11... | collective-permute-start | bytes 344072 | tf_op jit(solution)/shard_map/ppermute | solution.py:513
  32.6 1.5 %collective-permute-start.4 = (f32[64,8,128]{2,1,0:T(8,128)S(1)}, f32[64,8,128]{2,1,0:T(8,128)S(1)}, u32[]{:S(2)}, u32[]{:S(2)}) collective-permute-start(f32[64,8,128]{2,1,0:T(8,128)S(1)} %all_to_all.5.own_ref), channel_id=1, source_target_pairs={{0,1},{1,0},{2,3},{3,2},{4,5},{5,4},{6,7},{7,6},{8,9},{9,8},{10,11... | collective-permute-start | bytes 786440 | tf_op jit(solution)/shard_map/ppermute | solution.py:529

commit v2 on v1

--- a/solution.py
+++ b/solution.py
@@ -80,12 +80,23 @@
     )(*args)
 
 
-def pack_rows(f_ref, c_ref, a_ref, b_ref):
+def pack_rows(f_ref, c_ref, a_ref, b_ref, sems):
     rows = f_ref.shape[0]
     odd = lax.rem(lax.axis_index("gx"), 2)
+    copies = []
     for ref, at_end in ((a_ref, 1 - odd), (b_ref, odd)):
-        ref[0:DEEP_F] = f_ref[pl.ds(at_end * (rows - DEEP_F), DEEP_F)]
-        ref[DEEP_F:] = c_ref[pl.ds(at_end * (rows - DEEP_C), DEEP_C)]
+        for whole_ref, first, count in ((f_ref, 0, DEEP_F), (c_ref, DEEP_F, DEEP_C)):
+            copies.append(
+                pltpu.make_async_copy(
+                    whole_ref.at[pl.ds(at_end * (rows - count), count)],
+                    ref.at[pl.ds(first, count)],
+                    sems.at[len(copies)],
+                )
+            )
+    for copy in copies:
+        copy.start()
+    for copy in copies:
+        copy.wait()
 
 
 def row_sources(along_x, rows, f_ref, c_ref, a_ref, b_ref):
@@ -244,18 +255,22 @@
     zero1 = jnp.zeros(shape1, F32)
     inv_mid, ((keep, push),) = chebyshev(SMOOTH_LOW, SMOOTH_HIGH, SMOOTH)
 
-    mine = (iota((SUB, depth1), 0) < SUB // 2) != odd
+    low_half = iota((SUB, depth1), 0) < SUB // 2
     c_ref[PAD - 1] = zero1
     c_ref[PAD + rows1] = zero1
 
     def place(k):
         x, z = k // across, k % across
+        at = z * SUB if isinstance(z, int) else pl.multiple_of(z * SUB, SUB)
+        half = brick1 // 2
         for i in range(brick1):
-            own, other = own_ref[k * brick1 + i], other_ref[k * brick1 + i]
+            swapped = odd if i < half else jnp.logical_not(odd)
+            low, high = k * brick1 + i % half, k * brick1 + half + i % half
+            low = jnp.where(swapped, other_ref[low], own_ref[low])
+            high = jnp.where(swapped, other_ref[high], own_ref[high])
             row = PAD + x * brick1 + i
-            at = z * SUB if isinstance(z, int) else pl.multiple_of(z * SUB, SUB)
-            f_ref[row, pl.ds(at, SUB)] = jnp.where(mine, own, other)
-            c_ref[row, pl.ds(at, SUB)] = turn(jnp.where(mine, other, own), SUB // 2, 0)
+            f_ref[row, pl.ds(at, SUB)] = jnp.where(low_half, low, high)
+            c_ref[row, pl.ds(at, SUB)] = turn(jnp.where(low_half, high, low), SUB // 2, 0)
 
     each(along_x * across, brick1, place)
 
@@ -497,7 +512,10 @@
     assert along_x % 2 == 0 and along_y % 2 == 0
     small = 16 << 20
     strip = (DEEP_F + DEEP_C, cols, depth)
-    a, b = call(pack_rows, [strip] * 2, [], (right_side, coefficient), small)
+    odd = lax.rem(lax.axis_index("gx"), 2) == 1
+    first = jnp.concatenate([right_side[:DEEP_F], coefficient[:DEEP_C]])
+    last = jnp.concatenate([right_side[rows - DEEP_F :], coefficient[rows - DEEP_C :]])
+    a, b = jnp.where(odd, first, last), jnp.where(odd, last, first)
     a = lax.ppermute(a, "gx", pairs_from(0, along_x))
     b = lax.ppermute(b, "gx", pairs_from(1, along_x))
 
@@ -509,8 +527,8 @@
         (right_side, coefficient, a, b),
         small,
     )
+    k = lax.ppermute(k, "gy", pairs_from(0, along_y))
     z = lax.ppermute(z, "gy", pairs_from(1, along_y))
-    k = lax.ppermute(k, "gy", pairs_from(0, along_y))
 
     wide = (cols + 2 * DEEP_C, depth)
     half = (rows // 2, SUB, depth // 2)
@@ -523,9 +541,7 @@
         (right_side, coefficient, a, b, z, k),
         small + 2 * 4 * copies * half[0] * half[1] * half[2],
     )
-    flat = along_x * along_y
-    groups = [[i for i in range(flat) if i % 2 == core] for core in range(2)]
-    own = lax.all_to_all(send, ("gx", "gy"), 0, 0, axis_index_groups=groups, tiled=True)
+    own = lax.all_to_all(send, ("gx", "gy"), 0, 0, tiled=True)
     other = lax.ppermute(own, "gy", pairs_from(0, along_y))
 
     rows1, cols1, depth1 = along_x * half[0], along_y * (cols // 2), half[2]

time: 37.4 us -> 34.9 us (0.933)
  blocking collectives: 14.7 us -> 13.1 us
  local copies, waits for them, and re-layouts: 1.69 us -> 0.85 us
  starting transfers between devices: 6.77 us -> 7.26 us
  waiting for transfers between devices: 9.89 us -> 9.47 us
    ppermute x1, starting transfers between devices: 1.49 us -> 3.96 us  [body(): b = lax.ppermute(b, 'gx', pairs_from(1, along_x))]
    ppermute x1, starting transfers between devices: 3 us -> 0.54 us  [body(): a = lax.ppermute(a, 'gx', pairs_from(0, along_x))]
    unnamed x8 -> x4, local copies, waits for them, and re-layouts: 1.69 us -> 0.05 us
    all_to_all x1, blocking collectives: 14.7 us -> 13.1 us  [body(): own = lax.all_to_all(send, ('gx', 'gy'), 0, 0, tiled=True)]
    ppermute x1, waiting for transfers between devices: 0.73 us -> 1.89 us  [body(): a = lax.ppermute(a, 'gx', pairs_from(0, along_x))]
    ppermute x1, waiting for transfers between devices: 2.85 us -> 1.75 us  [body(): b = lax.ppermute(b, 'gx', pairs_from(1, along_x))]
    slice x0 -> x2, local copies, waits for them, and re-layouts: none -> 0.79 us  [body(): first = jnp.concatenate([right_side[:DEEP_F], coefficient[:DEEP_C]])]
    ppermute x1, starting transfers between devices: 0.01 us -> 0.39 us  [body(): other = lax.ppermute(own, 'gy', pairs_from(0, along_y))]
where the time goes in v2:
time: 34.9 us; the launch traced here: 34.8 us
  blocking collectives  13.1 us (38%)
  waiting for transfers between devices  9.47 us (27%)
  starting transfers between devices  7.26 us (21%)
  Pallas kernels  4.09 us (12%)
  local copies, waits for them, and re-layouts  0.85 us (2%)
    all_to_all x1, blocking collectives, body(): own = lax.all_to_all(send, ('gx', 'gy'), 0, 0, tiled=True)  13.1 us
    ppermute x1, waiting for transfers between devices, body(): z = lax.ppermute(z, 'gy', pairs_from(1, along_y))  4.66 us
    pallas_call x3, Pallas kernels, call(): pl.pallas_call(kernel, out_shape=[jax.ShapeDtypeStruct(s, F32) for s in o...  4.09 us
    ppermute x1, starting transfers between devices, body(): b = lax.ppermute(b, 'gx', pairs_from(1, along_x))  3.96 us
    ppermute x1, starting transfers between devices, body(): z = lax.ppermute(z, 'gy', pairs_from(1, along_y))  2.38 us
    ppermute x1, waiting for transfers between devices, body(): a = lax.ppermute(a, 'gx', pairs_from(0, along_x))  1.89 us
    ppermute x1, waiting for transfers between devices, body(): b = lax.ppermute(b, 'gx', pairs_from(1, along_x))  1.75 us
    ppermute x1, waiting for transfers between devices, body(): other = lax.ppermute(own, 'gy', pairs_from(0, along_y))  1.16 us
  transfers between devices with their start and end apart: 5, of which 4 were waited for; matrix products, arithmetic and copies ran while one was open for 0% of the time, Pallas kernels for 0%

profile of v2, /device:TPU:0, one launch (start us, length us, event | category | flops | bytes accessed | tf_op | source)
XLA Modules:
  0.0 34.8 jit_solution(10358590107309072847)
XLA Ops:
  0.0 0.0 copy-start
  0.0 0.8 %fusion.2 = (f32[3,8,256]{2,1,0:T(8,128)S(1)}, f32[3,8,256]{2,1,0:T(8,128)S(1)}) fusion(f32[8,8,256]{2,1,0:T(8,128)} %f_ref.3), kind=kLoop, calls=%fused_computation.4 | loop fusion | bytes 98304 | tf_op jit(solution)/shard_map/slice | solution.py:516
  0.8 0.0 copy-done
  0.8 0.0 copy-start.1
  0.9 4.0 %collective-permute-start.1 = (f32[7,8,256]{2,1,0:T(8,128)S(1)}, f32[7,8,256]{2,1,0:T(8,128)S(1)}, u32[]{:S(2)}, u32[]{:S(2)}) collective-permute-start(f32[7,8,256]{2,1,0:T(8,128)S(1)} %get-tuple-element.25), channel_id=1, source_target_pairs={{8,16},{16,8},{24,0},{0,24},{9,17},{17,9},{25,1},{1,25},{10,18},{1... | collective-permute-start | bytes 172040 | tf_op jit(solution)/shard_map/ppermute | solution.py:520
  4.8 0.5 %collective-permute-start = (f32[7,8,256]{2,1,0:T(8,128)S(1)}, f32[7,8,256]{2,1,0:T(8,128)S(1)}, u32[]{:S(2)}, u32[]{:S(2)}) collective-permute-start(f32[7,8,256]{2,1,0:T(8,128)S(1)} %get-tuple-element.26), channel_id=1, source_target_pairs={{0,8},{8,0},{16,24},{24,16},{1,9},{9,1},{17,25},{25,17},{2,10},{10... | collective-permute-start | bytes 172040 | tf_op jit(solution)/shard_map/ppermute | solution.py:519
  5.4 1.8 %collective-permute-done.1.b_ref = f32[7,8,256]{2,1,0:T(8,128)S(1)} collective-permute-done((f32[7,8,256]{2,1,0:T(8,128)S(1)}, f32[7,8,256]{2,1,0:T(8,128)S(1)}, u32[]{:S(2)}, u32[]{:S(2)}) %collective-permute-start.1) | collective-permute-done | bytes 57376 | tf_op jit(solution)/shard_map/ppermute | solution.py:520
  7.1 1.9 %collective-permute-done.a_ref = f32[7,8,256]{2,1,0:T(8,128)S(1)} collective-permute-done((f32[7,8,256]{2,1,0:T(8,128)S(1)}, f32[7,8,256]{2,1,0:T(8,128)S(1)}, u32[]{:S(2)}, u32[]{:S(2)}) %collective-permute-start) | collective-permute-done | bytes 57376 | tf_op jit(solution)/shard_map/ppermute | solution.py:519
  9.0 0.0 copy-done.1
  9.1 2.4 %collective-permute-start.2 = (f32[14,8,256]{2,1,0:T(8,128)S(1)}, f32[14,8,256]{2,1,0:T(8,128)S(1)}, u32[]{:S(2)}, u32[]{:S(2)}) collective-permute-start(f32[14,8,256]{2,1,0:T(8,128)S(1)} %get-tuple-element.15), channel_id=1, source_target_pairs={{1,2},{2,1},{3,4},{4,3},{5,6},{6,5},{7,0},{0,7},{9,10},{10,9},{11,... | collective-permute-start | bytes 344072 | tf_op jit(solution)/shard_map/ppermute | solution.py:531
  11.4 0.0 collective-permute-start.3
  11.4 4.7 %collective-permute-done.2.z_ref = f32[14,8,256]{2,1,0:T(8,128)S(1)} collective-permute-done((f32[14,8,256]{2,1,0:T(8,128)S(1)}, f32[14,8,256]{2,1,0:T(8,128)S(1)}, u32[]{:S(2)}, u32[]{:S(2)}) %collective-permute-start.2) | collective-permute-done | bytes 114720 | tf_op jit(solution)/shard_map/ppermute | solution.py:531
  16.1 0.0 collective-permute-done.3.k_ref
  16.1 1.0 %shard_map.29 = (f32[64,8,128]{2,1,0:T(8,128)S(1)}, f32[12,16,256]{2,1,0:T(8,128)S(1)}, f32[14,16,256]{2,1,0:T(8,128)S(1)}, f32[15,16,256]{2,1,0:T(8,128)S(1)}, ...) custom-call(f32[8,8,256]{2,1,0:T(8,128)S(1)} %copy-done.1, ...), custom_call_target="tpu_custom_call" | custom-call | tf_op jit(solution)/shard_map/pallas_call | solution.py:73
  17.1 13.1 %all_to_all.5.own_ref = f32[64,8,128]{2,1,0:T(8,128)S(1)} all-to-all(f32[64,8,128]{2,1,0:T(8,128)S(1)} %get-tuple-element.17), channel_id=1, replica_groups=mesh['gx'=4,'gy'=8] {'gx','gy'}, dimensions={0} | all-to-all | bytes 524288 | tf_op jit(solution)/shard_map/all_to_all | solution.py:544
  30.2 0.4 %collective-permute-start.4 = (f32[64,8,128]{2,1,0:T(8,128)S(1)}, f32[64,8,128]{2,1,0:T(8,128)S(1)}, u32[]{:S(2)}, u32[]{:S(2)}) collective-permute-start(f32[64,8,128]{2,1,0:T(8,128)S(1)} %all_to_all.5.own_ref), channel_id=1, source_target_pairs={{0,1},{1,0},{2,3},{3,2},{4,5},{5,4},{6,7},{7,6},{8,9},{9,8},{10,11... | collective-permute-start | bytes 786440 | tf_op jit(solution)/shard_map/ppermute | solution.py:545
  30.6 1.2 %collective-permute-done.4.other_ref = f32[64,8,128]{2,1,0:T(8,128)S(1)} collective-permute-done((f32[64,8,128]{2,1,0:T(8,128)S(1)}, f32[64,8,128]{2,1,0:T(8,128)S(1)}, u32[]{:S(2)}, u32[]{:S(2)}) %collective-permute-start.4) | collective-permute-done | bytes 262176 | tf_op jit(solution)/shard_map/ppermute | solution.py:545
  31.7 3.0 %shard_map.30 = f32[8,8,256]{2,1,0:T(8,128)} custom-call(f32[64,8,128]{2,1,0:T(8,128)S(1)} %all_to_all.5.own_ref, f32[64,8,128]{2,1,0:T(8,128)S(1)} %collective-permute-done.4.other_ref, f32[12,16,256]{2,1,0:T(8,128)S(1)} %get-tuple-element.18.u0_ref, f32[14,16,256]{2,1,0:T(8,128)S(1)} %get-tuple-element.19.fx_ref, ...), custom_call_target="tpu_custom_call" | custom-call | tf_op jit(solution)/shard_map/pallas_call | solution.py:73
  (3 shorter events, 0.1 us)
Async XLA Ops:
  0.0 0.8 %copy-start = (f32[8,8,256]{2,1,0:T(8,128)S(1)}, f32[8,8,256]{2,1,0:T(8,128)}, u32[]{:S(2)}) copy-start(f32[8,8,256]{2,1,0:T(8,128)} %c_ref.3) | copy-start | bytes 196612
  0.8 8.2 %copy-start.1 = (f32[8,8,256]{2,1,0:T(8,128)S(1)}, f32[8,8,256]{2,1,0:T(8,128)}, u32[]{:S(2)}) copy-start(f32[8,8,256]{2,1,0:T(8,128)} %f_ref.3) | copy-start | bytes 196612
  0.9 6.2 %collective-permute-start.1 = (f32[7,8,256]{2,1,0:T(8,128)S(1)}, f32[7,8,256]{2,1,0:T(8,128)S(1)}, u32[]{:S(2)}, u32[]{:S(2)}) collective-permute-start(f32[7,8,256]{2,1,0:T(8,128)S(1)} %get-tuple-element.25), channel_id=1, source_target_pairs={{8,16},{16,8},{24,0},{0,24},{9,17},{17,9},{25,1},{1,25},{10,18},{1... | collective-permute-start | bytes 172040 | tf_op jit(solution)/shard_map/ppermute | solution.py:520
  4.8 4.2 %collective-permute-start = (f32[7,8,256]{2,1,0:T(8,128)S(1)}, f32[7,8,256]{2,1,0:T(8,128)S(1)}, u32[]{:S(2)}, u32[]{:S(2)}) collective-permute-start(f32[7,8,256]{2,1,0:T(8,128)S(1)} %get-tuple-element.26), channel_id=1, source_target_pairs={{0,8},{8,0},{16,24},{24,16},{1,9},{9,1},{17,25},{25,17},{2,10},{10... | collective-permute-start | bytes 172040 | tf_op jit(solution)/shard_map/ppermute | solution.py:519
  9.1 7.0 %collective-permute-start.2 = (f32[14,8,256]{2,1,0:T(8,128)S(1)}, f32[14,8,256]{2,1,0:T(8,128)S(1)}, u32[]{:S(2)}, u32[]{:S(2)}) collective-permute-start(f32[14,8,256]{2,1,0:T(8,128)S(1)} %get-tuple-element.15), channel_id=1, source_target_pairs={{1,2},{2,1},{3,4},{4,3},{5,6},{6,5},{7,0},{0,7},{9,10},{10,9},{11,... | collective-permute-start | bytes 344072 | tf_op jit(solution)/shard_map/ppermute | solution.py:531
  11.4 4.7 %collective-permute-start.3 = (f32[14,8,256]{2,1,0:T(8,128)S(1)}, f32[14,8,256]{2,1,0:T(8,128)S(1)}, u32[]{:S(2)}, u32[]{:S(2)}) collective-permute-start(f32[14,8,256]{2,1,0:T(8,128)S(1)} %get-tuple-element.16), channel_id=1, source_target_pairs={{0,1},{1,0},{2,3},{3,2},{4,5},{5,4},{6,7},{7,6},{8,9},{9,8},{10,11... | collective-permute-start | bytes 344072 | tf_op jit(solution)/shard_map/ppermute | solution.py:530
  30.2 1.5 %collective-permute-start.4 = (f32[64,8,128]{2,1,0:T(8,128)S(1)}, f32[64,8,128]{2,1,0:T(8,128)S(1)}, u32[]{:S(2)}, u32[]{:S(2)}) collective-permute-start(f32[64,8,128]{2,1,0:T(8,128)S(1)} %all_to_all.5.own_ref), channel_id=1, source_target_pairs={{0,1},{1,0},{2,3},{3,2},{4,5},{5,4},{6,7},{7,6},{8,9},{9,8},{10,11... | collective-permute-start | bytes 786440 | tf_op jit(solution)/shard_map/ppermute | solution.py:545

commit v3 on v2

--- a/solution.py
+++ b/solution.py
@@ -505,6 +505,20 @@
     return swaps
 
 
+def swaps(along_x, along_y, axis, first):
+    pairs = []
+    for x in range(along_x):
+        for y in range(along_y):
+            place, count = (x, along_x) if axis == "gx" else (y, along_y)
+            other = place + 1 if (place - first) % 2 == 0 else place - 1
+            if 0 <= other < count:
+                to = (other, y) if axis == "gx" else (x, other)
+            else:
+                to = (x, y ^ 1) if axis == "gx" else (x ^ 1, y)
+            pairs.append((x * along_y + y, to[0] * along_y + to[1]))
+    return pairs
+
+
 def body(right_side, coefficient):
     along_x, along_y = lax.axis_size("gx"), lax.axis_size("gy")
     rows, cols, depth = right_side.shape
@@ -517,7 +531,7 @@
     last = jnp.concatenate([right_side[rows - DEEP_F :], coefficient[rows - DEEP_C :]])
     a, b = jnp.where(odd, first, last), jnp.where(odd, last, first)
     a = lax.ppermute(a, "gx", pairs_from(0, along_x))
-    b = lax.ppermute(b, "gx", pairs_from(1, along_x))
+    b = lax.ppermute(b, ("gx", "gy"), swaps(along_x, along_y, "gx", 1))
 
     tall = rows + 2 * DEEP_F
     z, k = call(
@@ -528,7 +542,7 @@
         small,
     )
     k = lax.ppermute(k, "gy", pairs_from(0, along_y))
-    z = lax.ppermute(z, "gy", pairs_from(1, along_y))
+    z = lax.ppermute(z, ("gx", "gy"), swaps(along_x, along_y, "gy", 1))
 
     wide = (cols + 2 * DEEP_C, depth)
     half = (rows // 2, SUB, depth // 2)

time: 34.9 us -> 33.5 us (0.960)
  waiting for transfers between devices: 9.47 us -> 7.12 us
  blocking collectives: 13.1 us -> 14.6 us
  starting transfers between devices: 7.26 us -> 6.64 us
    ppermute x2, starting transfers between devices: 6.34 us -> 1.9 us  [the longest x1 1.38 us: body(): z = lax.ppermute(z, ('gx', 'gy'), swaps(along_x, along_y, 'gy', 1))]
    ppermute x1, starting transfers between devices: 0.54 us -> 3.98 us  [body(): a = lax.ppermute(a, 'gx', pairs_from(0, along_x))]
    ppermute x2, waiting for transfers between devices: 6.41 us -> 3.1 us  [the longest x1 3.1 us: body(): z = lax.ppermute(z, ('gx', 'gy'), swaps(along_x, along_y, 'gy', 1))]
    all_to_all x1, blocking collectives: 13.1 us -> 14.6 us  [body(): own = lax.all_to_all(send, ('gx', 'gy'), 0, 0, tiled=True)]
    ppermute x1, waiting for transfers between devices: 1.89 us -> 2.86 us  [body(): a = lax.ppermute(a, 'gx', pairs_from(0, along_x))]
    ppermute x1, starting transfers between devices: 0.01 us -> 0.37 us  [body(): k = lax.ppermute(k, 'gy', pairs_from(0, along_y))]
  transfers between devices with their start and end apart: 5 -> 5, of which waited for: 4 -> 3; matrix products, arithmetic and copies ran while one was open for 0% -> 0% of each run, Pallas kernels for 0% -> 0%
where the time goes in v3:
time: 33.5 us; the launch traced here: 33.3 us
  blocking collectives  14.6 us (44%)
  waiting for transfers between devices  7.12 us (21%)
  starting transfers between devices  6.64 us (20%)
  Pallas kernels  4.09 us (12%)
  local copies, waits for them, and re-layouts  0.85 us (3%)
    all_to_all x1, blocking collectives, body(): own = lax.all_to_all(send, ('gx', 'gy'), 0, 0, tiled=True)  14.6 us
    pallas_call x3, Pallas kernels, call(): pl.pallas_call(kernel, out_shape=[jax.ShapeDtypeStruct(s, F32) for s in o...  4.09 us
    ppermute x1, starting transfers between devices, body(): a = lax.ppermute(a, 'gx', pairs_from(0, along_x))  3.98 us
    ppermute x1, waiting for transfers between devices, body(): z = lax.ppermute(z, ('gx', 'gy'), swaps(along_x, along_y, 'gy', 1))  3.1 us
    ppermute x1, waiting for transfers between devices, body(): a = lax.ppermute(a, 'gx', pairs_from(0, along_x))  2.86 us
    ppermute x1, starting transfers between devices, body(): z = lax.ppermute(z, ('gx', 'gy'), swaps(along_x, along_y, 'gy', 1))  1.38 us
    ppermute x1, waiting for transfers between devices, body(): other = lax.ppermute(own, 'gy', pairs_from(0, along_y))  1.16 us
    slice x2, local copies, waits for them, and re-layouts, body(): first = jnp.concatenate([right_side[:DEEP_F], coefficient[:DEEP_C]])  0.79 us
  transfers between devices with their start and end apart: 5, of which 3 were waited for; matrix products, arithmetic and copies ran while one was open for 0% of the time, Pallas kernels for 0%

profile of v3, /device:TPU:0, one launch (start us, length us, event | category | flops | bytes accessed | tf_op | source)
XLA Modules:
  0.0 33.3 jit_solution(16803400046182627217)
XLA Ops:
  0.0 0.0 copy-start
  0.0 0.8 %fusion.2 = (f32[3,8,256]{2,1,0:T(8,128)S(1)}, f32[3,8,256]{2,1,0:T(8,128)S(1)}) fusion(f32[8,8,256]{2,1,0:T(8,128)} %f_ref.3), kind=kLoop, calls=%fused_computation.4 | loop fusion | bytes 98304 | tf_op jit(solution)/shard_map/slice | solution.py:530
  0.8 0.0 copy-done
  0.8 0.0 copy-start.1
  0.9 0.5 %collective-permute-start.1 = (f32[7,8,256]{2,1,0:T(8,128)S(1)}, f32[7,8,256]{2,1,0:T(8,128)S(1)}, u32[]{:S(2)}, u32[]{:S(2)}) collective-permute-start(f32[7,8,256]{2,1,0:T(8,128)S(1)} %get-tuple-element.25), channel_id=1, source_target_pairs={{0,1},{1,0},{2,3},{3,2},{4,5},{5,4},{6,7},{7,6},{8,16},{9,17},{10,... | collective-permute-start | bytes 172040 | tf_op jit(solution)/shard_map/ppermute | solution.py:534
  1.4 4.0 %collective-permute-start = (f32[7,8,256]{2,1,0:T(8,128)S(1)}, f32[7,8,256]{2,1,0:T(8,128)S(1)}, u32[]{:S(2)}, u32[]{:S(2)}) collective-permute-start(f32[7,8,256]{2,1,0:T(8,128)S(1)} %get-tuple-element.26), channel_id=1, source_target_pairs={{0,8},{8,0},{16,24},{24,16},{1,9},{9,1},{17,25},{25,17},{2,10},{10... | collective-permute-start | bytes 172040 | tf_op jit(solution)/shard_map/ppermute | solution.py:533
  5.4 0.0 collective-permute-done.1.b_ref
  5.4 2.9 %collective-permute-done.a_ref = f32[7,8,256]{2,1,0:T(8,128)S(1)} collective-permute-done((f32[7,8,256]{2,1,0:T(8,128)S(1)}, f32[7,8,256]{2,1,0:T(8,128)S(1)}, u32[]{:S(2)}, u32[]{:S(2)}) %collective-permute-start) | collective-permute-done | bytes 57376 | tf_op jit(solution)/shard_map/ppermute | solution.py:533
  8.2 0.0 copy-done.1
  8.3 1.4 %collective-permute-start.2 = (f32[14,8,256]{2,1,0:T(8,128)S(1)}, f32[14,8,256]{2,1,0:T(8,128)S(1)}, u32[]{:S(2)}, u32[]{:S(2)}) collective-permute-start(f32[14,8,256]{2,1,0:T(8,128)S(1)} %get-tuple-element.15), channel_id=1, source_target_pairs={{0,8},{1,2},{2,1},{3,4},{4,3},{5,6},{6,5},{7,15},{8,0},{9,10},{10,... | collective-permute-start | bytes 344072 | tf_op jit(solution)/shard_map/ppermute | solution.py:545
  9.7 0.4 %collective-permute-start.3 = (f32[14,8,256]{2,1,0:T(8,128)S(1)}, f32[14,8,256]{2,1,0:T(8,128)S(1)}, u32[]{:S(2)}, u32[]{:S(2)}) collective-permute-start(f32[14,8,256]{2,1,0:T(8,128)S(1)} %get-tuple-element.16), channel_id=1, source_target_pairs={{0,1},{1,0},{2,3},{3,2},{4,5},{5,4},{6,7},{7,6},{8,9},{9,8},{10,11... | collective-permute-start | bytes 344072 | tf_op jit(solution)/shard_map/ppermute | solution.py:544
  10.0 3.1 %collective-permute-done.2.z_ref = f32[14,8,256]{2,1,0:T(8,128)S(1)} collective-permute-done((f32[14,8,256]{2,1,0:T(8,128)S(1)}, f32[14,8,256]{2,1,0:T(8,128)S(1)}, u32[]{:S(2)}, u32[]{:S(2)}) %collective-permute-start.2) | collective-permute-done | bytes 114720 | tf_op jit(solution)/shard_map/ppermute | solution.py:545
  13.1 0.0 collective-permute-done.3.k_ref
  13.1 1.0 %shard_map.29 = (f32[64,8,128]{2,1,0:T(8,128)S(1)}, f32[12,16,256]{2,1,0:T(8,128)S(1)}, f32[14,16,256]{2,1,0:T(8,128)S(1)}, f32[15,16,256]{2,1,0:T(8,128)S(1)}, ...) custom-call(f32[8,8,256]{2,1,0:T(8,128)S(1)} %copy-done.1, ...), custom_call_target="tpu_custom_call" | custom-call | tf_op jit(solution)/shard_map/pallas_call | solution.py:73
  14.1 14.6 %all_to_all.5.own_ref = f32[64,8,128]{2,1,0:T(8,128)S(1)} all-to-all(f32[64,8,128]{2,1,0:T(8,128)S(1)} %get-tuple-element.17), channel_id=1, replica_groups=mesh['gx'=4,'gy'=8] {'gx','gy'}, dimensions={0} | all-to-all | bytes 524288 | tf_op jit(solution)/shard_map/all_to_all | solution.py:558
  28.7 0.4 %collective-permute-start.4 = (f32[64,8,128]{2,1,0:T(8,128)S(1)}, f32[64,8,128]{2,1,0:T(8,128)S(1)}, u32[]{:S(2)}, u32[]{:S(2)}) collective-permute-start(f32[64,8,128]{2,1,0:T(8,128)S(1)} %all_to_all.5.own_ref), channel_id=1, source_target_pairs={{0,1},{1,0},{2,3},{3,2},{4,5},{5,4},{6,7},{7,6},{8,9},{9,8},{10,11... | collective-permute-start | bytes 786440 | tf_op jit(solution)/shard_map/ppermute | solution.py:559
  29.1 1.2 %collective-permute-done.4.other_ref = f32[64,8,128]{2,1,0:T(8,128)S(1)} collective-permute-done((f32[64,8,128]{2,1,0:T(8,128)S(1)}, f32[64,8,128]{2,1,0:T(8,128)S(1)}, u32[]{:S(2)}, u32[]{:S(2)}) %collective-permute-start.4) | collective-permute-done | bytes 262176 | tf_op jit(solution)/shard_map/ppermute | solution.py:559
  30.3 3.0 %shard_map.30 = f32[8,8,256]{2,1,0:T(8,128)} custom-call(f32[64,8,128]{2,1,0:T(8,128)S(1)} %all_to_all.5.own_ref, f32[64,8,128]{2,1,0:T(8,128)S(1)} %collective-permute-done.4.other_ref, f32[12,16,256]{2,1,0:T(8,128)S(1)} %get-tuple-element.18.u0_ref, f32[14,16,256]{2,1,0:T(8,128)S(1)} %get-tuple-element.19.fx_ref, ...), custom_call_target="tpu_custom_call" | custom-call | tf_op jit(solution)/shard_map/pallas_call | solution.py:73
  (3 shorter events, 0.1 us)
Async XLA Ops:
  0.0 0.8 %copy-start = (f32[8,8,256]{2,1,0:T(8,128)S(1)}, f32[8,8,256]{2,1,0:T(8,128)}, u32[]{:S(2)}) copy-start(f32[8,8,256]{2,1,0:T(8,128)} %c_ref.3) | copy-start | bytes 196612
  0.8 7.4 %copy-start.1 = (f32[8,8,256]{2,1,0:T(8,128)S(1)}, f32[8,8,256]{2,1,0:T(8,128)}, u32[]{:S(2)}) copy-start(f32[8,8,256]{2,1,0:T(8,128)} %f_ref.3) | copy-start | bytes 196612
  0.9 4.5 %collective-permute-start.1 = (f32[7,8,256]{2,1,0:T(8,128)S(1)}, f32[7,8,256]{2,1,0:T(8,128)S(1)}, u32[]{:S(2)}, u32[]{:S(2)}) collective-permute-start(f32[7,8,256]{2,1,0:T(8,128)S(1)} %get-tuple-element.25), channel_id=1, source_target_pairs={{0,1},{1,0},{2,3},{3,2},{4,5},{5,4},{6,7},{7,6},{8,16},{9,17},{10,... | collective-permute-start | bytes 172040 | tf_op jit(solution)/shard_map/ppermute | solution.py:534
  1.4 6.8 %collective-permute-start = (f32[7,8,256]{2,1,0:T(8,128)S(1)}, f32[7,8,256]{2,1,0:T(8,128)S(1)}, u32[]{:S(2)}, u32[]{:S(2)}) collective-permute-start(f32[7,8,256]{2,1,0:T(8,128)S(1)} %get-tuple-element.26), channel_id=1, source_target_pairs={{0,8},{8,0},{16,24},{24,16},{1,9},{9,1},{17,25},{25,17},{2,10},{10... | collective-permute-start | bytes 172040 | tf_op jit(solution)/shard_map/ppermute | solution.py:533
  8.3 4.9 %collective-permute-start.2 = (f32[14,8,256]{2,1,0:T(8,128)S(1)}, f32[14,8,256]{2,1,0:T(8,128)S(1)}, u32[]{:S(2)}, u32[]{:S(2)}) collective-permute-start(f32[14,8,256]{2,1,0:T(8,128)S(1)} %get-tuple-element.15), channel_id=1, source_target_pairs={{0,8},{1,2},{2,1},{3,4},{4,3},{5,6},{6,5},{7,15},{8,0},{9,10},{10,... | collective-permute-start | bytes 344072 | tf_op jit(solution)/shard_map/ppermute | solution.py:545
  9.7 3.5 %collective-permute-start.3 = (f32[14,8,256]{2,1,0:T(8,128)S(1)}, f32[14,8,256]{2,1,0:T(8,128)S(1)}, u32[]{:S(2)}, u32[]{:S(2)}) collective-permute-start(f32[14,8,256]{2,1,0:T(8,128)S(1)} %get-tuple-element.16), channel_id=1, source_target_pairs={{0,1},{1,0},{2,3},{3,2},{4,5},{5,4},{6,7},{7,6},{8,9},{9,8},{10,11... | collective-permute-start | bytes 344072 | tf_op jit(solution)/shard_map/ppermute | solution.py:544
  28.7 1.5 %collective-permute-start.4 = (f32[64,8,128]{2,1,0:T(8,128)S(1)}, f32[64,8,128]{2,1,0:T(8,128)S(1)}, u32[]{:S(2)}, u32[]{:S(2)}) collective-permute-start(f32[64,8,128]{2,1,0:T(8,128)S(1)} %all_to_all.5.own_ref), channel_id=1, source_target_pairs={{0,1},{1,0},{2,3},{3,2},{4,5},{5,4},{6,7},{7,6},{8,9},{9,8},{10,11... | collective-permute-start | bytes 786440 | tf_op jit(solution)/shard_map/ppermute | solution.py:559

commit v4 on v3

--- a/solution.py
+++ b/solution.py
@@ -1,4 +1,5 @@
 import functools
+import math
 
 import jax
 import jax.numpy as jnp
@@ -38,16 +39,15 @@
 
 
 def each(count, registers, step):
-    if count * registers <= WRITTEN_OUT:
-        for i in range(count):
-            step(i)
-    else:
-
-        def one(i, carry):
-            step(i)
-            return carry
-
-        lax.fori_loop(0, count, one, 0)
+    each_sum(count, registers, lambda i, carry: (step(i), carry)[1], 0)
+
+
+def each_sum(count, registers, step, carry):
+    if count * registers > WRITTEN_OUT:
+        return lax.fori_loop(0, count, step, carry)
+    for i in range(count):
+        carry = step(i, carry)
+    return carry
 
 
 def turn(value, amount, axis):
@@ -58,11 +58,20 @@
     return lax.broadcasted_iota(jnp.int32, shape, axis)
 
 
-def beside(v, below, above, w_below, w_above, w_cols, w_depth, stride=1):
+def beside(v, below, above, w_below, w_above, w_cols, w_depth):
+    span = below.shape[0]
     out = w_above * above + w_below * below
-    out = out + w_cols * turn(v, -1, 0)
-    out = out + w_depth * turn(v, -stride, 1)
-    return out + turn(w_cols * v, 1, 0) + turn(w_depth * v, stride, 1)
+    out = out + w_cols[:span] * turn(v, -1, 0)[:span]
+    out = out + turn(w_cols * v, 1, 0)[:span]
+    v = v[:span]
+    return out + w_depth * turn(v, -1, 1) + turn(w_depth * v, 1, 1)
+
+
+def inside_cols(col, cols, along_y):
+    gy = lax.axis_index("gy")
+    after = (col >= cols) & (col < cols + DEEP_C) & (gy == along_y - 1)
+    before = (col >= cols + DEEP_C) & (gy == 0)
+    return jnp.logical_not(after | before)
 
 
 def exact_dot(a, b):
@@ -128,20 +137,32 @@
     rows = f_ref.shape[0]
     f_row, c_row = row_sources(along_x, rows, f_ref, c_ref, a_ref, b_ref)
     odd = lax.rem(lax.axis_index("gy"), 2) == 1
-    low_half = iota(f_ref.shape[1:], 0) < DEEP_C
-    for t in range(rows + 2 * DEEP_F):
-        f, c = f_row(t - DEEP_F), c_row(t - DEEP_F)
-        first = jnp.where(low_half, c, turn(f, DEEP_C, 0))
-        last = jnp.where(low_half, turn(c, DEEP_C, 0), f)
+    sub = iota(f_ref.shape[1:], 0)
+    low_half = sub < DEEP_C
+
+    def put(t, first, last):
         z_ref[t] = jnp.where(odd, last, first)
         k_ref[t] = jnp.where(odd, first, last)
+
+    for t in range(rows + 2):
+        f, c = turn(f_row(t - 1), DEEP_C, 0), c_row(t - 1)
+        put(t, jnp.where(low_half, c, f), jnp.where(low_half, f, c))
+
+    def corners(sub, way):
+        near, near_f, far = c_row(-2), f_row(-2), c_row(-3)
+        out = jnp.where(sub < 2, near, jnp.where(sub == 2, turn(near_f, 2 * way, 0), turn(far, 3 * way, 0)))
+        near, near_f, far = c_row(rows + 1), f_row(rows + 1), c_row(rows + 2)
+        out = jnp.where(sub < 4, out, jnp.where(sub < 6, turn(near, 4 * way, 0), turn(near_f, 6 * way, 0)))
+        return jnp.where(sub < 7, out, turn(far, 7 * way, 0))
+
+    put(rows + 2, corners(sub, 1), corners(SUB - 1 - sub, -1))
 
 
 def fine_down(
     along_x, along_y, copies,
     f_ref, c_ref, a_ref, b_ref, z_ref, k_ref,
-    send_ref, u_ref, fx_ref, wx_ref, wy_ref, wz_ref, diag_ref, inv_ref,
-    cx_ref, v_ref, r_ref,
+    send_ref, u_ref, fx_ref, wx_ref, wy_ref, wz_ref, inv_ref,
+    cx_ref, v_ref, diag_ref,
 ):
     rows, cols, depth = f_ref.shape
     f_row, c_row = row_sources(along_x, rows, f_ref, c_ref, a_ref, b_ref)
@@ -153,26 +174,35 @@
     wide = (cols + 2 * DEEP_C, depth)
     lane = iota(wide, 1)
     col = iota(wide, 0)
-    col_inside = ((col >= DEEP_C) | (gy > 0)) & (
-        (col < DEEP_C + cols) | (gy < along_y - 1)
-    )
+    col_inside = inside_cols(col, cols, along_y)
     inv_mid, ((keep, push),) = chebyshev(SMOOTH_LOW, SMOOTH_HIGH, SMOOTH)
 
+    def sides(t):
+        left = jnp.where(odd, k_ref[t], z_ref[t]) * has_left
+        return left, jnp.where(odd, z_ref[t], k_ref[t]) * has_right
+
+    corner_tiles = sides(rows + 2)
     for t in range(rows + 2 * DEEP_C):
         row = t - DEEP_C
-        c = c_row(row)
-        turned = turn(c, DEEP_C, 0)
+        cx_ref[t, 0:cols] = c_row(row)
         s = row + DEEP_F
+        if -1 <= row <= rows:
+            left, right = sides(row + 1)
+            cx_ref[t, cols:] = jnp.where(low_half, right, left)
+            f = turn(jnp.where(low_half, left, right), DEEP_C, 0)
+        else:
+            left, right = corner_tiles
+            c_turn = {-2: 0, -3: 3, rows + 1: 4, rows + 2: 7}.get(row)
+            f_turn = {-2: 2, rows + 1: 6}.get(row)
+            c = f = jnp.zeros((cols, depth), F32)
+            if c_turn is not None:
+                c = jnp.where(low_half, turn(right, -c_turn, 0), turn(left, c_turn, 0))
+            if f_turn is not None:
+                f = jnp.where(low_half, turn(right, -f_turn, 0), turn(left, f_turn, 0))
+            cx_ref[t, cols:] = c
         if 0 <= s < rows + 2 * DEEP_F:
-            left = jnp.where(odd, k_ref[s], z_ref[s]) * has_left
-            right = jnp.where(odd, z_ref[s], k_ref[s]) * has_right
-            f = f_row(row)
-            fx_ref[s, 0:cols] = turn(jnp.where(low_half, f, left), DEEP_C, 0)
-            fx_ref[s, cols:] = jnp.where(low_half, turn(f, DEEP_C, 0), right)
-        else:
-            left = right = jnp.zeros_like(c)
-        cx_ref[t, 0:cols] = jnp.where(low_half, left, turned)
-        cx_ref[t, cols:] = jnp.where(low_half, turned, turn(right, DEEP_C, 0))
+            fx_ref[s, 0:cols] = f_row(row)
+            fx_ref[s, cols:] = f
 
     tall = rows + 2 * DEEP_F
     wx_ref[0] = 0.5 * (cx_ref[0] + cx_ref[1])
@@ -194,26 +224,28 @@
         inv = jnp.where(inside, 1.0 / diag, 0.0)
         wy_ref[s] = w_cols
         wz_ref[s] = w_depth
-        diag_ref[s] = diag
+        if DEEP_F <= s < DEEP_F + rows:
+            diag_ref[s - DEEP_F] = diag[:cols]
         inv_ref[s] = inv
         v_ref[s] = fx_ref[s] * inv * inv_mid
 
-    def residual(x_ref, shift, s):
-        x = x_ref[s - shift]
+    def pulled(x_ref, shift, s, span):
+        at = s - shift
         total = beside(
-            x, x_ref[s - shift - 1], x_ref[s - shift + 1],
-            wx_ref[s], wx_ref[s + 1], wy_ref[s], wz_ref[s],
+            x_ref[at], x_ref[at - 1, :span], x_ref[at + 1, :span],
+            wx_ref[s, :span], wx_ref[s + 1, :span], wy_ref[s], wz_ref[s, :span],
         )
-        return x, fx_ref[s] - (diag_ref[s] * x - total)
+        return fx_ref[s, :span] + total
 
     for s in range(1, tall - 1):
-        v, r = residual(v_ref, 0, s)
-        u_ref[s - 1] = v + (keep * v + push * (r * inv_ref[s]))
-    for i in range(rows):
-        _, r_ref[i] = residual(u_ref, 1, i + DEEP_F)
+        total = pulled(v_ref, 0, s, wide[0])
+        u_ref[s - 1] = (1.0 + keep - push) * v_ref[s] + push * (inv_ref[s] * total)
+
+    def residual(s):
+        return pulled(u_ref, 1, s, cols) - diag_ref[s - DEEP_F] * u_ref[s - 1, :cols]
 
     half_rows = rows // 2
-    summed = [r_ref[2 * i] + r_ref[2 * i + 1] for i in range(half_rows)]
+    summed = [residual(2 * i + DEEP_F) + residual(2 * i + 1 + DEEP_F) for i in range(half_rows)]
     summed += [c_ref[2 * i] + c_ref[2 * i + 1] for i in range(half_rows)]
     summed = jnp.concatenate(summed, axis=0)
     pairs = (depth, depth // 2)
@@ -224,8 +256,8 @@
     half_cols = cols // 2
     f_half = (place >= half_cols) == odd
     place = place % half_cols
-    f_from = wide[0] * block + DEEP_C + 2 * place
-    c_from = wide[0] * half_rows + cols * block + 2 * place
+    f_from = cols * block + 2 * place
+    c_from = f_from + cols * half_rows
     from_f = (source == f_from) | (source == f_from + 1)
     from_c = (source == c_from) | (source == c_from + 1)
     picker = jnp.where(f_half, jnp.where(from_f, 0.5, 0.0), jnp.where(from_c, 0.125, 0.0))
@@ -239,11 +271,11 @@
 
 def coarse_and_up(
     along_x, along_y,
-    own_ref, other_ref, u0_ref, fx_ref, wx0_ref, wy0_ref, wz0_ref, diag0_ref, inv0_ref,
+    own_ref, other_ref, u0_ref, fx_ref, wx0_ref, wy0_ref, wz0_ref, inv0_ref,
     out_ref,
     f_ref, c_ref, wx_ref, wy_ref, wz_ref, diag_ref, inv_ref, v_ref,
-    f2_ref, c2_ref, wx2_ref, wy2_ref, wz2_ref, diag2_ref, inv2_ref, d2_ref, e2_ref, e3_ref,
-    py_ref, vw_ref, dw_ref, vx_ref, e1_ref, yy_ref, v0_ref, d0_ref, x0_ref, o_ref,
+    f2_ref, c2_ref, diag2_ref, d2_ref, e2_ref, e3_ref, a2_ref,
+    py_ref, vw_ref, dw_ref, vx_ref, e1_ref, yy_ref, v0_ref, d0_ref, x0_ref,
 ):
     gx, gy = lax.axis_index("gx"), lax.axis_index("gy")
     odd = lax.rem(gy, 2) == 1
@@ -284,13 +316,13 @@
         w_depth = jnp.where(lane >= shape[1] - stride, 0.0, half + turn(half, -stride, 1))
         edge = jnp.where((col == 0) | (col == shape[0] - 1), half, 0.0)
         edge = edge + jnp.where((lane < stride) | (lane >= shape[1] - stride), half, 0.0)
-        diag = half + 0.5 * below + w_above + w_cols + turn(w_cols, 1, 0)
-        diag = diag + w_depth + turn(w_depth, stride, 1) + edge
-        return w_above, w_cols, w_depth, diag
+        w_below, w_before, w_back = half + 0.5 * below, turn(w_cols, 1, 0), turn(w_depth, stride, 1)
+        diag = w_below + w_above + w_cols + w_before + w_depth + w_back + edge
+        return (w_below, w_above, w_cols, w_before, w_depth, w_back), diag, edge
 
     def weigh1(i):
         row = PAD + i
-        w_above, w_cols, w_depth, diag = weigh(
+        (_, w_above, w_cols, _, w_depth, _), diag, _ = weigh(
             c_ref[row], c_ref[row - 1], c_ref[row + 1], shape1, 1
         )
         inv = 1.0 / diag
@@ -323,87 +355,75 @@
     each(rows2, 2 * registers1, restrict_c)
     u_ref = c_ref
 
-    def residual1(x_ref, at, row):
-        x = x_ref[at]
-        total = beside(
-            x, x_ref[at - 1], x_ref[at + 1],
+    def pulled1(x_ref, at, row):
+        return f_ref[row] + beside(
+            x_ref[at], x_ref[at - 1], x_ref[at + 1],
             wx_ref[row], wx_ref[row + 1], wy_ref[row], wz_ref[row],
         )
-        return x, f_ref[row] - (diag_ref[row] * x - total)
 
     def second1(i):
         row = PAD + i
-        v, r = residual1(v_ref, row, row)
-        u_ref[row] = v + (keep * v + push * (r * inv_ref[row]))
+        total = pulled1(v_ref, row, row)
+        u_ref[row] = (1.0 + keep - push) * v_ref[row] + push * (inv_ref[row] * total)
 
     each(rows1, registers1, second1)
+
+    def residual1(row):
+        return pulled1(u_ref, row, row) - diag_ref[row] * u_ref[row]
 
     def restrict(k):
         row = PAD + 2 * k
-        _, first = residual1(u_ref, row, row)
-        _, second = residual1(u_ref, row + 1, row + 1)
-        v_ref[k] = first + second
+        v_ref[k] = residual1(row) + residual1(row + 1)
         f2_ref[k] = 0.5 * fold(v_ref, k)
 
     each(rows2, 2 * registers1, restrict)
     c2_ref[0] = zero2
     c2_ref[rows2 + 1] = zero2
-    wx2_ref[0] = 0.5 * c2_ref[1]
     for ref in (e2_ref, e3_ref):
         ref[0] = zero2
         ref[rows2 + 1] = zero2
     inv_mid2, pairs2 = chebyshev(COARSE_LOW, COARSE_HIGH, COARSE_STEPS)
 
-    def weigh2(k):
-        w_above, w_cols, w_depth, diag = weigh(
-            c2_ref[k + 1], c2_ref[k], c2_ref[k + 2], shape2, 2
-        )
+    def weigh2(k, edges):
+        shares, diag, edge = weigh(c2_ref[k + 1], c2_ref[k], c2_ref[k + 2], shape2, 2)
         inv = 1.0 / diag
-        wx2_ref[k + 1] = w_above
-        wy2_ref[k] = w_cols
-        wz2_ref[k] = w_depth
+        for at, share in enumerate(shares):
+            a2_ref[at, k] = share * inv
         diag2_ref[k] = diag
-        inv2_ref[k] = inv
-        d = f2_ref[k] * inv * inv_mid2
+        scaled = f2_ref[k] * inv
+        f2_ref[k] = scaled
+        d = scaled * inv_mid2
         d2_ref[k] = d
         e2_ref[k + 1] = d
-
-    each(rows2, registers2, weigh2)
+        half = 0.5 * c2_ref[k + 1]
+        edge = edge + jnp.where(k == 0, half, 0.0) + jnp.where(k == rows2 - 1, half, 0.0)
+        return edges + edge
+
+    edges = each_sum(rows2, registers2, weigh2, zero2)
 
     def residual2(e_ref, k):
         e = e_ref[k + 1]
-        total = beside(
-            e, e_ref[k], e_ref[k + 2], wx2_ref[k], wx2_ref[k + 1], wy2_ref[k], wz2_ref[k], 2
-        )
-        return e, f2_ref[k] - (diag2_ref[k] * e - total)
+        r = f2_ref[k] - e + a2_ref[0, k] * e_ref[k] + a2_ref[1, k] * e_ref[k + 2]
+        r = r + (a2_ref[2, k] * turn(e, -1, 0) + a2_ref[3, k] * turn(e, 1, 0))
+        return r + (a2_ref[4, k] * turn(e, -2, 1) + a2_ref[5, k] * turn(e, 2, 1))
 
     now_ref, next_ref = e2_ref, e3_ref
     for keep2, push2 in pairs2:
 
         def step2(k):
-            e, r = residual2(now_ref, k)
-            d = keep2 * d2_ref[k] + push2 * (r * inv2_ref[k])
+            d = keep2 * d2_ref[k] + push2 * residual2(now_ref, k)
             d2_ref[k] = d
-            next_ref[k + 1] = e + d
+            next_ref[k + 1] = now_ref[k + 1] + d
 
         each(rows2, registers2, step2)
         now_ref, next_ref = next_ref, now_ref
 
-    def gather_sums(k, sums):
-        _, r = residual2(now_ref, k)
-        total = wx2_ref[k] * (k > 0) + wx2_ref[k + 1] * (k < rows2 - 1)
-        total = total + wy2_ref[k] + turn(wy2_ref[k], 1, 0)
-        total = total + wz2_ref[k] + turn(wz2_ref[k], 2, 1)
-        return sums[0] + r, sums[1] + (diag2_ref[k] - total)
-
-    sums = (zero2, zero2)
-    if rows2 * registers2 <= WRITTEN_OUT:
-        for k in range(rows2):
-            sums = gather_sums(k, sums)
-    else:
-        sums = lax.fori_loop(0, rows2, gather_sums, sums)
-    top = jnp.sum(sums[0], axis=(0, 1), keepdims=True)
-    bottom = jnp.sum(sums[1], axis=(0, 1), keepdims=True)
+    def add_residual(k, total):
+        return total + diag2_ref[k] * residual2(now_ref, k)
+
+    total = each_sum(rows2, registers2, add_residual, zero2)
+    top = jnp.sum(total, axis=(0, 1), keepdims=True)
+    bottom = jnp.sum(edges, axis=(0, 1), keepdims=True)
     mean = top / bottom
 
     span = brick1 + 2 * PAD
@@ -432,8 +452,8 @@
         vw_ref[m] = jnp.where(inside1(m), total, 0.0)
     for m in range(1, span - 1):
         row = PAD + start + m
-        v, r = residual1(vw_ref, m, row)
-        d = r * inv_ref[row] * inv_mid
+        v = vw_ref[m]
+        d = (inv_ref[row] * pulled1(vw_ref, m, row) - v) * inv_mid
         dw_ref[m] = d
         vx_ref[m] = jnp.where(inside1(m), v + d, 0.0)
     margin = SUB
@@ -441,8 +461,8 @@
     e1_ref[:, margin + cols1 :, :] = jnp.zeros((span - 4, margin, depth1), F32)
     for m in range(2, span - 2):
         row = PAD + start + m
-        v, r = residual1(vx_ref, m, row)
-        e = v + (keep * dw_ref[m] + push * (r * inv_ref[row]))
+        total = inv_ref[row] * pulled1(vx_ref, m, row)
+        e = (1.0 - push) * vx_ref[m] + (keep * dw_ref[m] + push * total)
         e1_ref[m - 2, margin : margin + cols1, :] = jnp.where(inside1(m), e, 0.0)
 
     rows, cols, depth = out_ref.shape
@@ -450,7 +470,7 @@
     half_wide = wide[0] // 2
     first_col = margin + gy * (cols // 2) - DEEP_C // 2
     for k in range(span - 4):
-        e = e1_ref[k, pl.ds(first_col, half_wide), :]
+        e = turn(e1_ref[k, pl.ds(first_col, half_wide), :], -(DEEP_C // 2), 0)
         at = k * wide[0]
         yy_ref[pl.ds(at, half_wide, stride=2), :] = 0.75 * e + 0.25 * turn(e, 1, 0)
         yy_ref[pl.ds(at + 1, half_wide, stride=2), :] = 0.75 * e + 0.25 * turn(e, -1, 0)
@@ -460,10 +480,7 @@
     near_cell = jnp.where(to_cell % 2 == 0, home - 1, home + 1)
     weights = jnp.where(from_cell == home, 0.75, 0.0) + jnp.where(from_cell == near_cell, 0.25, 0.0)
     carried = exact_dot(yy_ref[...], weights).reshape(span - 4, wide[0], depth)
-    col = iota(wide, 0)
-    col_inside = ((col >= DEEP_C) | (gy > 0)) & (
-        (col < DEEP_C + cols) | (gy < along_y - 1)
-    )
+    col_inside = inside_cols(iota(wide, 0), cols, along_y)
     for s in range(1, rows + 2 * DEEP_F - 1):
         row = s - DEEP_F
         near = row // 2 + 2
@@ -476,25 +493,21 @@
         total = u0_ref[s - 1] + (0.75 * carried[near] + 0.25 * carried[far])
         v0_ref[s] = jnp.where(inside, total, 0.0)
 
-    def residual0(x_ref, s):
-        x = x_ref[s]
-        total = beside(
-            x, x_ref[s - 1], x_ref[s + 1],
-            wx0_ref[s], wx0_ref[s + 1], wy0_ref[s], wz0_ref[s],
+    def pulled0(x_ref, s, span):
+        return fx_ref[s, :span] + beside(
+            x_ref[s], x_ref[s - 1, :span], x_ref[s + 1, :span],
+            wx0_ref[s, :span], wx0_ref[s + 1, :span], wy0_ref[s], wz0_ref[s, :span],
         )
-        return x, fx_ref[s] - (diag0_ref[s] * x - total)
 
     for s in range(2, rows + 2 * DEEP_F - 2):
-        v, r = residual0(v0_ref, s)
-        d = r * inv0_ref[s] * inv_mid
-        d0_ref[s] = d
+        v = v0_ref[s]
+        d = (inv0_ref[s] * pulled0(v0_ref, s, wide[0]) - v) * inv_mid
+        d0_ref[s] = d[:cols]
         x0_ref[s] = v + d
     for i in range(rows):
         s = i + DEEP_F
-        v, r = residual0(x0_ref, s)
-        o_ref[i] = v + (keep * d0_ref[s] + push * (r * inv0_ref[s]))
-    for i in range(rows):
-        out_ref[i] = o_ref[i, DEEP_C : DEEP_C + cols, :]
+        total = inv0_ref[s, :cols] * pulled0(x0_ref, s, cols)
+        out_ref[i] = (1.0 - push) * x0_ref[s, :cols] + (keep * d0_ref[s] + push * total)
 
 
 def pairs_from(first, count):
@@ -536,7 +549,7 @@
     tall = rows + 2 * DEEP_F
     z, k = call(
         functools.partial(pack_cols, along_x),
-        [(tall, cols, depth)] * 2,
+        [(rows + 3, cols, depth)] * 2,
         [],
         (right_side, coefficient, a, b),
         small,
@@ -550,8 +563,8 @@
     send, *state = call(
         functools.partial(fine_down, along_x, along_y, copies),
         [(copies * half[0],) + half[1:], (tall - 2,) + wide, (tall,) + wide, (tall + 1,) + wide]
-        + [(tall,) + wide] * 4,
-        [(tall + 2,) + wide, (tall,) + wide, (rows,) + wide],
+        + [(tall,) + wide] * 3,
+        [(tall + 2,) + wide, (tall,) + wide, (rows, cols, depth)],
         (right_side, coefficient, a, b, z, k),
         small + 2 * 4 * copies * half[0] * half[1] * half[2],
     )
@@ -564,11 +577,11 @@
     whole2 = (rows2 + 2, cols2, depth1)
     span = half[0] + 2 * PAD
     line = (cols1, depth1)
-    scratch = [(rows1 + 2 * PAD,) + line] + [whole1] * 7 + [whole2] * 10
+    scratch = [(rows1 + 2 * PAD,) + line] + [whole1] * 7 + [whole2] * 6 + [(6, rows2) + whole2[1:]]
     scratch += [(span // 2 + 2,) + line] + [(span,) + line] * 3
     scratch += [(span - 4, cols1 + 2 * SUB, depth1), ((span - 4) * wide[0], depth1)]
-    scratch += [(tall,) + wide] * 3 + [(rows,) + wide]
-    size = sum(4 * s[0] * s[1] * (s[2] if len(s) == 3 else 1) for s in scratch)
+    scratch += [(tall,) + wide, (tall, cols, depth), (tall,) + wide]
+    size = sum(4 * math.prod(s) for s in scratch)
     size += 2 * 4 * own.size + 4 * 8 * tall * wide[0] * wide[1]
     (out,) = call(
         functools.partial(coarse_and_up, along_x, along_y),

time: 33.5 us -> 32.9 us (0.982)
  Pallas kernels: 4.09 us -> 3.75 us
    pallas_call x3, Pallas kernels: 4.09 us -> 3.75 us  [call(): pl.pallas_call(kernel, out_shape=[jax.ShapeDtypeStruct(s, F32) for s in o...]
where the time goes in v4:
time: 32.9 us; the launch traced here: 32.7 us
  blocking collectives  14.6 us (44%)
  waiting for transfers between devices  6.86 us (21%)
  starting transfers between devices  6.64 us (20%)
  Pallas kernels  3.75 us (11%)
  local copies, waits for them, and re-layouts  0.85 us (3%)
    all_to_all x1, blocking collectives, body(): own = lax.all_to_all(send, ('gx', 'gy'), 0, 0, tiled=True)  14.6 us
    ppermute x1, starting transfers between devices, body(): a = lax.ppermute(a, 'gx', pairs_from(0, along_x))  3.98 us
    pallas_call x3, Pallas kernels, call(): pl.pallas_call(kernel, out_shape=[jax.ShapeDtypeStruct(s, F32) for s in o...  3.75 us
    ppermute x1, waiting for transfers between devices, body(): a = lax.ppermute(a, 'gx', pairs_from(0, along_x))  2.86 us
    ppermute x1, waiting for transfers between devices, body(): z = lax.ppermute(z, ('gx', 'gy'), swaps(along_x, along_y, 'gy', 1))  2.84 us
    ppermute x1, starting transfers between devices, body(): z = lax.ppermute(z, ('gx', 'gy'), swaps(along_x, along_y, 'gy', 1))  1.38 us
    ppermute x1, waiting for transfers between devices, body(): other = lax.ppermute(own, 'gy', pairs_from(0, along_y))  1.16 us
    slice x2, local copies, waits for them, and re-layouts, body(): first = jnp.concatenate([right_side[:DEEP_F], coefficient[:DEEP_C]])  0.79 us
  transfers between devices with their start and end apart: 5, of which 3 were waited for; matrix products, arithmetic and copies ran while one was open for 0% of the time, Pallas kernels for 0%

profile of v4, /device:TPU:0, one launch (start us, length us, event | category | flops | bytes accessed | tf_op | source)
XLA Modules:
  0.0 32.7 jit_solution(818320065501534355)
XLA Ops:
  0.0 0.0 copy-start
  0.0 0.8 %fusion.2 = (f32[3,8,256]{2,1,0:T(8,128)S(1)}, f32[3,8,256]{2,1,0:T(8,128)S(1)}) fusion(f32[8,8,256]{2,1,0:T(8,128)} %f_ref.3), kind=kLoop, calls=%fused_computation.4 | loop fusion | bytes 98304 | tf_op jit(solution)/shard_map/slice | solution.py:543
  0.8 0.0 copy-done
  0.8 0.0 copy-start.1
  0.9 0.5 %collective-permute-start.1 = (f32[7,8,256]{2,1,0:T(8,128)S(1)}, f32[7,8,256]{2,1,0:T(8,128)S(1)}, u32[]{:S(2)}, u32[]{:S(2)}) collective-permute-start(f32[7,8,256]{2,1,0:T(8,128)S(1)} %get-tuple-element.23), channel_id=1, source_target_pairs={{0,1},{1,0},{2,3},{3,2},{4,5},{5,4},{6,7},{7,6},{8,16},{9,17},{10,... | collective-permute-start | bytes 172040 | tf_op jit(solution)/shard_map/ppermute | solution.py:547
  1.4 4.0 %collective-permute-start = (f32[7,8,256]{2,1,0:T(8,128)S(1)}, f32[7,8,256]{2,1,0:T(8,128)S(1)}, u32[]{:S(2)}, u32[]{:S(2)}) collective-permute-start(f32[7,8,256]{2,1,0:T(8,128)S(1)} %get-tuple-element.24), channel_id=1, source_target_pairs={{0,8},{8,0},{16,24},{24,16},{1,9},{9,1},{17,25},{25,17},{2,10},{10... | collective-permute-start | bytes 172040 | tf_op jit(solution)/shard_map/ppermute | solution.py:546
  5.4 0.0 collective-permute-done.1.b_ref
  5.4 2.9 %collective-permute-done.a_ref = f32[7,8,256]{2,1,0:T(8,128)S(1)} collective-permute-done((f32[7,8,256]{2,1,0:T(8,128)S(1)}, f32[7,8,256]{2,1,0:T(8,128)S(1)}, u32[]{:S(2)}, u32[]{:S(2)}) %collective-permute-start) | collective-permute-done | bytes 57376 | tf_op jit(solution)/shard_map/ppermute | solution.py:546
  8.2 0.0 copy-done.1
  8.3 1.4 %collective-permute-start.2 = (f32[11,8,256]{2,1,0:T(8,128)S(1)}, f32[11,8,256]{2,1,0:T(8,128)S(1)}, u32[]{:S(2)}, u32[]{:S(2)}) collective-permute-start(f32[11,8,256]{2,1,0:T(8,128)S(1)} %get-tuple-element.14), channel_id=1, source_target_pairs={{0,8},{1,2},{2,1},{3,4},{4,3},{5,6},{6,5},{7,15},{8,0},{9,10},{10,... | collective-permute-start | bytes 270344 | tf_op jit(solution)/shard_map/ppermute | solution.py:558
  9.6 0.4 %collective-permute-start.3 = (f32[11,8,256]{2,1,0:T(8,128)S(1)}, f32[11,8,256]{2,1,0:T(8,128)S(1)}, u32[]{:S(2)}, u32[]{:S(2)}) collective-permute-start(f32[11,8,256]{2,1,0:T(8,128)S(1)} %get-tuple-element.15), channel_id=1, source_target_pairs={{0,1},{1,0},{2,3},{3,2},{4,5},{5,4},{6,7},{7,6},{8,9},{9,8},{10,11... | collective-permute-start | bytes 270344 | tf_op jit(solution)/shard_map/ppermute | solution.py:557
  10.0 2.8 %collective-permute-done.2.z_ref = f32[11,8,256]{2,1,0:T(8,128)S(1)} collective-permute-done((f32[11,8,256]{2,1,0:T(8,128)S(1)}, f32[11,8,256]{2,1,0:T(8,128)S(1)}, u32[]{:S(2)}, u32[]{:S(2)}) %collective-permute-start.2) | collective-permute-done | bytes 90144 | tf_op jit(solution)/shard_map/ppermute | solution.py:558
  12.9 0.0 collective-permute-done.3.k_ref
  12.9 0.8 %shard_map.29 = (f32[64,8,128]{2,1,0:T(8,128)S(1)}, f32[12,16,256]{2,1,0:T(8,128)S(1)}, f32[14,16,256]{2,1,0:T(8,128)S(1)}, f32[15,16,256]{2,1,0:T(8,128)S(1)}, ...) custom-call(f32[8,8,256]{2,1,0:T(8,128)S(1)} %copy-done.1, ...), custom_call_target="tpu_custom_call" | custom-call | tf_op jit(solution)/shard_map/pallas_call | solution.py:82
  13.7 14.6 %all_to_all.5.own_ref = f32[64,8,128]{2,1,0:T(8,128)S(1)} all-to-all(f32[64,8,128]{2,1,0:T(8,128)S(1)} %get-tuple-element.16), channel_id=1, replica_groups=mesh['gx'=4,'gy'=8] {'gx','gy'}, dimensions={0} | all-to-all | bytes 524288 | tf_op jit(solution)/shard_map/all_to_all | solution.py:571
  28.3 0.4 %collective-permute-start.4 = (f32[64,8,128]{2,1,0:T(8,128)S(1)}, f32[64,8,128]{2,1,0:T(8,128)S(1)}, u32[]{:S(2)}, u32[]{:S(2)}) collective-permute-start(f32[64,8,128]{2,1,0:T(8,128)S(1)} %all_to_all.5.own_ref), channel_id=1, source_target_pairs={{0,1},{1,0},{2,3},{3,2},{4,5},{5,4},{6,7},{7,6},{8,9},{9,8},{10,11... | collective-permute-start | bytes 786440 | tf_op jit(solution)/shard_map/ppermute | solution.py:572
  28.7 1.2 %collective-permute-done.4.other_ref = f32[64,8,128]{2,1,0:T(8,128)S(1)} collective-permute-done((f32[64,8,128]{2,1,0:T(8,128)S(1)}, f32[64,8,128]{2,1,0:T(8,128)S(1)}, u32[]{:S(2)}, u32[]{:S(2)}) %collective-permute-start.4) | collective-permute-done | bytes 262176 | tf_op jit(solution)/shard_map/ppermute | solution.py:572
  29.8 2.9 %shard_map.30 = f32[8,8,256]{2,1,0:T(8,128)} custom-call(f32[64,8,128]{2,1,0:T(8,128)S(1)} %all_to_all.5.own_ref, f32[64,8,128]{2,1,0:T(8,128)S(1)} %collective-permute-done.4.other_ref, f32[12,16,256]{2,1,0:T(8,128)S(1)} %get-tuple-element.17.u0_ref, f32[14,16,256]{2,1,0:T(8,128)S(1)} %get-tuple-element.18.fx_ref, ...), custom_call_target="tpu_custom_call" | custom-call | tf_op jit(solution)/shard_map/pallas_call | solution.py:82
  (3 shorter events, 0.1 us)
Async XLA Ops:
  0.0 0.8 %copy-start = (f32[8,8,256]{2,1,0:T(8,128)S(1)}, f32[8,8,256]{2,1,0:T(8,128)}, u32[]{:S(2)}) copy-start(f32[8,8,256]{2,1,0:T(8,128)} %c_ref.3) | copy-start | bytes 196612
  0.8 7.4 %copy-start.1 = (f32[8,8,256]{2,1,0:T(8,128)S(1)}, f32[8,8,256]{2,1,0:T(8,128)}, u32[]{:S(2)}) copy-start(f32[8,8,256]{2,1,0:T(8,128)} %f_ref.3) | copy-start | bytes 196612
  0.9 4.5 %collective-permute-start.1 = (f32[7,8,256]{2,1,0:T(8,128)S(1)}, f32[7,8,256]{2,1,0:T(8,128)S(1)}, u32[]{:S(2)}, u32[]{:S(2)}) collective-permute-start(f32[7,8,256]{2,1,0:T(8,128)S(1)} %get-tuple-element.23), channel_id=1, source_target_pairs={{0,1},{1,0},{2,3},{3,2},{4,5},{5,4},{6,7},{7,6},{8,16},{9,17},{10,... | collective-permute-start | bytes 172040 | tf_op jit(solution)/shard_map/ppermute | solution.py:547
  1.4 6.8 %collective-permute-start = (f32[7,8,256]{2,1,0:T(8,128)S(1)}, f32[7,8,256]{2,1,0:T(8,128)S(1)}, u32[]{:S(2)}, u32[]{:S(2)}) collective-permute-start(f32[7,8,256]{2,1,0:T(8,128)S(1)} %get-tuple-element.24), channel_id=1, source_target_pairs={{0,8},{8,0},{16,24},{24,16},{1,9},{9,1},{17,25},{25,17},{2,10},{10... | collective-permute-start | bytes 172040 | tf_op jit(solution)/shard_map/ppermute | solution.py:546
  8.3 4.6 %collective-permute-start.2 = (f32[11,8,256]{2,1,0:T(8,128)S(1)}, f32[11,8,256]{2,1,0:T(8,128)S(1)}, u32[]{:S(2)}, u32[]{:S(2)}) collective-permute-start(f32[11,8,256]{2,1,0:T(8,128)S(1)} %get-tuple-element.14), channel_id=1, source_target_pairs={{0,8},{1,2},{2,1},{3,4},{4,3},{5,6},{6,5},{7,15},{8,0},{9,10},{10,... | collective-permute-start | bytes 270344 | tf_op jit(solution)/shard_map/ppermute | solution.py:558
  9.6 3.2 %collective-permute-start.3 = (f32[11,8,256]{2,1,0:T(8,128)S(1)}, f32[11,8,256]{2,1,0:T(8,128)S(1)}, u32[]{:S(2)}, u32[]{:S(2)}) collective-permute-start(f32[11,8,256]{2,1,0:T(8,128)S(1)} %get-tuple-element.15), channel_id=1, source_target_pairs={{0,1},{1,0},{2,3},{3,2},{4,5},{5,4},{6,7},{7,6},{8,9},{9,8},{10,11... | collective-permute-start | bytes 270344 | tf_op jit(solution)/shard_map/ppermute | solution.py:557
  28.3 1.5 %collective-permute-start.4 = (f32[64,8,128]{2,1,0:T(8,128)S(1)}, f32[64,8,128]{2,1,0:T(8,128)S(1)}, u32[]{:S(2)}, u32[]{:S(2)}) collective-permute-start(f32[64,8,128]{2,1,0:T(8,128)S(1)} %all_to_all.5.own_ref), channel_id=1, source_target_pairs={{0,1},{1,0},{2,3},{3,2},{4,5},{5,4},{6,7},{7,6},{8,9},{9,8},{10,11... | collective-permute-start | bytes 786440 | tf_op jit(solution)/shard_map/ppermute | solution.py:572

commit v5 on v4

--- a/solution.py
+++ b/solution.py
@@ -19,6 +19,7 @@
 DEEP_C = 2 * SMOOTH
 SUB = 8
 PAD = 4
+MARGIN = SUB
 WRITTEN_OUT = 512
 
 VMEM = pl.BlockSpec(memory_space=pltpu.VMEM)
@@ -184,11 +185,11 @@
     corner_tiles = sides(rows + 2)
     for t in range(rows + 2 * DEEP_C):
         row = t - DEEP_C
-        cx_ref[t, 0:cols] = c_row(row)
+        cx_ref[t, 0:cols] = 0.5 * c_row(row)
         s = row + DEEP_F
         if -1 <= row <= rows:
             left, right = sides(row + 1)
-            cx_ref[t, cols:] = jnp.where(low_half, right, left)
+            cx_ref[t, cols:] = 0.5 * jnp.where(low_half, right, left)
             f = turn(jnp.where(low_half, left, right), DEEP_C, 0)
         else:
             left, right = corner_tiles
@@ -199,31 +200,29 @@
                 c = jnp.where(low_half, turn(right, -c_turn, 0), turn(left, c_turn, 0))
             if f_turn is not None:
                 f = jnp.where(low_half, turn(right, -f_turn, 0), turn(left, f_turn, 0))
-            cx_ref[t, cols:] = c
+            cx_ref[t, cols:] = 0.5 * c
         if 0 <= s < rows + 2 * DEEP_F:
             fx_ref[s, 0:cols] = f_row(row)
             fx_ref[s, cols:] = f
 
     tall = rows + 2 * DEEP_F
-    wx_ref[0] = 0.5 * (cx_ref[0] + cx_ref[1])
+    wx_ref[0] = cx_ref[0] + cx_ref[1]
     for s in range(tall):
-        c = cx_ref[s + 1]
-        half = 0.5 * c
-        above = half + 0.5 * cx_ref[s + 2]
+        half = cx_ref[s + 1]
+        above = half + cx_ref[s + 2]
+        after = half + turn(half, -1, 0)
+        deeper = jnp.where(lane == depth - 1, 0.0, half + turn(half, -1, 1))
         wx_ref[s + 1] = above
-        w_cols = half + turn(half, -1, 0)
-        w_depth = jnp.where(lane == depth - 1, 0.0, half + turn(half, -1, 1))
-        edge = jnp.where((lane == 0) | (lane == depth - 1), half, 0.0)
-        diag = wx_ref[s] + above + w_cols + turn(w_cols, 1, 0)
-        diag = diag + w_depth + turn(w_depth, 1, 1) + edge
+        wy_ref[s] = after
+        wz_ref[s] = deeper
+        diag = wx_ref[s] + above + after + turn(after, 1, 0) + deeper + turn(deeper, 1, 1)
+        diag = diag + jnp.where((lane == 0) | (lane == depth - 1), half, 0.0)
         inside = col_inside
         if s < DEEP_F:
             inside = inside & (gx > 0)
         if s >= rows + DEEP_F:
             inside = inside & (gx < along_x - 1)
         inv = jnp.where(inside, 1.0 / diag, 0.0)
-        wy_ref[s] = w_cols
-        wz_ref[s] = w_depth
         if DEEP_F <= s < DEEP_F + rows:
             diag_ref[s - DEEP_F] = diag[:cols]
         inv_ref[s] = inv
@@ -260,7 +259,7 @@
     c_from = f_from + cols * half_rows
     from_f = (source == f_from) | (source == f_from + 1)
     from_c = (source == c_from) | (source == c_from + 1)
-    picker = jnp.where(f_half, jnp.where(from_f, 0.5, 0.0), jnp.where(from_c, 0.125, 0.0))
+    picker = jnp.where(f_half, jnp.where(from_f, 0.5, 0.0), jnp.where(from_c, 0.0625, 0.0))
     tile = exact_dot(picker, thin).reshape(half_rows, SUB, depth // 2)
 
     def put(i):
@@ -273,27 +272,25 @@
     along_x, along_y,
     own_ref, other_ref, u0_ref, fx_ref, wx0_ref, wy0_ref, wz0_ref, inv0_ref,
     out_ref,
-    f_ref, c_ref, wx_ref, wy_ref, wz_ref, diag_ref, inv_ref, v_ref,
-    f2_ref, c2_ref, diag2_ref, d2_ref, e2_ref, e3_ref, a2_ref,
-    py_ref, vw_ref, dw_ref, vx_ref, e1_ref, yy_ref, v0_ref, d0_ref, x0_ref,
+    f_ref, h_ref, wx_ref, wy_ref, wz_ref, inv_ref, v_ref, diag_ref,
+    f2_ref, h2_ref, e2_ref, e3_ref, py_ref, vw_ref, dw_ref, vx_ref, e1_ref, yy_ref, v0_ref, d0_ref, x0_ref,
 ):
     gx, gy = lax.axis_index("gx"), lax.axis_index("gy")
     odd = lax.rem(gy, 2) == 1
     brick1 = own_ref.shape[0] // (along_x * (along_y // 2))
-    rows1, cols1, depth1 = f_ref.shape[0] - 2 * PAD, f_ref.shape[1], f_ref.shape[2]
+    rows1, cols1, depth1 = diag_ref.shape
     across = cols1 // SUB
     registers1 = across * (depth1 // 128)
-    shape1 = (cols1, depth1)
-    zero1 = jnp.zeros(shape1, F32)
     inv_mid, ((keep, push),) = chebyshev(SMOOTH_LOW, SMOOTH_HIGH, SMOOTH)
+    inner = pl.ds(MARGIN, cols1)
 
     low_half = iota((SUB, depth1), 0) < SUB // 2
-    c_ref[PAD - 1] = zero1
-    c_ref[PAD + rows1] = zero1
 
     def place(k):
         x, z = k // across, k % across
-        at = z * SUB if isinstance(z, int) else pl.multiple_of(z * SUB, SUB)
+        at = z * SUB + MARGIN
+        if not isinstance(z, int):
+            at = pl.multiple_of(at, SUB)
         half = brick1 // 2
         for i in range(brick1):
             swapped = odd if i < half else jnp.logical_not(odd)
@@ -302,39 +299,51 @@
             high = jnp.where(swapped, other_ref[high], own_ref[high])
             row = PAD + x * brick1 + i
             f_ref[row, pl.ds(at, SUB)] = jnp.where(low_half, low, high)
-            c_ref[row, pl.ds(at, SUB)] = turn(jnp.where(low_half, high, low), SUB // 2, 0)
+            h_ref[row, pl.ds(at, SUB)] = turn(jnp.where(low_half, high, low), SUB // 2, 0)
 
     each(along_x * across, brick1, place)
 
-    wx_ref[PAD] = 0.5 * c_ref[PAD]
-
-    def weigh(c, below, above, shape, stride):
-        col, lane = iota(shape, 0), iota(shape, 1)
-        half = 0.5 * c
-        w_above = half + 0.5 * above
-        w_cols = jnp.where(col == shape[0] - 1, 0.0, half + turn(half, -1, 0))
-        w_depth = jnp.where(lane >= shape[1] - stride, 0.0, half + turn(half, -stride, 1))
-        edge = jnp.where((col == 0) | (col == shape[0] - 1), half, 0.0)
-        edge = edge + jnp.where((lane < stride) | (lane >= shape[1] - stride), half, 0.0)
-        w_below, w_before, w_back = half + 0.5 * below, turn(w_cols, 1, 0), turn(w_depth, stride, 1)
-        diag = w_below + w_above + w_cols + w_before + w_depth + w_back + edge
-        return (w_below, w_above, w_cols, w_before, w_depth, w_back), diag, edge
+    def clear_beside(ref, row):
+        zero = jnp.zeros((MARGIN, depth1), F32)
+        ref[row, 0:MARGIN] = zero
+        ref[row, pl.ds(ref.shape[1] - MARGIN, MARGIN)] = zero
+
+    def clear(i):
+        for ref in (h_ref, v_ref):
+            clear_beside(ref, PAD + i)
+        wy_ref[PAD + i, 0:MARGIN] = jnp.zeros((MARGIN, depth1), F32)
+
+    each(rows1, 1, clear)
+    for ref in (h_ref, v_ref):
+        for row in (PAD - 1, PAD + rows1):
+            ref[row] = jnp.zeros(ref.shape[1:], F32)
+
+    def weigh(ref, row, cols, stride):
+        half = ref[row, pl.ds(MARGIN, cols)]
+        lane = iota(half.shape, 1)
+        first, last = lane < stride, lane >= half.shape[1] - stride
+        around = [ref[row - 1, pl.ds(MARGIN, cols)], ref[row + 1, pl.ds(MARGIN, cols)]]
+        around += [ref[row, pl.ds(MARGIN - 1, cols)], ref[row, pl.ds(MARGIN + 1, cols)]]
+        around += [
+            jnp.where(first, 0.0, turn(half, stride, 1)),
+            jnp.where(last, 0.0, turn(half, -stride, 1)),
+        ]
+        total = (around[0] + around[1]) + (around[2] + around[3]) + (around[4] + around[5])
+        return half, around, 6.0 * half + total, first, last
+
+    wx_ref[PAD, inner] = h_ref[PAD, inner]
 
     def weigh1(i):
         row = PAD + i
-        (_, w_above, w_cols, _, w_depth, _), diag, _ = weigh(
-            c_ref[row], c_ref[row - 1], c_ref[row + 1], shape1, 1
-        )
+        half, around, diag, _, last = weigh(h_ref, row, cols1, 1)
         inv = 1.0 / diag
-        wx_ref[row + 1] = w_above
-        wy_ref[row] = w_cols
-        wz_ref[row] = w_depth
-        diag_ref[row] = diag
-        inv_ref[row] = inv
-        v_ref[row] = f_ref[row] * inv * inv_mid
-
-    v_ref[PAD - 1] = zero1
-    v_ref[PAD + rows1] = zero1
+        wx_ref[row + 1, inner] = half + around[1]
+        wy_ref[row, inner] = half + around[3]
+        wz_ref[row, inner] = jnp.where(last, 0.0, half + around[5])
+        diag_ref[i] = diag
+        inv_ref[row, inner] = inv
+        v_ref[row, inner] = f_ref[row, inner] * inv * inv_mid
+
     each(rows1, registers1, weigh1)
 
     rows2, cols2 = rows1 // 2, cols1 // 2
@@ -343,134 +352,166 @@
     zero2 = jnp.zeros(shape2, F32)
     lane2, col2 = iota(shape2, 1), iota(shape2, 0)
     even2 = lane2 % 2 == 0
+    inner2 = pl.ds(MARGIN, cols2)
 
     def fold(ref, row):
-        half = ref[row, pl.ds(0, cols2, stride=2), :] + ref[row, pl.ds(1, cols2, stride=2), :]
-        return half + jnp.where(even2, turn(half, -1, 1), turn(half, 1, 1))
-
-    def restrict_c(k):
+        half = ref[row, pl.ds(MARGIN, cols2, stride=2), :] + ref[row, pl.ds(MARGIN + 1, cols2, stride=2), :]
+        return half + turn(half, -1, 1)
+
+    def restrict_h(k):
         row = PAD + 2 * k
-        c2_ref[k + 1] = 0.125 * (fold(c_ref, row) + fold(c_ref, row + 1))
-
-    each(rows2, 2 * registers1, restrict_c)
-    u_ref = c_ref
-
-    def pulled1(x_ref, at, row):
-        return f_ref[row] + beside(
-            x_ref[at], x_ref[at - 1], x_ref[at + 1],
-            wx_ref[row], wx_ref[row + 1], wy_ref[row], wz_ref[row],
-        )
+        h2_ref[k + 1, inner2] = 0.125 * (fold(h_ref, row) + fold(h_ref, row + 1))
+
+    each(rows2, 2 * registers1, restrict_h)
+    u_ref = h_ref
+
+    def pulled1(x_ref, at, x_first, row, first, count):
+        def part(ref, i, begin, shift=0):
+            return ref[i, pl.ds(begin + shift, count), :]
+
+        x, depths = part(x_ref, at, x_first), part(wz_ref, row, first)
+        total = part(wx_ref, row + 1, first) * part(x_ref, at + 1, x_first)
+        total = total + part(wx_ref, row, first) * part(x_ref, at - 1, x_first)
+        total = total + part(wy_ref, row, first) * part(x_ref, at, x_first, 1)
+        total = total + part(wy_ref, row, first, -1) * part(x_ref, at, x_first, -1)
+        total = total + depths * turn(x, -1, 1) + turn(depths * x, 1, 1)
+        return x, part(f_ref, row, first) + total
 
     def second1(i):
         row = PAD + i
-        total = pulled1(v_ref, row, row)
-        u_ref[row] = (1.0 + keep - push) * v_ref[row] + push * (inv_ref[row] * total)
+        v, total = pulled1(v_ref, row, MARGIN, row, MARGIN, cols1)
+        u_ref[row, inner] = (1.0 + keep - push) * v + push * (inv_ref[row, inner] * total)
 
     each(rows1, registers1, second1)
 
-    def residual1(row):
-        return pulled1(u_ref, row, row) - diag_ref[row] * u_ref[row]
+    def residual1(i):
+        u, total = pulled1(u_ref, PAD + i, MARGIN, PAD + i, MARGIN, cols1)
+        return total - diag_ref[i] * u
 
     def restrict(k):
-        row = PAD + 2 * k
-        v_ref[k] = residual1(row) + residual1(row + 1)
+        v_ref[k, inner] = residual1(2 * k) + residual1(2 * k + 1)
         f2_ref[k] = 0.5 * fold(v_ref, k)
 
     each(rows2, 2 * registers1, restrict)
-    c2_ref[0] = zero2
-    c2_ref[rows2 + 1] = zero2
-    for ref in (e2_ref, e3_ref):
-        ref[0] = zero2
-        ref[rows2 + 1] = zero2
+    for ref in (h2_ref, e2_ref, e3_ref):
+        for row in (0, rows2 + 1):
+            ref[row] = jnp.zeros(ref.shape[1:], F32)
+
+    def clear2(k):
+        for ref in (h2_ref, e2_ref, e3_ref):
+            clear_beside(ref, k + 1)
+
+    each(rows2, 1, clear2)
     inv_mid2, pairs2 = chebyshev(COARSE_LOW, COARSE_HIGH, COARSE_STEPS)
 
+    def kept(at, k):
+        ref, at, begin = (diag_ref, at, 0) if at < 4 else (v_ref, at - 4, MARGIN)
+        return ref, 2 * k + at // 2, pl.ds(begin + at % 2 * cols2, cols2)
+
+    def keep_value(at, k, value):
+        ref, row, columns = kept(at, k)
+        ref[row, columns] = value
+
+    def kept_value(at, k):
+        ref, row, columns = kept(at, k)
+        return ref[row, columns]
+
+    diagonal, direction = 6, 7
+
     def weigh2(k, edges):
-        shares, diag, edge = weigh(c2_ref[k + 1], c2_ref[k], c2_ref[k + 2], shape2, 2)
+        half, around, diag, first, last = weigh(h2_ref, k + 1, cols2, 2)
         inv = 1.0 / diag
-        for at, share in enumerate(shares):
-            a2_ref[at, k] = share * inv
-        diag2_ref[k] = diag
-        scaled = f2_ref[k] * inv
-        f2_ref[k] = scaled
-        d = scaled * inv_mid2
-        d2_ref[k] = d
-        e2_ref[k + 1] = d
-        half = 0.5 * c2_ref[k + 1]
-        edge = edge + jnp.where(k == 0, half, 0.0) + jnp.where(k == rows2 - 1, half, 0.0)
-        return edges + edge
+        scaled = half * inv
+        for at in range(4):
+            keep_value(at, k, scaled + around[at] * inv)
+        keep_value(4, k, jnp.where(first, 0.0, scaled + around[4] * inv))
+        keep_value(5, k, jnp.where(last, 0.0, scaled + around[5] * inv))
+        keep_value(diagonal, k, diag)
+        f = f2_ref[k] * inv
+        f2_ref[k] = f
+        d = f * inv_mid2
+        keep_value(direction, k, d)
+        e2_ref[k + 1, inner2] = d
+        edges = edges + jnp.where((col2 == 0) | (col2 == cols2 - 1), half, 0.0)
+        edges = edges + jnp.where(first | last, half, 0.0)
+        return edges + jnp.where(k == 0, half, 0.0) + jnp.where(k == rows2 - 1, half, 0.0)
 
     edges = each_sum(rows2, registers2, weigh2, zero2)
 
     def residual2(e_ref, k):
-        e = e_ref[k + 1]
-        r = f2_ref[k] - e + a2_ref[0, k] * e_ref[k] + a2_ref[1, k] * e_ref[k + 2]
-        r = r + (a2_ref[2, k] * turn(e, -1, 0) + a2_ref[3, k] * turn(e, 1, 0))
-        return r + (a2_ref[4, k] * turn(e, -2, 1) + a2_ref[5, k] * turn(e, 2, 1))
+        e = e_ref[k + 1, inner2]
+        r = f2_ref[k] - e + kept_value(0, k) * e_ref[k, inner2] + kept_value(1, k) * e_ref[k + 2, inner2]
+        r = r + kept_value(2, k) * e_ref[k + 1, pl.ds(MARGIN - 1, cols2)]
+        r = r + kept_value(3, k) * e_ref[k + 1, pl.ds(MARGIN + 1, cols2)]
+        return e, r + (kept_value(4, k) * turn(e, 2, 1) + kept_value(5, k) * turn(e, -2, 1))
 
     now_ref, next_ref = e2_ref, e3_ref
     for keep2, push2 in pairs2:
 
         def step2(k):
-            d = keep2 * d2_ref[k] + push2 * residual2(now_ref, k)
-            d2_ref[k] = d
-            next_ref[k + 1] = now_ref[k + 1] + d
+            e, r = residual2(now_ref, k)
+            d = keep2 * kept_value(direction, k) + push2 * r
+            keep_value(direction, k, d)
+            next_ref[k + 1, inner2] = e + d
 
         each(rows2, registers2, step2)
         now_ref, next_ref = next_ref, now_ref
 
     def add_residual(k, total):
-        return total + diag2_ref[k] * residual2(now_ref, k)
+        return total + kept_value(diagonal, k) * residual2(now_ref, k)[1]
 
     total = each_sum(rows2, registers2, add_residual, zero2)
-    top = jnp.sum(total, axis=(0, 1), keepdims=True)
-    bottom = jnp.sum(edges, axis=(0, 1), keepdims=True)
+    top = jnp.sum(jnp.where(even2, total, 0.0), axis=(0, 1), keepdims=True)
+    bottom = jnp.sum(jnp.where(even2, edges, 0.0), axis=(0, 1), keepdims=True)
     mean = top / bottom
 
-    span = brick1 + 2 * PAD
-    start = gx * brick1 - PAD
+    span, broad = brick1 + 2 * PAD, 2 * SUB
+    start, first_col = gx * brick1 - PAD, gy * (cols1 // along_y) - PAD
     coarse_span = span // 2 + 2
     for k in range(coarse_span):
         row = lax.div(gx * brick1, 2) - PAD // 2 - 1 + k
         good = (row >= 0) & (row < rows2)
-        e = now_ref[jnp.clip(row, 0, rows2 - 1) + 1] + mean
+        e = now_ref[jnp.clip(row, 0, rows2 - 1) + 1, inner2] + mean
         e = jnp.where(good, e, 0.0)
         back = jnp.where(lane2 < 2, 0.0, turn(e, 2, 1))
-        ahead = jnp.where(lane2 >= depth1 - 2, 0.0, turn(e, -2, 1))
-        e = 0.75 * e + 0.25 * jnp.where(even2, back, ahead)
+        ahead = jnp.where(lane2 >= depth1 - 2, 0.0, turn(e, -1, 1))
+        home = jnp.where(even2, e, turn(e, 1, 1))
+        e = 0.75 * home + 0.25 * jnp.where(even2, back, ahead)
         back = jnp.where(col2 == 0, 0.0, turn(e, 1, 0))
         ahead = jnp.where(col2 == cols2 - 1, 0.0, turn(e, -1, 0))
-        py_ref[k, pl.ds(0, cols2, stride=2), :] = 0.75 * e + 0.25 * back
-        py_ref[k, pl.ds(1, cols2, stride=2), :] = 0.75 * e + 0.25 * ahead
+        py_ref[k, pl.ds(MARGIN, cols2, stride=2), :] = 0.75 * e + 0.25 * back
+        py_ref[k, pl.ds(MARGIN + 1, cols2, stride=2), :] = 0.75 * e + 0.25 * ahead
+
+    window, held = pl.ds(MARGIN + first_col, broad), pl.ds(MARGIN, broad)
+    col1 = first_col + iota((broad, depth1), 0)
+    col_good = (col1 >= 0) & (col1 < cols1)
 
     def inside1(m):
-        return (start + m >= 0) & (start + m < rows1)
+        return col_good & ((start + m >= 0) & (start + m < rows1))
 
     for m in range(span):
         near = m // 2 + 1
         far = near - 1 if m % 2 == 0 else near + 1
-        total = u_ref[PAD + start + m] + (0.75 * py_ref[near] + 0.25 * py_ref[far])
-        vw_ref[m] = jnp.where(inside1(m), total, 0.0)
+        total = u_ref[PAD + start + m, window, :]
+        total = total + (0.75 * py_ref[near, window, :] + 0.25 * py_ref[far, window, :])
+        vw_ref[m, held] = jnp.where(inside1(m), total, 0.0)
     for m in range(1, span - 1):
         row = PAD + start + m
-        v = vw_ref[m]
-        d = (inv_ref[row] * pulled1(vw_ref, m, row) - v) * inv_mid
+        v, total = pulled1(vw_ref, m, MARGIN, row, MARGIN + first_col, broad)
+        d = (inv_ref[row, window, :] * total - v) * inv_mid
         dw_ref[m] = d
-        vx_ref[m] = jnp.where(inside1(m), v + d, 0.0)
-    margin = SUB
-    e1_ref[:, 0:margin, :] = jnp.zeros((span - 4, margin, depth1), F32)
-    e1_ref[:, margin + cols1 :, :] = jnp.zeros((span - 4, margin, depth1), F32)
+        vx_ref[m, held] = jnp.where(inside1(m), v + d, 0.0)
     for m in range(2, span - 2):
         row = PAD + start + m
-        total = inv_ref[row] * pulled1(vx_ref, m, row)
-        e = (1.0 - push) * vx_ref[m] + (keep * dw_ref[m] + push * total)
-        e1_ref[m - 2, margin : margin + cols1, :] = jnp.where(inside1(m), e, 0.0)
+        v, total = pulled1(vx_ref, m, MARGIN, row, MARGIN + first_col, broad)
+        e = (1.0 - push) * v + (keep * dw_ref[m] + push * (inv_ref[row, window, :] * total))
+        e1_ref[m - 2] = jnp.where(inside1(m), e, 0.0)
 
     rows, cols, depth = out_ref.shape
     wide = (cols + 2 * DEEP_C, depth)
     half_wide = wide[0] // 2
-    first_col = margin + gy * (cols // 2) - DEEP_C // 2
     for k in range(span - 4):
-        e = turn(e1_ref[k, pl.ds(first_col, half_wide), :], -(DEEP_C // 2), 0)
+        e = turn(e1_ref[k, pl.ds(PAD - DEEP_C // 2, half_wide), :], -(DEEP_C // 2), 0)
         at = k * wide[0]
         yy_ref[pl.ds(at, half_wide, stride=2), :] = 0.75 * e + 0.25 * turn(e, 1, 0)
         yy_ref[pl.ds(at + 1, half_wide, stride=2), :] = 0.75 * e + 0.25 * turn(e, -1, 0)
@@ -572,14 +613,15 @@
     other = lax.ppermute(own, "gy", pairs_from(0, along_y))
 
     rows1, cols1, depth1 = along_x * half[0], along_y * (cols // 2), half[2]
-    whole1 = (rows1 + 2 * PAD + 1, cols1, depth1)
+    whole1 = (rows1 + 2 * PAD + 1, cols1 + 2 * MARGIN, depth1)
     rows2, cols2 = rows1 // 2, cols1 // 2
-    whole2 = (rows2 + 2, cols2, depth1)
-    span = half[0] + 2 * PAD
-    line = (cols1, depth1)
-    scratch = [(rows1 + 2 * PAD,) + line] + [whole1] * 7 + [whole2] * 6 + [(6, rows2) + whole2[1:]]
-    scratch += [(span // 2 + 2,) + line] + [(span,) + line] * 3
-    scratch += [(span - 4, cols1 + 2 * SUB, depth1), ((span - 4) * wide[0], depth1)]
+    whole2 = (rows2 + 2, cols2 + 2 * MARGIN, depth1)
+    span, broad = half[0] + 2 * PAD, 2 * SUB
+    window = (span, broad + 2 * MARGIN, depth1)
+    scratch = [whole1] * 7 + [(rows1, cols1, depth1)]
+    scratch += [(rows2, cols2, depth1)] + [whole2] * 3
+    scratch += [(span // 2 + 2,) + whole1[1:], window, (span, broad, depth1), window]
+    scratch += [(span - 4, broad, depth1), ((span - 4) * wide[0], depth1)]
     scratch += [(tall,) + wide, (tall, cols, depth), (tall,) + wide]
     size = sum(4 * math.prod(s) for s in scratch)
     size += 2 * 4 * own.size + 4 * 8 * tall * wide[0] * wide[1]

time: 32.9 us -> 32.8 us (level)
  no operation moved by 1% of the time
where the time goes in v5:
time: 32.8 us; the launch traced here: 32.6 us
  blocking collectives  14.6 us (45%)
  waiting for transfers between devices  6.86 us (21%)
  starting transfers between devices  6.64 us (20%)
  Pallas kernels  3.64 us (11%)
  local copies, waits for them, and re-layouts  0.85 us (3%)
    all_to_all x1, blocking collectives, body(): own = lax.all_to_all(send, ('gx', 'gy'), 0, 0, tiled=True)  14.6 us
    ppermute x1, starting transfers between devices, body(): a = lax.ppermute(a, 'gx', pairs_from(0, along_x))  3.98 us
    pallas_call x3, Pallas kernels, call(): pl.pallas_call(kernel, out_shape=[jax.ShapeDtypeStruct(s, F32) for s in o...  3.64 us
    ppermute x1, waiting for transfers between devices, body(): a = lax.ppermute(a, 'gx', pairs_from(0, along_x))  2.86 us
    ppermute x1, waiting for transfers between devices, body(): z = lax.ppermute(z, ('gx', 'gy'), swaps(along_x, along_y, 'gy', 1))  2.84 us
    ppermute x1, starting transfers between devices, body(): z = lax.ppermute(z, ('gx', 'gy'), swaps(along_x, along_y, 'gy', 1))  1.38 us
    ppermute x1, waiting for transfers between devices, body(): other = lax.ppermute(own, 'gy', pairs_from(0, along_y))  1.16 us
    slice x2, local copies, waits for them, and re-layouts, body(): first = jnp.concatenate([right_side[:DEEP_F], coefficient[:DEEP_C]])  0.79 us
  transfers between devices with their start and end apart: 5, of which 3 were waited for; matrix products, arithmetic and copies ran while one was open for 0% of the time, Pallas kernels for 0%

profile of v5, /device:TPU:0, one launch (start us, length us, event | category | flops | bytes accessed | tf_op | source)
XLA Modules:
  0.0 32.6 jit_solution(7045571810591733858)
XLA Ops:
  0.0 0.0 copy-start
  0.0 0.8 %fusion.2 = (f32[3,8,256]{2,1,0:T(8,128)S(1)}, f32[3,8,256]{2,1,0:T(8,128)S(1)}) fusion(f32[8,8,256]{2,1,0:T(8,128)} %f_ref.3), kind=kLoop, calls=%fused_computation.4 | loop fusion | bytes 98304 | tf_op jit(solution)/shard_map/slice | solution.py:584
  0.8 0.0 copy-done
  0.8 0.0 copy-start.1
  0.9 0.5 %collective-permute-start.1 = (f32[7,8,256]{2,1,0:T(8,128)S(1)}, f32[7,8,256]{2,1,0:T(8,128)S(1)}, u32[]{:S(2)}, u32[]{:S(2)}) collective-permute-start(f32[7,8,256]{2,1,0:T(8,128)S(1)} %get-tuple-element.23), channel_id=1, source_target_pairs={{0,1},{1,0},{2,3},{3,2},{4,5},{5,4},{6,7},{7,6},{8,16},{9,17},{10,... | collective-permute-start | bytes 172040 | tf_op jit(solution)/shard_map/ppermute | solution.py:588
  1.4 4.0 %collective-permute-start = (f32[7,8,256]{2,1,0:T(8,128)S(1)}, f32[7,8,256]{2,1,0:T(8,128)S(1)}, u32[]{:S(2)}, u32[]{:S(2)}) collective-permute-start(f32[7,8,256]{2,1,0:T(8,128)S(1)} %get-tuple-element.24), channel_id=1, source_target_pairs={{0,8},{8,0},{16,24},{24,16},{1,9},{9,1},{17,25},{25,17},{2,10},{10... | collective-permute-start | bytes 172040 | tf_op jit(solution)/shard_map/ppermute | solution.py:587
  5.4 0.0 collective-permute-done.1.b_ref
  5.4 2.9 %collective-permute-done.a_ref = f32[7,8,256]{2,1,0:T(8,128)S(1)} collective-permute-done((f32[7,8,256]{2,1,0:T(8,128)S(1)}, f32[7,8,256]{2,1,0:T(8,128)S(1)}, u32[]{:S(2)}, u32[]{:S(2)}) %collective-permute-start) | collective-permute-done | bytes 57376 | tf_op jit(solution)/shard_map/ppermute | solution.py:587
  8.2 0.0 copy-done.1
  8.3 1.4 %collective-permute-start.2 = (f32[11,8,256]{2,1,0:T(8,128)S(1)}, f32[11,8,256]{2,1,0:T(8,128)S(1)}, u32[]{:S(2)}, u32[]{:S(2)}) collective-permute-start(f32[11,8,256]{2,1,0:T(8,128)S(1)} %get-tuple-element.14), channel_id=1, source_target_pairs={{0,8},{1,2},{2,1},{3,4},{4,3},{5,6},{6,5},{7,15},{8,0},{9,10},{10,... | collective-permute-start | bytes 270344 | tf_op jit(solution)/shard_map/ppermute | solution.py:599
  9.6 0.4 %collective-permute-start.3 = (f32[11,8,256]{2,1,0:T(8,128)S(1)}, f32[11,8,256]{2,1,0:T(8,128)S(1)}, u32[]{:S(2)}, u32[]{:S(2)}) collective-permute-start(f32[11,8,256]{2,1,0:T(8,128)S(1)} %get-tuple-element.15), channel_id=1, source_target_pairs={{0,1},{1,0},{2,3},{3,2},{4,5},{5,4},{6,7},{7,6},{8,9},{9,8},{10,11... | collective-permute-start | bytes 270344 | tf_op jit(solution)/shard_map/ppermute | solution.py:598
  10.0 2.8 %collective-permute-done.2.z_ref = f32[11,8,256]{2,1,0:T(8,128)S(1)} collective-permute-done((f32[11,8,256]{2,1,0:T(8,128)S(1)}, f32[11,8,256]{2,1,0:T(8,128)S(1)}, u32[]{:S(2)}, u32[]{:S(2)}) %collective-permute-start.2) | collective-permute-done | bytes 90144 | tf_op jit(solution)/shard_map/ppermute | solution.py:599
  12.9 0.0 collective-permute-done.3.k_ref
  12.9 0.8 %shard_map.29 = (f32[64,8,128]{2,1,0:T(8,128)S(1)}, f32[12,16,256]{2,1,0:T(8,128)S(1)}, f32[14,16,256]{2,1,0:T(8,128)S(1)}, f32[15,16,256]{2,1,0:T(8,128)S(1)}, ...) custom-call(f32[8,8,256]{2,1,0:T(8,128)S(1)} %copy-done.1, ...), custom_call_target="tpu_custom_call" | custom-call | tf_op jit(solution)/shard_map/pallas_call | solution.py:83
  13.7 14.6 %all_to_all.5.own_ref = f32[64,8,128]{2,1,0:T(8,128)S(1)} all-to-all(f32[64,8,128]{2,1,0:T(8,128)S(1)} %get-tuple-element.16), channel_id=1, replica_groups=mesh['gx'=4,'gy'=8] {'gx','gy'}, dimensions={0} | all-to-all | bytes 524288 | tf_op jit(solution)/shard_map/all_to_all | solution.py:612
  28.3 0.4 %collective-permute-start.4 = (f32[64,8,128]{2,1,0:T(8,128)S(1)}, f32[64,8,128]{2,1,0:T(8,128)S(1)}, u32[]{:S(2)}, u32[]{:S(2)}) collective-permute-start(f32[64,8,128]{2,1,0:T(8,128)S(1)} %all_to_all.5.own_ref), channel_id=1, source_target_pairs={{0,1},{1,0},{2,3},{3,2},{4,5},{5,4},{6,7},{7,6},{8,9},{9,8},{10,11... | collective-permute-start | bytes 786440 | tf_op jit(solution)/shard_map/ppermute | solution.py:613
  28.7 1.2 %collective-permute-done.4.other_ref = f32[64,8,128]{2,1,0:T(8,128)S(1)} collective-permute-done((f32[64,8,128]{2,1,0:T(8,128)S(1)}, f32[64,8,128]{2,1,0:T(8,128)S(1)}, u32[]{:S(2)}, u32[]{:S(2)}) %collective-permute-start.4) | collective-permute-done | bytes 262176 | tf_op jit(solution)/shard_map/ppermute | solution.py:613
  29.9 2.8 %shard_map.30 = f32[8,8,256]{2,1,0:T(8,128)} custom-call(f32[64,8,128]{2,1,0:T(8,128)S(1)} %all_to_all.5.own_ref, f32[64,8,128]{2,1,0:T(8,128)S(1)} %collective-permute-done.4.other_ref, f32[12,16,256]{2,1,0:T(8,128)S(1)} %get-tuple-element.17.u0_ref, f32[14,16,256]{2,1,0:T(8,128)S(1)} %get-tuple-element.18.fx_ref, ...), custom_call_target="tpu_custom_call" | custom-call | tf_op jit(solution)/shard_map/pallas_call | solution.py:83
  (3 shorter events, 0.1 us)
Async XLA Ops:
  0.0 0.8 %copy-start = (f32[8,8,256]{2,1,0:T(8,128)S(1)}, f32[8,8,256]{2,1,0:T(8,128)}, u32[]{:S(2)}) copy-start(f32[8,8,256]{2,1,0:T(8,128)} %c_ref.3) | copy-start | bytes 196612
  0.8 7.4 %copy-start.1 = (f32[8,8,256]{2,1,0:T(8,128)S(1)}, f32[8,8,256]{2,1,0:T(8,128)}, u32[]{:S(2)}) copy-start(f32[8,8,256]{2,1,0:T(8,128)} %f_ref.3) | copy-start | bytes 196612
  0.9 4.5 %collective-permute-start.1 = (f32[7,8,256]{2,1,0:T(8,128)S(1)}, f32[7,8,256]{2,1,0:T(8,128)S(1)}, u32[]{:S(2)}, u32[]{:S(2)}) collective-permute-start(f32[7,8,256]{2,1,0:T(8,128)S(1)} %get-tuple-element.23), channel_id=1, source_target_pairs={{0,1},{1,0},{2,3},{3,2},{4,5},{5,4},{6,7},{7,6},{8,16},{9,17},{10,... | collective-permute-start | bytes 172040 | tf_op jit(solution)/shard_map/ppermute | solution.py:588
  1.4 6.8 %collective-permute-start = (f32[7,8,256]{2,1,0:T(8,128)S(1)}, f32[7,8,256]{2,1,0:T(8,128)S(1)}, u32[]{:S(2)}, u32[]{:S(2)}) collective-permute-start(f32[7,8,256]{2,1,0:T(8,128)S(1)} %get-tuple-element.24), channel_id=1, source_target_pairs={{0,8},{8,0},{16,24},{24,16},{1,9},{9,1},{17,25},{25,17},{2,10},{10... | collective-permute-start | bytes 172040 | tf_op jit(solution)/shard_map/ppermute | solution.py:587
  8.3 4.6 %collective-permute-start.2 = (f32[11,8,256]{2,1,0:T(8,128)S(1)}, f32[11,8,256]{2,1,0:T(8,128)S(1)}, u32[]{:S(2)}, u32[]{:S(2)}) collective-permute-start(f32[11,8,256]{2,1,0:T(8,128)S(1)} %get-tuple-element.14), channel_id=1, source_target_pairs={{0,8},{1,2},{2,1},{3,4},{4,3},{5,6},{6,5},{7,15},{8,0},{9,10},{10,... | collective-permute-start | bytes 270344 | tf_op jit(solution)/shard_map/ppermute | solution.py:599
  9.6 3.2 %collective-permute-start.3 = (f32[11,8,256]{2,1,0:T(8,128)S(1)}, f32[11,8,256]{2,1,0:T(8,128)S(1)}, u32[]{:S(2)}, u32[]{:S(2)}) collective-permute-start(f32[11,8,256]{2,1,0:T(8,128)S(1)} %get-tuple-element.15), channel_id=1, source_target_pairs={{0,1},{1,0},{2,3},{3,2},{4,5},{5,4},{6,7},{7,6},{8,9},{9,8},{10,11... | collective-permute-start | bytes 270344 | tf_op jit(solution)/shard_map/ppermute | solution.py:598
  28.3 1.5 %collective-permute-start.4 = (f32[64,8,128]{2,1,0:T(8,128)S(1)}, f32[64,8,128]{2,1,0:T(8,128)S(1)}, u32[]{:S(2)}, u32[]{:S(2)}) collective-permute-start(f32[64,8,128]{2,1,0:T(8,128)S(1)} %all_to_all.5.own_ref), channel_id=1, source_target_pairs={{0,1},{1,0},{2,3},{3,2},{4,5},{5,4},{6,7},{7,6},{8,9},{9,8},{10,11... | collective-permute-start | bytes 786440 | tf_op jit(solution)/shard_map/ppermute | solution.py:613

commit v6 on v5

--- a/solution.py
+++ b/solution.py
@@ -159,8 +159,16 @@
     put(rows + 2, corners(sub, 1), corners(SUB - 1 - sub, -1))
 
 
+def line_up(axis, *refs):
+    *block_refs, out_ref = refs
+    here = lax.axis_index("gx") if axis == "gx" else lax.div(lax.axis_index("gy"), 2)
+    size = block_refs[0].shape[0]
+    for distance, ref in enumerate(block_refs):
+        out_ref[pl.ds((here ^ distance) * size, size)] = ref[...]
+
+
 def fine_down(
-    along_x, along_y, copies,
+    along_x, along_y,
     f_ref, c_ref, a_ref, b_ref, z_ref, k_ref,
     send_ref, u_ref, fx_ref, wx_ref, wy_ref, wz_ref, inv_ref,
     cx_ref, v_ref, diag_ref,
@@ -262,10 +270,7 @@
     picker = jnp.where(f_half, jnp.where(from_f, 0.5, 0.0), jnp.where(from_c, 0.0625, 0.0))
     tile = exact_dot(picker, thin).reshape(half_rows, SUB, depth // 2)
 
-    def put(i):
-        send_ref[pl.ds(i * half_rows, half_rows)] = tile
-
-    each(copies, half_rows, put)
+    send_ref[...] = tile
 
 
 def coarse_and_up(
@@ -286,17 +291,17 @@
 
     low_half = iota((SUB, depth1), 0) < SUB // 2
 
+    chip = lax.div(gy, 2)
+
     def place(k):
         x, z = k // across, k % across
         at = z * SUB + MARGIN
         if not isinstance(z, int):
             at = pl.multiple_of(at, SUB)
-        half = brick1 // 2
+        swapped = odd == (z == chip)
         for i in range(brick1):
-            swapped = odd if i < half else jnp.logical_not(odd)
-            low, high = k * brick1 + i % half, k * brick1 + half + i % half
-            low = jnp.where(swapped, other_ref[low], own_ref[low])
-            high = jnp.where(swapped, other_ref[high], own_ref[high])
+            own, other = own_ref[k * brick1 + i], other_ref[k * brick1 + i]
+            low, high = jnp.where(swapped, other, own), jnp.where(swapped, own, other)
             row = PAD + x * brick1 + i
             f_ref[row, pl.ds(at, SUB)] = jnp.where(low_half, low, high)
             h_ref[row, pl.ds(at, SUB)] = turn(jnp.where(low_half, high, low), SUB // 2, 0)
@@ -573,11 +578,20 @@
     return pairs
 
 
+def at_distance(along_x, along_y, axis, distance):
+    pairs = []
+    for x in range(along_x):
+        for y in range(along_y):
+            to = (x ^ distance, y) if axis == "gx" else (x, y ^ (2 * distance + 1))
+            pairs.append((x * along_y + y, to[0] * along_y + to[1]))
+    return pairs
+
+
 def body(right_side, coefficient):
     along_x, along_y = lax.axis_size("gx"), lax.axis_size("gy")
     rows, cols, depth = right_side.shape
     assert cols == 2 * DEEP_C and rows % 4 == 0 and depth % 256 == 0
-    assert along_x % 2 == 0 and along_y % 2 == 0
+    assert along_x & (along_x - 1) == 0 and along_y & (along_y - 1) == 0 and along_x * along_y > 3
     small = 16 << 20
     strip = (DEEP_F + DEEP_C, cols, depth)
     odd = lax.rem(lax.axis_index("gx"), 2) == 1
@@ -600,16 +614,22 @@
 
     wide = (cols + 2 * DEEP_C, depth)
     half = (rows // 2, SUB, depth // 2)
-    copies = along_x * along_y // 2
     send, *state = call(
-        functools.partial(fine_down, along_x, along_y, copies),
-        [(copies * half[0],) + half[1:], (tall - 2,) + wide, (tall,) + wide, (tall + 1,) + wide]
+        functools.partial(fine_down, along_x, along_y),
+        [half, (tall - 2,) + wide, (tall,) + wide, (tall + 1,) + wide]
         + [(tall,) + wide] * 3,
         [(tall + 2,) + wide, (tall,) + wide, (rows, cols, depth)],
         (right_side, coefficient, a, b, z, k),
-        small + 2 * 4 * copies * half[0] * half[1] * half[2],
+        small,
     )
-    own = lax.all_to_all(send, ("gx", "gy"), 0, 0, tiled=True)
+    own = send
+    for axis, count in [("gy", along_y // 2), ("gx", along_x)]:
+        parts = [own] + [
+            lax.ppermute(own, ("gx", "gy"), at_distance(along_x, along_y, axis, distance))
+            for distance in range(1, count)
+        ]
+        shape = (count * own.shape[0],) + own.shape[1:]
+        (own,) = call(functools.partial(line_up, axis), [shape], [], parts, small + 8 * math.prod(shape))
     other = lax.ppermute(own, "gy", pairs_from(0, along_y))
 
     rows1, cols1, depth1 = along_x * half[0], along_y * (cols // 2), half[2]

time: 32.8 us -> 31.1 us (0.948)
  blocking collectives: 14.6 us -> 0 us
  starting transfers between devices: 6.64 us -> 13.5 us
  waiting for transfers between devices: 6.86 us -> 13 us
    all_to_all x1 -> x0, blocking collectives: 14.6 us -> none  [body(): own = lax.all_to_all(send, ('gx', 'gy'), 0, 0, tiled=True)]
    ppermute x0 -> x6, starting transfers between devices: none -> 6.99 us  [body(): lax.ppermute(own, ('gx', 'gy'), at_distance(along_x, along_y, axis, dista...]
    ppermute x0 -> x6, waiting for transfers between devices: none -> 5.89 us  [body(): lax.ppermute(own, ('gx', 'gy'), at_distance(along_x, along_y, axis, dista...]
    pallas_call x3 -> x5, Pallas kernels: 3.64 us -> 3.61 us  [call(): pl.pallas_call(kernel, out_shape=[jax.ShapeDtypeStruct(s, F32) for s in o...]
  transfers between devices with their start and end apart: 5 -> 11, of which waited for: 3 -> 8; matrix products, arithmetic and copies ran while one was open for 0% -> 0% of each run, Pallas kernels for 0% -> 0%
where the time goes in v6:
time: 31.1 us; the launch traced here: 30.9 us
  starting transfers between devices  13.5 us (43%)
  waiting for transfers between devices  13 us (42%)
  Pallas kernels  3.61 us (12%)
  local copies, waits for them, and re-layouts  0.85 us (3%)
    ppermute x6, starting transfers between devices, body(): lax.ppermute(own, ('gx', 'gy'), at_distance(along_x, along_y, axis, dista...  6.99 us
    ppermute x6, waiting for transfers between devices, body(): lax.ppermute(own, ('gx', 'gy'), at_distance(along_x, along_y, axis, dista...  5.89 us
    ppermute x1, starting transfers between devices, body(): a = lax.ppermute(a, 'gx', pairs_from(0, along_x))  3.98 us
    pallas_call x5, Pallas kernels, call(): pl.pallas_call(kernel, out_shape=[jax.ShapeDtypeStruct(s, F32) for s in o...  3.61 us
    ppermute x1, waiting for transfers between devices, body(): a = lax.ppermute(a, 'gx', pairs_from(0, along_x))  2.86 us
    ppermute x1, waiting for transfers between devices, body(): z = lax.ppermute(z, ('gx', 'gy'), swaps(along_x, along_y, 'gy', 1))  2.84 us
    ppermute x1, starting transfers between devices, body(): z = lax.ppermute(z, ('gx', 'gy'), swaps(along_x, along_y, 'gy', 1))  1.38 us
    ppermute x1, waiting for transfers between devices, body(): other = lax.ppermute(own, 'gy', pairs_from(0, along_y))  1.38 us
  transfers between devices with their start and end apart: 11, of which 8 were waited for; matrix products, arithmetic and copies ran while one was open for 0% of the time, Pallas kernels for 0%

profile of v6, /device:TPU:0, one launch (start us, length us, event | category | flops | bytes accessed | tf_op | source)
XLA Modules:
  0.0 30.9 jit_solution(9917582339081948678)
XLA Ops:
  0.0 0.8 %fusion.2 = (f32[3,8,256]{2,1,0:T(8,128)S(1)}, f32[3,8,256]{2,1,0:T(8,128)S(1)}) fusion(f32[8,8,256]{2,1,0:T(8,128)} %f_ref.3), kind=kLoop, calls=%fused_computation.4 | loop fusion | bytes 98304 | tf_op jit(solution)/shard_map/slice | solution.py:598
  0.8 0.0 copy-done
  0.9 0.5 %collective-permute-start.1 = (f32[7,8,256]{2,1,0:T(8,128)S(1)}, f32[7,8,256]{2,1,0:T(8,128)S(1)}, u32[]{:S(2)}, u32[]{:S(2)}) collective-permute-start(f32[7,8,256]{2,1,0:T(8,128)S(1)} %get-tuple-element.23), channel_id=1, source_target_pairs={{0,1},{1,0},{2,3},{3,2},{4,5},{5,4},{6,7},{7,6},{8,16},{9,17},{10,... | collective-permute-start | bytes 172040 | tf_op jit(solution)/shard_map/ppermute | solution.py:602
  1.4 4.0 %collective-permute-start = (f32[7,8,256]{2,1,0:T(8,128)S(1)}, f32[7,8,256]{2,1,0:T(8,128)S(1)}, u32[]{:S(2)}, u32[]{:S(2)}) collective-permute-start(f32[7,8,256]{2,1,0:T(8,128)S(1)} %get-tuple-element.24), channel_id=1, source_target_pairs={{0,8},{8,0},{16,24},{24,16},{1,9},{9,1},{17,25},{25,17},{2,10},{10... | collective-permute-start | bytes 172040 | tf_op jit(solution)/shard_map/ppermute | solution.py:601
  5.4 2.9 %collective-permute-done.a_ref = f32[7,8,256]{2,1,0:T(8,128)S(1)} collective-permute-done((f32[7,8,256]{2,1,0:T(8,128)S(1)}, f32[7,8,256]{2,1,0:T(8,128)S(1)}, u32[]{:S(2)}, u32[]{:S(2)}) %collective-permute-start) | collective-permute-done | bytes 57376 | tf_op jit(solution)/shard_map/ppermute | solution.py:601
  8.3 1.4 %collective-permute-start.2 = (f32[11,8,256]{2,1,0:T(8,128)S(1)}, f32[11,8,256]{2,1,0:T(8,128)S(1)}, u32[]{:S(2)}, u32[]{:S(2)}) collective-permute-start(f32[11,8,256]{2,1,0:T(8,128)S(1)} %get-tuple-element.14), channel_id=1, source_target_pairs={{0,8},{1,2},{2,1},{3,4},{4,3},{5,6},{6,5},{7,15},{8,0},{9,10},{10,... | collective-permute-start | bytes 270344 | tf_op jit(solution)/shard_map/ppermute | solution.py:613
  9.6 0.4 %collective-permute-start.3 = (f32[11,8,256]{2,1,0:T(8,128)S(1)}, f32[11,8,256]{2,1,0:T(8,128)S(1)}, u32[]{:S(2)}, u32[]{:S(2)}) collective-permute-start(f32[11,8,256]{2,1,0:T(8,128)S(1)} %get-tuple-element.15), channel_id=1, source_target_pairs={{0,1},{1,0},{2,3},{3,2},{4,5},{5,4},{6,7},{7,6},{8,9},{9,8},{10,11... | collective-permute-start | bytes 270344 | tf_op jit(solution)/shard_map/ppermute | solution.py:612
  10.0 2.8 %collective-permute-done.2.z_ref = f32[11,8,256]{2,1,0:T(8,128)S(1)} collective-permute-done((f32[11,8,256]{2,1,0:T(8,128)S(1)}, f32[11,8,256]{2,1,0:T(8,128)S(1)}, u32[]{:S(2)}, u32[]{:S(2)}) %collective-permute-start.2) | collective-permute-done | bytes 90144 | tf_op jit(solution)/shard_map/ppermute | solution.py:613
  12.9 0.8 %shard_map.29 = (f32[4,8,128]{2,1,0:T(8,128)S(1)}, f32[12,16,256]{2,1,0:T(8,128)S(1)}, f32[14,16,256]{2,1,0:T(8,128)S(1)}, f32[15,16,256]{2,1,0:T(8,128)S(1)}, f...) custom-call(f32[8,8,256]{2,1,0:T(8,128)S(1)} %copy-done.1, ...), custom_call_target="tpu_custom_call" | custom-call | tf_op jit(solution)/shard_map/pallas_call | solution.py:83
  13.6 0.8 %collective-permute-start.6 = (f32[4,8,128]{2,1,0:T(8,128)S(1)}, f32[4,8,128]{2,1,0:T(8,128)S(1)}, u32[]{:S(2)}, u32[]{:S(2)}) collective-permute-start(f32[4,8,128]{2,1,0:T(8,128)S(1)} %get-tuple-element.16.refs_0_), channel_id=1, source_target_pairs={{0,7},{1,6},{2,5},{3,4},{4,3},{5,2},{6,1},{7,0},{8,15},{9,14},{10,... | collective-permute-start | bytes 49160 | tf_op jit(solution)/shard_map/ppermute | solution.py:628
  14.4 1.5 %collective-permute-start.5 = (f32[4,8,128]{2,1,0:T(8,128)S(1)}, f32[4,8,128]{2,1,0:T(8,128)S(1)}, u32[]{:S(2)}, u32[]{:S(2)}) collective-permute-start(f32[4,8,128]{2,1,0:T(8,128)S(1)} %get-tuple-element.16.refs_0_), channel_id=1, source_target_pairs={{0,5},{1,4},{2,7},{3,6},{4,1},{5,0},{6,3},{7,2},{8,13},{9,12},{10,... | collective-permute-start | bytes 49160 | tf_op jit(solution)/shard_map/ppermute | solution.py:628
  15.9 1.2 %collective-permute-start.4 = (f32[4,8,128]{2,1,0:T(8,128)S(1)}, f32[4,8,128]{2,1,0:T(8,128)S(1)}, u32[]{:S(2)}, u32[]{:S(2)}) collective-permute-start(f32[4,8,128]{2,1,0:T(8,128)S(1)} %get-tuple-element.16.refs_0_), channel_id=1, source_target_pairs={{0,3},{1,2},{2,1},{3,0},{4,7},{5,6},{6,5},{7,4},{8,11},{9,10},{10,... | collective-permute-start | bytes 49160 | tf_op jit(solution)/shard_map/ppermute | solution.py:628
  17.1 1.7 %collective-permute-done.6.refs_3_ = f32[4,8,128]{2,1,0:T(8,128)S(1)} collective-permute-done((f32[4,8,128]{2,1,0:T(8,128)S(1)}, f32[4,8,128]{2,1,0:T(8,128)S(1)}, u32[]{:S(2)}, u32[]{:S(2)}) %collective-permute-start.6) | collective-permute-done | bytes 16416 | tf_op jit(solution)/shard_map/ppermute | solution.py:628
  18.8 0.0 collective-permute-done.5.refs_2_
  18.8 0.2 collective-permute-done.4.refs_1_
  19.1 1.6 %collective-permute-start.9 = (f32[16,8,128]{2,1,0:T(8,128)S(1)}, f32[16,8,128]{2,1,0:T(8,128)S(1)}, u32[]{:S(2)}, u32[]{:S(2)}) collective-permute-start(f32[16,8,128]{2,1,0:T(8,128)S(1)} %shard_map.30.refs_0_), channel_id=1, source_target_pairs={{0,24},{1,25},{2,26},{3,27},{4,28},{5,29},{6,30},{7,31},{8,16},{9,... | collective-permute-start | bytes 196616 | tf_op jit(solution)/shard_map/ppermute | solution.py:628
  20.7 1.2 %collective-permute-start.8 = (f32[16,8,128]{2,1,0:T(8,128)S(1)}, f32[16,8,128]{2,1,0:T(8,128)S(1)}, u32[]{:S(2)}, u32[]{:S(2)}) collective-permute-start(f32[16,8,128]{2,1,0:T(8,128)S(1)} %shard_map.30.refs_0_), channel_id=1, source_target_pairs={{0,16},{1,17},{2,18},{3,19},{4,20},{5,21},{6,22},{7,23},{8,24},{9,... | collective-permute-start | bytes 196616 | tf_op jit(solution)/shard_map/ppermute | solution.py:628
  21.9 0.7 %collective-permute-start.7 = (f32[16,8,128]{2,1,0:T(8,128)S(1)}, f32[16,8,128]{2,1,0:T(8,128)S(1)}, u32[]{:S(2)}, u32[]{:S(2)}) collective-permute-start(f32[16,8,128]{2,1,0:T(8,128)S(1)} %shard_map.30.refs_0_), channel_id=1, source_target_pairs={{0,8},{1,9},{2,10},{3,11},{4,12},{5,13},{6,14},{7,15},{8,0},{9,1},... | collective-permute-start | bytes 196616 | tf_op jit(solution)/shard_map/ppermute | solution.py:628
  22.6 1.7 %collective-permute-done.9.refs_3_ = f32[16,8,128]{2,1,0:T(8,128)S(1)} collective-permute-done((f32[16,8,128]{2,1,0:T(8,128)S(1)}, f32[16,8,128]{2,1,0:T(8,128)S(1)}, u32[]{:S(2)}, u32[]{:S(2)}) %collective-permute-start.9) | collective-permute-done | bytes 65568 | tf_op jit(solution)/shard_map/ppermute | solution.py:628
  24.3 1.9 %collective-permute-done.8.refs_2_ = f32[16,8,128]{2,1,0:T(8,128)S(1)} collective-permute-done((f32[16,8,128]{2,1,0:T(8,128)S(1)}, f32[16,8,128]{2,1,0:T(8,128)S(1)}, u32[]{:S(2)}, u32[]{:S(2)}) %collective-permute-start.8) | collective-permute-done | bytes 65568 | tf_op jit(solution)/shard_map/ppermute | solution.py:628
  26.2 0.4 %collective-permute-done.7.refs_1_ = f32[16,8,128]{2,1,0:T(8,128)S(1)} collective-permute-done((f32[16,8,128]{2,1,0:T(8,128)S(1)}, f32[16,8,128]{2,1,0:T(8,128)S(1)}, u32[]{:S(2)}, u32[]{:S(2)}) %collective-permute-start.7) | collective-permute-done | bytes 65568 | tf_op jit(solution)/shard_map/ppermute | solution.py:628
  26.6 0.2 collective-permute-start.10
  26.8 1.4 %collective-permute-done.10.other_ref = f32[64,8,128]{2,1,0:T(8,128)S(1)} collective-permute-done((f32[64,8,128]{2,1,0:T(8,128)S(1)}, f32[64,8,128]{2,1,0:T(8,128)S(1)}, u32[]{:S(2)}, u32[]{:S(2)}) %collective-permute-start.10) | collective-permute-done | bytes 262176 | tf_op jit(solution)/shard_map/ppermute | solution.py:633
  28.2 2.8 %shard_map.32 = f32[8,8,256]{2,1,0:T(8,128)} custom-call(f32[64,8,128]{2,1,0:T(8,128)S(1)} %shard_map.31.own_ref, f32[64,8,128]{2,1,0:T(8,128)S(1)} %collective-permute-done.10.other_ref, f32[12,16,256]{2,1,0:T(8,128)S(1)} %get-tuple-element.17.u0_ref, f32[14,16,256]{2,1,0:T(8,128)S(1)} %get-tuple-element.18.fx_ref, ...), custom_call_target="tpu_custom_call" | custom-call | tf_op jit(solution)/shard_map/pallas_call | solution.py:83
  (10 shorter events, 0.1 us)
Async XLA Ops:
  0.0 0.8 %copy-start = (f32[8,8,256]{2,1,0:T(8,128)S(1)}, f32[8,8,256]{2,1,0:T(8,128)}, u32[]{:S(2)}) copy-start(f32[8,8,256]{2,1,0:T(8,128)} %c_ref.3) | copy-start | bytes 196612
  0.8 7.4 %copy-start.1 = (f32[8,8,256]{2,1,0:T(8,128)S(1)}, f32[8,8,256]{2,1,0:T(8,128)}, u32[]{:S(2)}) copy-start(f32[8,8,256]{2,1,0:T(8,128)} %f_ref.3) | copy-start | bytes 196612
  0.9 4.5 %collective-permute-start.1 = (f32[7,8,256]{2,1,0:T(8,128)S(1)}, f32[7,8,256]{2,1,0:T(8,128)S(1)}, u32[]{:S(2)}, u32[]{:S(2)}) collective-permute-start(f32[7,8,256]{2,1,0:T(8,128)S(1)} %get-tuple-element.23), channel_id=1, source_target_pairs={{0,1},{1,0},{2,3},{3,2},{4,5},{5,4},{6,7},{7,6},{8,16},{9,17},{10,... | collective-permute-start | bytes 172040 | tf_op jit(solution)/shard_map/ppermute | solution.py:602
  1.4 6.8 %collective-permute-start = (f32[7,8,256]{2,1,0:T(8,128)S(1)}, f32[7,8,256]{2,1,0:T(8,128)S(1)}, u32[]{:S(2)}, u32[]{:S(2)}) collective-permute-start(f32[7,8,256]{2,1,0:T(8,128)S(1)} %get-tuple-element.24), channel_id=1, source_target_pairs={{0,8},{8,0},{16,24},{24,16},{1,9},{9,1},{17,25},{25,17},{2,10},{10... | collective-permute-start | bytes 172040 | tf_op jit(solution)/shard_map/ppermute | solution.py:601
  8.3 4.6 %collective-permute-start.2 = (f32[11,8,256]{2,1,0:T(8,128)S(1)}, f32[11,8,256]{2,1,0:T(8,128)S(1)}, u32[]{:S(2)}, u32[]{:S(2)}) collective-permute-start(f32[11,8,256]{2,1,0:T(8,128)S(1)} %get-tuple-element.14), channel_id=1, source_target_pairs={{0,8},{1,2},{2,1},{3,4},{4,3},{5,6},{6,5},{7,15},{8,0},{9,10},{10,... | collective-permute-start | bytes 270344 | tf_op jit(solution)/shard_map/ppermute | solution.py:613
  9.6 3.2 %collective-permute-start.3 = (f32[11,8,256]{2,1,0:T(8,128)S(1)}, f32[11,8,256]{2,1,0:T(8,128)S(1)}, u32[]{:S(2)}, u32[]{:S(2)}) collective-permute-start(f32[11,8,256]{2,1,0:T(8,128)S(1)} %get-tuple-element.15), channel_id=1, source_target_pairs={{0,1},{1,0},{2,3},{3,2},{4,5},{5,4},{6,7},{7,6},{8,9},{9,8},{10,11... | collective-permute-start | bytes 270344 | tf_op jit(solution)/shard_map/ppermute | solution.py:612
  13.6 5.1 %collective-permute-start.6 = (f32[4,8,128]{2,1,0:T(8,128)S(1)}, f32[4,8,128]{2,1,0:T(8,128)S(1)}, u32[]{:S(2)}, u32[]{:S(2)}) collective-permute-start(f32[4,8,128]{2,1,0:T(8,128)S(1)} %get-tuple-element.16.refs_0_), channel_id=1, source_target_pairs={{0,7},{1,6},{2,5},{3,4},{4,3},{5,2},{6,1},{7,0},{8,15},{9,14},{10,... | collective-permute-start | bytes 49160 | tf_op jit(solution)/shard_map/ppermute | solution.py:628
  14.4 4.4 %collective-permute-start.5 = (f32[4,8,128]{2,1,0:T(8,128)S(1)}, f32[4,8,128]{2,1,0:T(8,128)S(1)}, u32[]{:S(2)}, u32[]{:S(2)}) collective-permute-start(f32[4,8,128]{2,1,0:T(8,128)S(1)} %get-tuple-element.16.refs_0_), channel_id=1, source_target_pairs={{0,5},{1,4},{2,7},{3,6},{4,1},{5,0},{6,3},{7,2},{8,13},{9,12},{10,... | collective-permute-start | bytes 49160 | tf_op jit(solution)/shard_map/ppermute | solution.py:628
  15.9 3.2 %collective-permute-start.4 = (f32[4,8,128]{2,1,0:T(8,128)S(1)}, f32[4,8,128]{2,1,0:T(8,128)S(1)}, u32[]{:S(2)}, u32[]{:S(2)}) collective-permute-start(f32[4,8,128]{2,1,0:T(8,128)S(1)} %get-tuple-element.16.refs_0_), channel_id=1, source_target_pairs={{0,3},{1,2},{2,1},{3,0},{4,7},{5,6},{6,5},{7,4},{8,11},{9,10},{10,... | collective-permute-start | bytes 49160 | tf_op jit(solution)/shard_map/ppermute | solution.py:628
  19.1 5.2 %collective-permute-start.9 = (f32[16,8,128]{2,1,0:T(8,128)S(1)}, f32[16,8,128]{2,1,0:T(8,128)S(1)}, u32[]{:S(2)}, u32[]{:S(2)}) collective-permute-start(f32[16,8,128]{2,1,0:T(8,128)S(1)} %shard_map.30.refs_0_), channel_id=1, source_target_pairs={{0,24},{1,25},{2,26},{3,27},{4,28},{5,29},{6,30},{7,31},{8,16},{9,... | collective-permute-start | bytes 196616 | tf_op jit(solution)/shard_map/ppermute | solution.py:628
  20.7 5.5 %collective-permute-start.8 = (f32[16,8,128]{2,1,0:T(8,128)S(1)}, f32[16,8,128]{2,1,0:T(8,128)S(1)}, u32[]{:S(2)}, u32[]{:S(2)}) collective-permute-start(f32[16,8,128]{2,1,0:T(8,128)S(1)} %shard_map.30.refs_0_), channel_id=1, source_target_pairs={{0,16},{1,17},{2,18},{3,19},{4,20},{5,21},{6,22},{7,23},{8,24},{9,... | collective-permute-start | bytes 196616 | tf_op jit(solution)/shard_map/ppermute | solution.py:628
  21.9 4.6 %collective-permute-start.7 = (f32[16,8,128]{2,1,0:T(8,128)S(1)}, f32[16,8,128]{2,1,0:T(8,128)S(1)}, u32[]{:S(2)}, u32[]{:S(2)}) collective-permute-start(f32[16,8,128]{2,1,0:T(8,128)S(1)} %shard_map.30.refs_0_), channel_id=1, source_target_pairs={{0,8},{1,9},{2,10},{3,11},{4,12},{5,13},{6,14},{7,15},{8,0},{9,1},... | collective-permute-start | bytes 196616 | tf_op jit(solution)/shard_map/ppermute | solution.py:628
  26.6 1.6 %collective-permute-start.10 = (f32[64,8,128]{2,1,0:T(8,128)S(1)}, f32[64,8,128]{2,1,0:T(8,128)S(1)}, u32[]{:S(2)}, u32[]{:S(2)}) collective-permute-start(f32[64,8,128]{2,1,0:T(8,128)S(1)} %shard_map.31.own_ref), channel_id=1, source_target_pairs={{0,1},{1,0},{2,3},{3,2},{4,5},{5,4},{6,7},{7,6},{8,9},{9,8},{10,11... | collective-permute-start | bytes 786440 | tf_op jit(solution)/shard_map/ppermute | solution.py:633

commit v7 on v6

--- a/solution.py
+++ b/solution.py
@@ -159,9 +159,9 @@
     put(rows + 2, corners(sub, 1), corners(SUB - 1 - sub, -1))
 
 
-def line_up(axis, *refs):
+def line_up(*refs):
     *block_refs, out_ref = refs
-    here = lax.axis_index("gx") if axis == "gx" else lax.div(lax.axis_index("gy"), 2)
+    here = lax.div(lax.axis_index("gy"), 2)
     size = block_refs[0].shape[0]
     for distance, ref in enumerate(block_refs):
         out_ref[pl.ds((here ^ distance) * size, size)] = ref[...]
@@ -273,16 +273,14 @@
     send_ref[...] = tile
 
 
-def coarse_and_up(
-    along_x, along_y,
-    own_ref, other_ref, u0_ref, fx_ref, wx0_ref, wy0_ref, wz0_ref, inv0_ref,
-    out_ref,
-    f_ref, h_ref, wx_ref, wy_ref, wz_ref, inv_ref, v_ref, diag_ref,
-    f2_ref, h2_ref, e2_ref, e3_ref, py_ref, vw_ref, dw_ref, vx_ref, e1_ref, yy_ref, v0_ref, d0_ref, x0_ref,
-):
+def coarse_and_up(along_x, along_y, *refs):
+    own_refs, other_refs, refs = refs[:along_x], refs[along_x : 2 * along_x], refs[2 * along_x :]
+    u0_ref, fx_ref, wx0_ref, wy0_ref, wz0_ref, inv0_ref, out_ref, *refs = refs
+    f_ref, h_ref, wx_ref, wy_ref, wz_ref, inv_ref, v_ref, diag_ref, f2_ref, h2_ref, e2_ref, e3_ref, *refs = refs
+    py_ref, vw_ref, dw_ref, vx_ref, e1_ref, yy_ref, v0_ref, d0_ref, x0_ref = refs
     gx, gy = lax.axis_index("gx"), lax.axis_index("gy")
     odd = lax.rem(gy, 2) == 1
-    brick1 = own_ref.shape[0] // (along_x * (along_y // 2))
+    brick1 = own_refs[0].shape[0] // (along_y // 2)
     rows1, cols1, depth1 = diag_ref.shape
     across = cols1 // SUB
     registers1 = across * (depth1 // 128)
@@ -293,20 +291,21 @@
 
     chip = lax.div(gy, 2)
 
-    def place(k):
-        x, z = k // across, k % across
+    def place(distance, z):
+        own_ref, other_ref, x = own_refs[distance], other_refs[distance], gx ^ distance
         at = z * SUB + MARGIN
         if not isinstance(z, int):
             at = pl.multiple_of(at, SUB)
         swapped = odd == (z == chip)
         for i in range(brick1):
-            own, other = own_ref[k * brick1 + i], other_ref[k * brick1 + i]
+            own, other = own_ref[z * brick1 + i], other_ref[z * brick1 + i]
             low, high = jnp.where(swapped, other, own), jnp.where(swapped, own, other)
             row = PAD + x * brick1 + i
             f_ref[row, pl.ds(at, SUB)] = jnp.where(low_half, low, high)
             h_ref[row, pl.ds(at, SUB)] = turn(jnp.where(low_half, high, low), SUB // 2, 0)
 
-    each(along_x * across, brick1, place)
+    for distance in range(along_x):
+        each(across, brick1, functools.partial(place, distance))
 
     def clear_beside(ref, row):
         zero = jnp.zeros((MARGIN, depth1), F32)
@@ -622,15 +621,18 @@
         (right_side, coefficient, a, b, z, k),
         small,
     )
-    own = send
-    for axis, count in [("gy", along_y // 2), ("gx", along_x)]:
-        parts = [own] + [
-            lax.ppermute(own, ("gx", "gy"), at_distance(along_x, along_y, axis, distance))
-            for distance in range(1, count)
-        ]
-        shape = (count * own.shape[0],) + own.shape[1:]
-        (own,) = call(functools.partial(line_up, axis), [shape], [], parts, small + 8 * math.prod(shape))
-    other = lax.ppermute(own, "gy", pairs_from(0, along_y))
+    chips = along_y // 2
+    parts = [send] + [
+        lax.ppermute(send, ("gx", "gy"), at_distance(along_x, along_y, "gy", distance))
+        for distance in range(1, chips)
+    ]
+    shape = (chips * half[0],) + half[1:]
+    (line,) = call(line_up, [shape], [], parts, small + 8 * math.prod(shape))
+    own = [line] + [
+        lax.ppermute(line, ("gx", "gy"), at_distance(along_x, along_y, "gx", distance))
+        for distance in range(1, along_x)
+    ]
+    other = [lax.ppermute(line, "gy", pairs_from(0, along_y)) for line in own]
 
     rows1, cols1, depth1 = along_x * half[0], along_y * (cols // 2), half[2]
     whole1 = (rows1 + 2 * PAD + 1, cols1 + 2 * MARGIN, depth1)
@@ -644,12 +646,12 @@
     scratch += [(span - 4, broad, depth1), ((span - 4) * wide[0], depth1)]
     scratch += [(tall,) + wide, (tall, cols, depth), (tall,) + wide]
     size = sum(4 * math.prod(s) for s in scratch)
-    size += 2 * 4 * own.size + 4 * 8 * tall * wide[0] * wide[1]
+    size += 2 * 4 * along_x * line.size + 4 * 8 * tall * wide[0] * wide[1]
     (out,) = call(
         functools.partial(coarse_and_up, along_x, along_y),
         [right_side.shape],
         scratch,
-        (own, other, *state),
+        (*own, *other, *state),
         size + (12 << 20),
     )
     return out

time: 31.1 us -> 30.7 us (0.987)
  waiting for transfers between devices: 13 us -> 10.5 us
  starting transfers between devices: 13.5 us -> 15.5 us
    ppermute x7 -> x10, waiting for transfers between devices: 7.27 us -> 4.85 us  [the longest x3 1.96 us: body(): lax.ppermute(send, ('gx', 'gy'), at_distance(along_x, along_y, 'gy', dist...]
    ppermute x7 -> x10, starting transfers between devices: 7.21 us -> 9.28 us  [the longest x3 3.55 us: body(): lax.ppermute(line, ('gx', 'gy'), at_distance(along_x, along_y, 'gx', dist...]
    pallas_call x5 -> x4, Pallas kernels: 3.61 us -> 3.63 us  [call(): pl.pallas_call(kernel, out_shape=[jax.ShapeDtypeStruct(s, F32) for s in o...]
  transfers between devices with their start and end apart: 11 -> 14, of which waited for: 8 -> 8; matrix products, arithmetic and copies ran while one was open for 0% -> 0% of each run, Pallas kernels for 0% -> 0%
where the time goes in v7:
time: 30.7 us; the launch traced here: 30.6 us
  starting transfers between devices  15.5 us (50%)
  waiting for transfers between devices  10.5 us (34%)
  Pallas kernels  3.63 us (12%)
  local copies, waits for them, and re-layouts  0.85 us (3%)
    ppermute x1, starting transfers between devices, body(): a = lax.ppermute(a, 'gx', pairs_from(0, along_x))  3.98 us
    pallas_call x4, Pallas kernels, call(): pl.pallas_call(kernel, out_shape=[jax.ShapeDtypeStruct(s, F32) for s in o...  3.63 us
    ppermute x3, starting transfers between devices, body(): lax.ppermute(line, ('gx', 'gy'), at_distance(along_x, along_y, 'gx', dist...  3.55 us
    ppermute x3, starting transfers between devices, body(): lax.ppermute(send, ('gx', 'gy'), at_distance(along_x, along_y, 'gy', dist...  3.43 us
    ppermute x1, waiting for transfers between devices, body(): a = lax.ppermute(a, 'gx', pairs_from(0, along_x))  2.86 us
    ppermute x1, waiting for transfers between devices, body(): z = lax.ppermute(z, ('gx', 'gy'), swaps(along_x, along_y, 'gy', 1))  2.84 us
    ppermute x4, starting transfers between devices, body(): other = [lax.ppermute(line, 'gy', pairs_from(0, along_y)) for line in own]  2.29 us
    ppermute x3, waiting for transfers between devices, body(): lax.ppermute(send, ('gx', 'gy'), at_distance(along_x, along_y, 'gy', dist...  1.96 us
  transfers between devices with their start and end apart: 14, of which 8 were waited for; matrix products, arithmetic and copies ran while one was open for 0% of the time, Pallas kernels for 0%

profile of v7, /device:TPU:0, one launch (start us, length us, event | category | flops | bytes accessed | tf_op | source)
XLA Modules:
  0.0 30.6 jit_solution(5268661891702769173)
XLA Ops:
  0.0 0.8 %fusion.2 = (f32[3,8,256]{2,1,0:T(8,128)S(1)}, f32[3,8,256]{2,1,0:T(8,128)S(1)}) fusion(f32[8,8,256]{2,1,0:T(8,128)} %f_ref.3), kind=kLoop, calls=%fused_computation.4 | loop fusion | bytes 98304 | tf_op jit(solution)/shard_map/slice | solution.py:597
  0.9 0.5 %collective-permute-start.1 = (f32[7,8,256]{2,1,0:T(8,128)S(1)}, f32[7,8,256]{2,1,0:T(8,128)S(1)}, u32[]{:S(2)}, u32[]{:S(2)}) collective-permute-start(f32[7,8,256]{2,1,0:T(8,128)S(1)} %get-tuple-element.23), channel_id=1, source_target_pairs={{0,1},{1,0},{2,3},{3,2},{4,5},{5,4},{6,7},{7,6},{8,16},{9,17},{10,... | collective-permute-start | bytes 172040 | tf_op jit(solution)/shard_map/ppermute | solution.py:601
  1.4 4.0 %collective-permute-start = (f32[7,8,256]{2,1,0:T(8,128)S(1)}, f32[7,8,256]{2,1,0:T(8,128)S(1)}, u32[]{:S(2)}, u32[]{:S(2)}) collective-permute-start(f32[7,8,256]{2,1,0:T(8,128)S(1)} %get-tuple-element.24), channel_id=1, source_target_pairs={{0,8},{8,0},{16,24},{24,16},{1,9},{9,1},{17,25},{25,17},{2,10},{10... | collective-permute-start | bytes 172040 | tf_op jit(solution)/shard_map/ppermute | solution.py:600
  5.4 2.9 %collective-permute-done.a_ref = f32[7,8,256]{2,1,0:T(8,128)S(1)} collective-permute-done((f32[7,8,256]{2,1,0:T(8,128)S(1)}, f32[7,8,256]{2,1,0:T(8,128)S(1)}, u32[]{:S(2)}, u32[]{:S(2)}) %collective-permute-start) | collective-permute-done | bytes 57376 | tf_op jit(solution)/shard_map/ppermute | solution.py:600
  8.3 1.4 %collective-permute-start.2 = (f32[11,8,256]{2,1,0:T(8,128)S(1)}, f32[11,8,256]{2,1,0:T(8,128)S(1)}, u32[]{:S(2)}, u32[]{:S(2)}) collective-permute-start(f32[11,8,256]{2,1,0:T(8,128)S(1)} %get-tuple-element.14), channel_id=1, source_target_pairs={{0,8},{1,2},{2,1},{3,4},{4,3},{5,6},{6,5},{7,15},{8,0},{9,10},{10,... | collective-permute-start | bytes 270344 | tf_op jit(solution)/shard_map/ppermute | solution.py:612
  9.6 0.4 %collective-permute-start.3 = (f32[11,8,256]{2,1,0:T(8,128)S(1)}, f32[11,8,256]{2,1,0:T(8,128)S(1)}, u32[]{:S(2)}, u32[]{:S(2)}) collective-permute-start(f32[11,8,256]{2,1,0:T(8,128)S(1)} %get-tuple-element.15), channel_id=1, source_target_pairs={{0,1},{1,0},{2,3},{3,2},{4,5},{5,4},{6,7},{7,6},{8,9},{9,8},{10,11... | collective-permute-start | bytes 270344 | tf_op jit(solution)/shard_map/ppermute | solution.py:611
  10.0 2.8 %collective-permute-done.2.z_ref = f32[11,8,256]{2,1,0:T(8,128)S(1)} collective-permute-done((f32[11,8,256]{2,1,0:T(8,128)S(1)}, f32[11,8,256]{2,1,0:T(8,128)S(1)}, u32[]{:S(2)}, u32[]{:S(2)}) %collective-permute-start.2) | collective-permute-done | bytes 90144 | tf_op jit(solution)/shard_map/ppermute | solution.py:612
  12.9 0.8 %shard_map.29 = (f32[4,8,128]{2,1,0:T(8,128)S(1)}, f32[12,16,256]{2,1,0:T(8,128)S(1)}, f32[14,16,256]{2,1,0:T(8,128)S(1)}, f32[15,16,256]{2,1,0:T(8,128)S(1)}, f...) custom-call(f32[8,8,256]{2,1,0:T(8,128)S(1)} %copy-done.1, ...), custom_call_target="tpu_custom_call" | custom-call | tf_op jit(solution)/shard_map/pallas_call | solution.py:83
  13.6 0.8 %collective-permute-start.6 = (f32[4,8,128]{2,1,0:T(8,128)S(1)}, f32[4,8,128]{2,1,0:T(8,128)S(1)}, u32[]{:S(2)}, u32[]{:S(2)}) collective-permute-start(f32[4,8,128]{2,1,0:T(8,128)S(1)} %get-tuple-element.16.refs_0_), channel_id=1, source_target_pairs={{0,7},{1,6},{2,5},{3,4},{4,3},{5,2},{6,1},{7,0},{8,15},{9,14},{10,... | collective-permute-start | bytes 49160 | tf_op jit(solution)/shard_map/ppermute | solution.py:626
  14.4 1.5 %collective-permute-start.5 = (f32[4,8,128]{2,1,0:T(8,128)S(1)}, f32[4,8,128]{2,1,0:T(8,128)S(1)}, u32[]{:S(2)}, u32[]{:S(2)}) collective-permute-start(f32[4,8,128]{2,1,0:T(8,128)S(1)} %get-tuple-element.16.refs_0_), channel_id=1, source_target_pairs={{0,5},{1,4},{2,7},{3,6},{4,1},{5,0},{6,3},{7,2},{8,13},{9,12},{10,... | collective-permute-start | bytes 49160 | tf_op jit(solution)/shard_map/ppermute | solution.py:626
  15.9 1.2 %collective-permute-start.4 = (f32[4,8,128]{2,1,0:T(8,128)S(1)}, f32[4,8,128]{2,1,0:T(8,128)S(1)}, u32[]{:S(2)}, u32[]{:S(2)}) collective-permute-start(f32[4,8,128]{2,1,0:T(8,128)S(1)} %get-tuple-element.16.refs_0_), channel_id=1, source_target_pairs={{0,3},{1,2},{2,1},{3,0},{4,7},{5,6},{6,5},{7,4},{8,11},{9,10},{10,... | collective-permute-start | bytes 49160 | tf_op jit(solution)/shard_map/ppermute | solution.py:626
  17.1 1.7 %collective-permute-done.6.refs_3_ = f32[4,8,128]{2,1,0:T(8,128)S(1)} collective-permute-done((f32[4,8,128]{2,1,0:T(8,128)S(1)}, f32[4,8,128]{2,1,0:T(8,128)S(1)}, u32[]{:S(2)}, u32[]{:S(2)}) %collective-permute-start.6) | collective-permute-done | bytes 16416 | tf_op jit(solution)/shard_map/ppermute | solution.py:626
  18.8 0.2 collective-permute-done.4.refs_1_
  19.1 1.6 %collective-permute-start.9 = (f32[16,8,128]{2,1,0:T(8,128)S(1)}, f32[16,8,128]{2,1,0:T(8,128)S(1)}, u32[]{:S(2)}, u32[]{:S(2)}) collective-permute-start(f32[16,8,128]{2,1,0:T(8,128)S(1)} %shard_map.30.refs_0_), channel_id=1, source_target_pairs={{0,24},{1,25},{2,26},{3,27},{4,28},{5,29},{6,30},{7,31},{8,16},{9,... | collective-permute-start | bytes 196616 | tf_op jit(solution)/shard_map/ppermute | solution.py:632
  20.7 1.2 %collective-permute-start.8 = (f32[16,8,128]{2,1,0:T(8,128)S(1)}, f32[16,8,128]{2,1,0:T(8,128)S(1)}, u32[]{:S(2)}, u32[]{:S(2)}) collective-permute-start(f32[16,8,128]{2,1,0:T(8,128)S(1)} %shard_map.30.refs_0_), channel_id=1, source_target_pairs={{0,16},{1,17},{2,18},{3,19},{4,20},{5,21},{6,22},{7,23},{8,24},{9,... | collective-permute-start | bytes 196616 | tf_op jit(solution)/shard_map/ppermute | solution.py:632
  21.9 0.7 %collective-permute-start.7 = (f32[16,8,128]{2,1,0:T(8,128)S(1)}, f32[16,8,128]{2,1,0:T(8,128)S(1)}, u32[]{:S(2)}, u32[]{:S(2)}) collective-permute-start(f32[16,8,128]{2,1,0:T(8,128)S(1)} %shard_map.30.refs_0_), channel_id=1, source_target_pairs={{0,8},{1,9},{2,10},{3,11},{4,12},{5,13},{6,14},{7,15},{8,0},{9,1},... | collective-permute-start | bytes 196616 | tf_op jit(solution)/shard_map/ppermute | solution.py:632
  22.6 1.0 %collective-permute-start.10 = (f32[16,8,128]{2,1,0:T(8,128)S(1)}, f32[16,8,128]{2,1,0:T(8,128)S(1)}, u32[]{:S(2)}, u32[]{:S(2)}) collective-permute-start(f32[16,8,128]{2,1,0:T(8,128)S(1)} %shard_map.30.refs_0_), channel_id=1, source_target_pairs={{0,1},{1,0},{2,3},{3,2},{4,5},{5,4},{6,7},{7,6},{8,9},{9,8},{10,11... | collective-permute-start | bytes 196616 | tf_op jit(solution)/shard_map/ppermute | solution.py:635
  23.6 0.7 %collective-permute-done.9.refs_3_ = f32[16,8,128]{2,1,0:T(8,128)S(1)} collective-permute-done((f32[16,8,128]{2,1,0:T(8,128)S(1)}, f32[16,8,128]{2,1,0:T(8,128)S(1)}, u32[]{:S(2)}, u32[]{:S(2)}) %collective-permute-start.9) | collective-permute-done | bytes 65568 | tf_op jit(solution)/shard_map/ppermute | solution.py:632
  24.3 0.8 %collective-permute-start.13 = (f32[16,8,128]{2,1,0:T(8,128)S(1)}, f32[16,8,128]{2,1,0:T(8,128)S(1)}, u32[]{:S(2)}, u32[]{:S(2)}) collective-permute-start(f32[16,8,128]{2,1,0:T(8,128)S(1)} %collective-permute-done.9.refs_3_), channel_id=1, source_target_pairs={{0,1},{1,0},{2,3},{3,2},{4,5},{5,4},{6,7},{7,6},{8,9},{9,8},{10,11... | collective-permute-start | bytes 196616 | tf_op jit(solution)/shard_map/ppermute | solution.py:635
  25.1 1.1 %collective-permute-done.8.refs_2_ = f32[16,8,128]{2,1,0:T(8,128)S(1)} collective-permute-done((f32[16,8,128]{2,1,0:T(8,128)S(1)}, f32[16,8,128]{2,1,0:T(8,128)S(1)}, u32[]{:S(2)}, u32[]{:S(2)}) %collective-permute-start.8) | collective-permute-done | bytes 65568 | tf_op jit(solution)/shard_map/ppermute | solution.py:632
  26.2 0.3 %collective-permute-start.12 = (f32[16,8,128]{2,1,0:T(8,128)S(1)}, f32[16,8,128]{2,1,0:T(8,128)S(1)}, u32[]{:S(2)}, u32[]{:S(2)}) collective-permute-start(f32[16,8,128]{2,1,0:T(8,128)S(1)} %collective-permute-done.8.refs_2_), channel_id=1, source_target_pairs={{0,1},{1,0},{2,3},{3,2},{4,5},{5,4},{6,7},{7,6},{8,9},{9,8},{10,11... | collective-permute-start | bytes 196616 | tf_op jit(solution)/shard_map/ppermute | solution.py:635
  26.7 0.7 %collective-permute-done.12.refs_6_ = f32[16,8,128]{2,1,0:T(8,128)S(1)} collective-permute-done((f32[16,8,128]{2,1,0:T(8,128)S(1)}, f32[16,8,128]{2,1,0:T(8,128)S(1)}, u32[]{:S(2)}, u32[]{:S(2)}) %collective-permute-start.12) | collective-permute-done | bytes 65568 | tf_op jit(solution)/shard_map/ppermute | solution.py:635
  27.4 0.4 %collective-permute-done.11.refs_5_ = f32[16,8,128]{2,1,0:T(8,128)S(1)} collective-permute-done((f32[16,8,128]{2,1,0:T(8,128)S(1)}, f32[16,8,128]{2,1,0:T(8,128)S(1)}, u32[]{:S(2)}, u32[]{:S(2)}) %collective-permute-start.11) | collective-permute-done | bytes 65568 | tf_op jit(solution)/shard_map/ppermute | solution.py:635
  27.8 2.8 %shard_map.31 = f32[8,8,256]{2,1,0:T(8,128)} custom-call(f32[16,8,128]{2,1,0:T(8,128)S(1)} %shard_map.30.refs_0_, f32[16,8,128]{2,1,0:T(8,128)S(1)} %collective-permute-done.7.refs_1_, f32[16,8,128]{2,1,0:T(8,128)S(1)} %collective-permute-done.8.refs_2_, f32[16,8,128]{2,1,0:T(8,128)S(1)} %collective-permute-done.9.refs_3_, ...), custom_call_target="tpu_custom_call" | custom-call | tf_op jit(solution)/shard_map/pallas_call | solution.py:83
  (15 shorter events, 0.4 us)
Async XLA Ops:
  0.0 0.8 %copy-start = (f32[8,8,256]{2,1,0:T(8,128)S(1)}, f32[8,8,256]{2,1,0:T(8,128)}, u32[]{:S(2)}) copy-start(f32[8,8,256]{2,1,0:T(8,128)} %c_ref.3) | copy-start | bytes 196612
  0.8 7.4 %copy-start.1 = (f32[8,8,256]{2,1,0:T(8,128)S(1)}, f32[8,8,256]{2,1,0:T(8,128)}, u32[]{:S(2)}) copy-start(f32[8,8,256]{2,1,0:T(8,128)} %f_ref.3) | copy-start | bytes 196612
  0.9 4.5 %collective-permute-start.1 = (f32[7,8,256]{2,1,0:T(8,128)S(1)}, f32[7,8,256]{2,1,0:T(8,128)S(1)}, u32[]{:S(2)}, u32[]{:S(2)}) collective-permute-start(f32[7,8,256]{2,1,0:T(8,128)S(1)} %get-tuple-element.23), channel_id=1, source_target_pairs={{0,1},{1,0},{2,3},{3,2},{4,5},{5,4},{6,7},{7,6},{8,16},{9,17},{10,... | collective-permute-start | bytes 172040 | tf_op jit(solution)/shard_map/ppermute | solution.py:601
  1.4 6.8 %collective-permute-start = (f32[7,8,256]{2,1,0:T(8,128)S(1)}, f32[7,8,256]{2,1,0:T(8,128)S(1)}, u32[]{:S(2)}, u32[]{:S(2)}) collective-permute-start(f32[7,8,256]{2,1,0:T(8,128)S(1)} %get-tuple-element.24), channel_id=1, source_target_pairs={{0,8},{8,0},{16,24},{24,16},{1,9},{9,1},{17,25},{25,17},{2,10},{10... | collective-permute-start | bytes 172040 | tf_op jit(solution)/shard_map/ppermute | solution.py:600
  8.3 4.6 %collective-permute-start.2 = (f32[11,8,256]{2,1,0:T(8,128)S(1)}, f32[11,8,256]{2,1,0:T(8,128)S(1)}, u32[]{:S(2)}, u32[]{:S(2)}) collective-permute-start(f32[11,8,256]{2,1,0:T(8,128)S(1)} %get-tuple-element.14), channel_id=1, source_target_pairs={{0,8},{1,2},{2,1},{3,4},{4,3},{5,6},{6,5},{7,15},{8,0},{9,10},{10,... | collective-permute-start | bytes 270344 | tf_op jit(solution)/shard_map/ppermute | solution.py:612
  9.6 3.2 %collective-permute-start.3 = (f32[11,8,256]{2,1,0:T(8,128)S(1)}, f32[11,8,256]{2,1,0:T(8,128)S(1)}, u32[]{:S(2)}, u32[]{:S(2)}) collective-permute-start(f32[11,8,256]{2,1,0:T(8,128)S(1)} %get-tuple-element.15), channel_id=1, source_target_pairs={{0,1},{1,0},{2,3},{3,2},{4,5},{5,4},{6,7},{7,6},{8,9},{9,8},{10,11... | collective-permute-start | bytes 270344 | tf_op jit(solution)/shard_map/ppermute | solution.py:611
  13.6 5.1 %collective-permute-start.6 = (f32[4,8,128]{2,1,0:T(8,128)S(1)}, f32[4,8,128]{2,1,0:T(8,128)S(1)}, u32[]{:S(2)}, u32[]{:S(2)}) collective-permute-start(f32[4,8,128]{2,1,0:T(8,128)S(1)} %get-tuple-element.16.refs_0_), channel_id=1, source_target_pairs={{0,7},{1,6},{2,5},{3,4},{4,3},{5,2},{6,1},{7,0},{8,15},{9,14},{10,... | collective-permute-start | bytes 49160 | tf_op jit(solution)/shard_map/ppermute | solution.py:626
  14.4 4.4 %collective-permute-start.5 = (f32[4,8,128]{2,1,0:T(8,128)S(1)}, f32[4,8,128]{2,1,0:T(8,128)S(1)}, u32[]{:S(2)}, u32[]{:S(2)}) collective-permute-start(f32[4,8,128]{2,1,0:T(8,128)S(1)} %get-tuple-element.16.refs_0_), channel_id=1, source_target_pairs={{0,5},{1,4},{2,7},{3,6},{4,1},{5,0},{6,3},{7,2},{8,13},{9,12},{10,... | collective-permute-start | bytes 49160 | tf_op jit(solution)/shard_map/ppermute | solution.py:626
  15.9 3.2 %collective-permute-start.4 = (f32[4,8,128]{2,1,0:T(8,128)S(1)}, f32[4,8,128]{2,1,0:T(8,128)S(1)}, u32[]{:S(2)}, u32[]{:S(2)}) collective-permute-start(f32[4,8,128]{2,1,0:T(8,128)S(1)} %get-tuple-element.16.refs_0_), channel_id=1, source_target_pairs={{0,3},{1,2},{2,1},{3,0},{4,7},{5,6},{6,5},{7,4},{8,11},{9,10},{10,... | collective-permute-start | bytes 49160 | tf_op jit(solution)/shard_map/ppermute | solution.py:626
  19.1 5.2 %collective-permute-start.9 = (f32[16,8,128]{2,1,0:T(8,128)S(1)}, f32[16,8,128]{2,1,0:T(8,128)S(1)}, u32[]{:S(2)}, u32[]{:S(2)}) collective-permute-start(f32[16,8,128]{2,1,0:T(8,128)S(1)} %shard_map.30.refs_0_), channel_id=1, source_target_pairs={{0,24},{1,25},{2,26},{3,27},{4,28},{5,29},{6,30},{7,31},{8,16},{9,... | collective-permute-start | bytes 196616 | tf_op jit(solution)/shard_map/ppermute | solution.py:632
  20.7 5.5 %collective-permute-start.8 = (f32[16,8,128]{2,1,0:T(8,128)S(1)}, f32[16,8,128]{2,1,0:T(8,128)S(1)}, u32[]{:S(2)}, u32[]{:S(2)}) collective-permute-start(f32[16,8,128]{2,1,0:T(8,128)S(1)} %shard_map.30.refs_0_), channel_id=1, source_target_pairs={{0,16},{1,17},{2,18},{3,19},{4,20},{5,21},{6,22},{7,23},{8,24},{9,... | collective-permute-start | bytes 196616 | tf_op jit(solution)/shard_map/ppermute | solution.py:632
  21.9 4.6 %collective-permute-start.7 = (f32[16,8,128]{2,1,0:T(8,128)S(1)}, f32[16,8,128]{2,1,0:T(8,128)S(1)}, u32[]{:S(2)}, u32[]{:S(2)}) collective-permute-start(f32[16,8,128]{2,1,0:T(8,128)S(1)} %shard_map.30.refs_0_), channel_id=1, source_target_pairs={{0,8},{1,9},{2,10},{3,11},{4,12},{5,13},{6,14},{7,15},{8,0},{9,1},... | collective-permute-start | bytes 196616 | tf_op jit(solution)/shard_map/ppermute | solution.py:632
  22.6 4.1 %collective-permute-start.10 = (f32[16,8,128]{2,1,0:T(8,128)S(1)}, f32[16,8,128]{2,1,0:T(8,128)S(1)}, u32[]{:S(2)}, u32[]{:S(2)}) collective-permute-start(f32[16,8,128]{2,1,0:T(8,128)S(1)} %shard_map.30.refs_0_), channel_id=1, source_target_pairs={{0,1},{1,0},{2,3},{3,2},{4,5},{5,4},{6,7},{7,6},{8,9},{9,8},{10,11... | collective-permute-start | bytes 196616 | tf_op jit(solution)/shard_map/ppermute | solution.py:635
  24.3 2.4 %collective-permute-start.13 = (f32[16,8,128]{2,1,0:T(8,128)S(1)}, f32[16,8,128]{2,1,0:T(8,128)S(1)}, u32[]{:S(2)}, u32[]{:S(2)}) collective-permute-start(f32[16,8,128]{2,1,0:T(8,128)S(1)} %collective-permute-done.9.refs_3_), channel_id=1, source_target_pairs={{0,1},{1,0},{2,3},{3,2},{4,5},{5,4},{6,7},{7,6},{8,9},{9,8},{10,11... | collective-permute-start | bytes 196616 | tf_op jit(solution)/shard_map/ppermute | solution.py:635
  26.2 1.3 %collective-permute-start.12 = (f32[16,8,128]{2,1,0:T(8,128)S(1)}, f32[16,8,128]{2,1,0:T(8,128)S(1)}, u32[]{:S(2)}, u32[]{:S(2)}) collective-permute-start(f32[16,8,128]{2,1,0:T(8,128)S(1)} %collective-permute-done.8.refs_2_), channel_id=1, source_target_pairs={{0,1},{1,0},{2,3},{3,2},{4,5},{5,4},{6,7},{7,6},{8,9},{9,8},{10,11... | collective-permute-start | bytes 196616 | tf_op jit(solution)/shard_map/ppermute | solution.py:635
  26.5 1.3 %collective-permute-start.11 = (f32[16,8,128]{2,1,0:T(8,128)S(1)}, f32[16,8,128]{2,1,0:T(8,128)S(1)}, u32[]{:S(2)}, u32[]{:S(2)}) collective-permute-start(f32[16,8,128]{2,1,0:T(8,128)S(1)} %collective-permute-done.7.refs_1_), channel_id=1, source_target_pairs={{0,1},{1,0},{2,3},{3,2},{4,5},{5,4},{6,7},{7,6},{8,9},{9,8},{10,11... | collective-permute-start | bytes 196616 | tf_op jit(solution)/shard_map/ppermute | solution.py:635

commit v8 on v7

--- a/solution.py
+++ b/solution.py
@@ -75,8 +75,20 @@
     return jnp.logical_not(after | before)
 
 
+def thirds(value):
+    parts = []
+    for _ in range(3):
+        parts.append(value.astype(jnp.bfloat16))
+        value = value - parts[-1].astype(F32)
+    return parts
+
+
 def exact_dot(a, b):
-    return jnp.dot(a, b, precision=lax.Precision.HIGHEST, preferred_element_type=F32)
+    if a.dtype == F32:
+        terms = [jnp.dot(part, b, preferred_element_type=F32) for part in thirds(a)]
+    else:
+        terms = [jnp.dot(a, part, preferred_element_type=F32) for part in thirds(b)]
+    return (terms[2] + terms[1]) + terms[0]
 
 
 def call(kernel, out_shapes, scratch, args, limit):
@@ -109,17 +121,14 @@
         copy.wait()
 
 
-def row_sources(along_x, rows, f_ref, c_ref, a_ref, b_ref):
-    gx = lax.axis_index("gx")
-    odd = lax.rem(gx, 2) == 1
-    has_before = (gx > 0).astype(F32)
-    has_after = (gx < along_x - 1).astype(F32)
+def row_sources(rows, f_ref, c_ref, a_ref, b_ref):
+    odd = lax.rem(lax.axis_index("gx"), 2) == 1
 
     def before(i):
-        return jnp.where(odd, a_ref[i], b_ref[i]) * has_before
+        return jnp.where(odd, a_ref[i], b_ref[i])
 
     def after(i):
-        return jnp.where(odd, b_ref[i], a_ref[i]) * has_after
+        return jnp.where(odd, b_ref[i], a_ref[i])
 
     def f_row(i):
         if i < 0:
@@ -134,29 +143,27 @@
     return f_row, c_row
 
 
-def pack_cols(along_x, f_ref, c_ref, a_ref, b_ref, z_ref, k_ref):
+def pack_cols(f_ref, c_ref, a_ref, b_ref, z_ref, k_ref):
     rows = f_ref.shape[0]
-    f_row, c_row = row_sources(along_x, rows, f_ref, c_ref, a_ref, b_ref)
+    f_row, c_row = row_sources(rows, f_ref, c_ref, a_ref, b_ref)
     odd = lax.rem(lax.axis_index("gy"), 2) == 1
     sub = iota(f_ref.shape[1:], 0)
     low_half = sub < DEEP_C
-
-    def put(t, first, last):
+    two_beyond, three_beyond = {-1: -2, rows: rows + 1}, {0: -3, rows - 1: rows + 2}
+    for t in range(rows + 2):
+        row = t - 1
+        f, c = turn(f_row(row), DEEP_C, 0), c_row(row)
+        first, last = jnp.where(low_half, c, f), jnp.where(low_half, f, c)
+        if row in two_beyond:
+            f, c = f_row(two_beyond[row]), c_row(two_beyond[row])
+            first = jnp.where(sub >= 6, turn(c, 6, 0), jnp.where(sub == 3, turn(f, 3, 0), first))
+            last = jnp.where(sub <= 1, turn(c, -6, 0), jnp.where(sub == 4, turn(f, -3, 0), last))
+        if row in three_beyond:
+            c = c_row(three_beyond[row])
+            first = jnp.where(sub == 7, turn(c, 7, 0), first)
+            last = jnp.where(sub == 0, turn(c, -7, 0), last)
         z_ref[t] = jnp.where(odd, last, first)
         k_ref[t] = jnp.where(odd, first, last)
-
-    for t in range(rows + 2):
-        f, c = turn(f_row(t - 1), DEEP_C, 0), c_row(t - 1)
-        put(t, jnp.where(low_half, c, f), jnp.where(low_half, f, c))
-
-    def corners(sub, way):
-        near, near_f, far = c_row(-2), f_row(-2), c_row(-3)
-        out = jnp.where(sub < 2, near, jnp.where(sub == 2, turn(near_f, 2 * way, 0), turn(far, 3 * way, 0)))
-        near, near_f, far = c_row(rows + 1), f_row(rows + 1), c_row(rows + 2)
-        out = jnp.where(sub < 4, out, jnp.where(sub < 6, turn(near, 4 * way, 0), turn(near_f, 6 * way, 0)))
-        return jnp.where(sub < 7, out, turn(far, 7 * way, 0))
-
-    put(rows + 2, corners(sub, 1), corners(SUB - 1 - sub, -1))
 
 
 def line_up(*refs):
@@ -174,12 +181,13 @@
     cx_ref, v_ref, diag_ref,
 ):
     rows, cols, depth = f_ref.shape
-    f_row, c_row = row_sources(along_x, rows, f_ref, c_ref, a_ref, b_ref)
+    f_row, c_row = row_sources(rows, f_ref, c_ref, a_ref, b_ref)
     gx, gy = lax.axis_index("gx"), lax.axis_index("gy")
     odd = lax.rem(gy, 2) == 1
-    has_left = (gy > 0).astype(F32)
-    has_right = (gy < along_y - 1).astype(F32)
     low_half = iota((cols, depth), 0) < DEEP_C
+    half_before = 0.5 * (gx > 0).astype(F32)
+    half_after = 0.5 * (gx < along_x - 1).astype(F32)
+    half_beside = jnp.where(low_half, 0.5 * (gy < along_y - 1).astype(F32), 0.5 * (gy > 0).astype(F32))
     wide = (cols + 2 * DEEP_C, depth)
     lane = iota(wide, 1)
     col = iota(wide, 0)
@@ -187,28 +195,28 @@
     inv_mid, ((keep, push),) = chebyshev(SMOOTH_LOW, SMOOTH_HIGH, SMOOTH)
 
     def sides(t):
-        left = jnp.where(odd, k_ref[t], z_ref[t]) * has_left
-        return left, jnp.where(odd, z_ref[t], k_ref[t]) * has_right
-
-    corner_tiles = sides(rows + 2)
+        return jnp.where(odd, k_ref[t], z_ref[t]), jnp.where(odd, z_ref[t], k_ref[t])
+
+    c_places = {-2: (0, 6), rows + 1: (rows + 1, 6), -3: (1, 7), rows + 2: (rows, 7)}
+    f_places = {-2: (0, 3), rows + 1: (rows + 1, 3)}
     for t in range(rows + 2 * DEEP_C):
         row = t - DEEP_C
-        cx_ref[t, 0:cols] = 0.5 * c_row(row)
+        half = half_before if row < 0 else 0.5 if row < rows else half_after
+        beside_row = half_beside if 0 <= row < rows else half_beside * (2.0 * half)
+        cx_ref[t, 0:cols] = half * c_row(row)
         s = row + DEEP_F
         if -1 <= row <= rows:
             left, right = sides(row + 1)
-            cx_ref[t, cols:] = 0.5 * jnp.where(low_half, right, left)
+            cx_ref[t, cols:] = beside_row * jnp.where(low_half, right, left)
             f = turn(jnp.where(low_half, left, right), DEEP_C, 0)
         else:
-            left, right = corner_tiles
-            c_turn = {-2: 0, -3: 3, rows + 1: 4, rows + 2: 7}.get(row)
-            f_turn = {-2: 2, rows + 1: 6}.get(row)
             c = f = jnp.zeros((cols, depth), F32)
-            if c_turn is not None:
-                c = jnp.where(low_half, turn(right, -c_turn, 0), turn(left, c_turn, 0))
-            if f_turn is not None:
-                f = jnp.where(low_half, turn(right, -f_turn, 0), turn(left, f_turn, 0))
-            cx_ref[t, cols:] = 0.5 * c
+            if row in c_places:
+                left, right = sides(c_places[row][0])
+                c = jnp.where(low_half, turn(right, -c_places[row][1], 0), turn(left, c_places[row][1], 0))
+            if row in f_places:
+                f = jnp.where(low_half, turn(right, -f_places[row][1], 0), turn(left, f_places[row][1], 0))
+            cx_ref[t, cols:] = beside_row * c
         if 0 <= s < rows + 2 * DEEP_F:
             fx_ref[s, 0:cols] = f_row(row)
             fx_ref[s, cols:] = f
@@ -256,7 +264,7 @@
     summed += [c_ref[2 * i] + c_ref[2 * i + 1] for i in range(half_rows)]
     summed = jnp.concatenate(summed, axis=0)
     pairs = (depth, depth // 2)
-    thin = exact_dot(summed, (iota(pairs, 0) // 2 == iota(pairs, 1)).astype(F32))
+    thin = exact_dot(summed, (iota(pairs, 0) // 2 == iota(pairs, 1)).astype(F32).astype(jnp.bfloat16))
     choice = (SUB * half_rows, summed.shape[0])
     line, source = iota(choice, 0), iota(choice, 1)
     block, place = line // SUB, line % SUB
@@ -268,7 +276,7 @@
     from_f = (source == f_from) | (source == f_from + 1)
     from_c = (source == c_from) | (source == c_from + 1)
     picker = jnp.where(f_half, jnp.where(from_f, 0.5, 0.0), jnp.where(from_c, 0.0625, 0.0))
-    tile = exact_dot(picker, thin).reshape(half_rows, SUB, depth // 2)
+    tile = exact_dot(picker.astype(jnp.bfloat16), thin).reshape(half_rows, SUB, depth // 2)
 
     send_ref[...] = tile
 
@@ -524,7 +532,7 @@
     home = to_cell // 2
     near_cell = jnp.where(to_cell % 2 == 0, home - 1, home + 1)
     weights = jnp.where(from_cell == home, 0.75, 0.0) + jnp.where(from_cell == near_cell, 0.25, 0.0)
-    carried = exact_dot(yy_ref[...], weights).reshape(span - 4, wide[0], depth)
+    carried = exact_dot(yy_ref[...], weights.astype(jnp.bfloat16)).reshape(span - 4, wide[0], depth)
     col_inside = inside_cols(iota(wide, 0), cols, along_y)
     for s in range(1, rows + 2 * DEEP_F - 1):
         row = s - DEEP_F
@@ -602,8 +610,8 @@
 
     tall = rows + 2 * DEEP_F
     z, k = call(
-        functools.partial(pack_cols, along_x),
-        [(rows + 3, cols, depth)] * 2,
+        pack_cols,
+        [(rows + 2, cols, depth)] * 2,
         [],
         (right_side, coefficient, a, b),
         small,

time: 30.7 us -> 30.5 us (level)
  no operation moved by 1% of the time
where the time goes in v8:
time: 30.5 us; the launch traced here: 30.3 us
  starting transfers between devices  15.5 us (51%)
  waiting for transfers between devices  10.5 us (34%)
  Pallas kernels  3.5 us (11%)
  local copies, waits for them, and re-layouts  0.85 us (3%)
    ppermute x1, starting transfers between devices, body(): a = lax.ppermute(a, 'gx', pairs_from(0, along_x))  3.98 us
    ppermute x3, starting transfers between devices, body(): lax.ppermute(line, ('gx', 'gy'), at_distance(along_x, along_y, 'gx', dist...  3.55 us
    pallas_call x4, Pallas kernels, call(): pl.pallas_call(kernel, out_shape=[jax.ShapeDtypeStruct(s, F32) for s in o...  3.5 us
    ppermute x3, starting transfers between devices, body(): lax.ppermute(send, ('gx', 'gy'), at_distance(along_x, along_y, 'gy', dist...  3.39 us
    ppermute x1, waiting for transfers between devices, body(): a = lax.ppermute(a, 'gx', pairs_from(0, along_x))  2.86 us
    ppermute x1, waiting for transfers between devices, body(): z = lax.ppermute(z, ('gx', 'gy'), swaps(along_x, along_y, 'gy', 1))  2.75 us
    ppermute x4, starting transfers between devices, body(): other = [lax.ppermute(line, 'gy', pairs_from(0, along_y)) for line in own]  2.29 us
    ppermute x3, waiting for transfers between devices, body(): lax.ppermute(send, ('gx', 'gy'), at_distance(along_x, along_y, 'gy', dist...  1.96 us
  transfers between devices with their start and end apart: 14, of which 8 were waited for; matrix products, arithmetic and copies ran while one was open for 0% of the time, Pallas kernels for 0%

profile of v8, /device:TPU:0, one launch (start us, length us, event | category | flops | bytes accessed | tf_op | source)
XLA Modules:
  0.0 30.3 jit_solution(17238169139756049911)
XLA Ops:
  0.0 0.8 %fusion.2 = (f32[3,8,256]{2,1,0:T(8,128)S(1)}, f32[3,8,256]{2,1,0:T(8,128)S(1)}) fusion(f32[8,8,256]{2,1,0:T(8,128)} %f_ref.3), kind=kLoop, calls=%fused_computation.4 | loop fusion | bytes 98304 | tf_op jit(solution)/shard_map/slice | solution.py:605
  0.9 0.5 %collective-permute-start.1 = (f32[7,8,256]{2,1,0:T(8,128)S(1)}, f32[7,8,256]{2,1,0:T(8,128)S(1)}, u32[]{:S(2)}, u32[]{:S(2)}) collective-permute-start(f32[7,8,256]{2,1,0:T(8,128)S(1)} %get-tuple-element.23), channel_id=1, source_target_pairs={{0,1},{1,0},{2,3},{3,2},{4,5},{5,4},{6,7},{7,6},{8,16},{9,17},{10,... | collective-permute-start | bytes 172040 | tf_op jit(solution)/shard_map/ppermute | solution.py:609
  1.4 4.0 %collective-permute-start = (f32[7,8,256]{2,1,0:T(8,128)S(1)}, f32[7,8,256]{2,1,0:T(8,128)S(1)}, u32[]{:S(2)}, u32[]{:S(2)}) collective-permute-start(f32[7,8,256]{2,1,0:T(8,128)S(1)} %get-tuple-element.24), channel_id=1, source_target_pairs={{0,8},{8,0},{16,24},{24,16},{1,9},{9,1},{17,25},{25,17},{2,10},{10... | collective-permute-start | bytes 172040 | tf_op jit(solution)/shard_map/ppermute | solution.py:608
  5.4 2.9 %collective-permute-done.a_ref = f32[7,8,256]{2,1,0:T(8,128)S(1)} collective-permute-done((f32[7,8,256]{2,1,0:T(8,128)S(1)}, f32[7,8,256]{2,1,0:T(8,128)S(1)}, u32[]{:S(2)}, u32[]{:S(2)}) %collective-permute-start) | collective-permute-done | bytes 57376 | tf_op jit(solution)/shard_map/ppermute | solution.py:608
  8.3 1.4 %collective-permute-start.2 = (f32[10,8,256]{2,1,0:T(8,128)S(1)}, f32[10,8,256]{2,1,0:T(8,128)S(1)}, u32[]{:S(2)}, u32[]{:S(2)}) collective-permute-start(f32[10,8,256]{2,1,0:T(8,128)S(1)} %get-tuple-element.14), channel_id=1, source_target_pairs={{0,8},{1,2},{2,1},{3,4},{4,3},{5,6},{6,5},{7,15},{8,0},{9,10},{10,... | collective-permute-start | bytes 245768 | tf_op jit(solution)/shard_map/ppermute | solution.py:620
  9.6 0.4 %collective-permute-start.3 = (f32[10,8,256]{2,1,0:T(8,128)S(1)}, f32[10,8,256]{2,1,0:T(8,128)S(1)}, u32[]{:S(2)}, u32[]{:S(2)}) collective-permute-start(f32[10,8,256]{2,1,0:T(8,128)S(1)} %get-tuple-element.15), channel_id=1, source_target_pairs={{0,1},{1,0},{2,3},{3,2},{4,5},{5,4},{6,7},{7,6},{8,9},{9,8},{10,11... | collective-permute-start | bytes 245768 | tf_op jit(solution)/shard_map/ppermute | solution.py:619
  10.0 2.7 %collective-permute-done.2.z_ref = f32[10,8,256]{2,1,0:T(8,128)S(1)} collective-permute-done((f32[10,8,256]{2,1,0:T(8,128)S(1)}, f32[10,8,256]{2,1,0:T(8,128)S(1)}, u32[]{:S(2)}, u32[]{:S(2)}) %collective-permute-start.2) | collective-permute-done | bytes 81952 | tf_op jit(solution)/shard_map/ppermute | solution.py:620
  12.8 0.7 %shard_map.29 = (f32[4,8,128]{2,1,0:T(8,128)S(1)}, f32[12,16,256]{2,1,0:T(8,128)S(1)}, f32[14,16,256]{2,1,0:T(8,128)S(1)}, f32[15,16,256]{2,1,0:T(8,128)S(1)}, f...) custom-call(f32[8,8,256]{2,1,0:T(8,128)S(1)} %copy-done.1, ...), custom_call_target="tpu_custom_call" | custom-call | tf_op jit(solution)/shard_map/pallas_call | solution.py:95
  13.5 0.7 %collective-permute-start.6 = (f32[4,8,128]{2,1,0:T(8,128)S(1)}, f32[4,8,128]{2,1,0:T(8,128)S(1)}, u32[]{:S(2)}, u32[]{:S(2)}) collective-permute-start(f32[4,8,128]{2,1,0:T(8,128)S(1)} %get-tuple-element.16.refs_0_), channel_id=1, source_target_pairs={{0,7},{1,6},{2,5},{3,4},{4,3},{5,2},{6,1},{7,0},{8,15},{9,14},{10,... | collective-permute-start | bytes 49160 | tf_op jit(solution)/shard_map/ppermute | solution.py:634
  14.2 1.5 %collective-permute-start.5 = (f32[4,8,128]{2,1,0:T(8,128)S(1)}, f32[4,8,128]{2,1,0:T(8,128)S(1)}, u32[]{:S(2)}, u32[]{:S(2)}) collective-permute-start(f32[4,8,128]{2,1,0:T(8,128)S(1)} %get-tuple-element.16.refs_0_), channel_id=1, source_target_pairs={{0,5},{1,4},{2,7},{3,6},{4,1},{5,0},{6,3},{7,2},{8,13},{9,12},{10,... | collective-permute-start | bytes 49160 | tf_op jit(solution)/shard_map/ppermute | solution.py:634
  15.7 1.2 %collective-permute-start.4 = (f32[4,8,128]{2,1,0:T(8,128)S(1)}, f32[4,8,128]{2,1,0:T(8,128)S(1)}, u32[]{:S(2)}, u32[]{:S(2)}) collective-permute-start(f32[4,8,128]{2,1,0:T(8,128)S(1)} %get-tuple-element.16.refs_0_), channel_id=1, source_target_pairs={{0,3},{1,2},{2,1},{3,0},{4,7},{5,6},{6,5},{7,4},{8,11},{9,10},{10,... | collective-permute-start | bytes 49160 | tf_op jit(solution)/shard_map/ppermute | solution.py:634
  16.9 1.7 %collective-permute-done.6.refs_3_ = f32[4,8,128]{2,1,0:T(8,128)S(1)} collective-permute-done((f32[4,8,128]{2,1,0:T(8,128)S(1)}, f32[4,8,128]{2,1,0:T(8,128)S(1)}, u32[]{:S(2)}, u32[]{:S(2)}) %collective-permute-start.6) | collective-permute-done | bytes 16416 | tf_op jit(solution)/shard_map/ppermute | solution.py:634
  18.7 0.2 collective-permute-done.4.refs_1_
  18.9 1.6 %collective-permute-start.9 = (f32[16,8,128]{2,1,0:T(8,128)S(1)}, f32[16,8,128]{2,1,0:T(8,128)S(1)}, u32[]{:S(2)}, u32[]{:S(2)}) collective-permute-start(f32[16,8,128]{2,1,0:T(8,128)S(1)} %shard_map.30.refs_0_), channel_id=1, source_target_pairs={{0,24},{1,25},{2,26},{3,27},{4,28},{5,29},{6,30},{7,31},{8,16},{9,... | collective-permute-start | bytes 196616 | tf_op jit(solution)/shard_map/ppermute | solution.py:640
  20.5 1.2 %collective-permute-start.8 = (f32[16,8,128]{2,1,0:T(8,128)S(1)}, f32[16,8,128]{2,1,0:T(8,128)S(1)}, u32[]{:S(2)}, u32[]{:S(2)}) collective-permute-start(f32[16,8,128]{2,1,0:T(8,128)S(1)} %shard_map.30.refs_0_), channel_id=1, source_target_pairs={{0,16},{1,17},{2,18},{3,19},{4,20},{5,21},{6,22},{7,23},{8,24},{9,... | collective-permute-start | bytes 196616 | tf_op jit(solution)/shard_map/ppermute | solution.py:640
  21.7 0.7 %collective-permute-start.7 = (f32[16,8,128]{2,1,0:T(8,128)S(1)}, f32[16,8,128]{2,1,0:T(8,128)S(1)}, u32[]{:S(2)}, u32[]{:S(2)}) collective-permute-start(f32[16,8,128]{2,1,0:T(8,128)S(1)} %shard_map.30.refs_0_), channel_id=1, source_target_pairs={{0,8},{1,9},{2,10},{3,11},{4,12},{5,13},{6,14},{7,15},{8,0},{9,1},... | collective-permute-start | bytes 196616 | tf_op jit(solution)/shard_map/ppermute | solution.py:640
  22.4 1.0 %collective-permute-start.10 = (f32[16,8,128]{2,1,0:T(8,128)S(1)}, f32[16,8,128]{2,1,0:T(8,128)S(1)}, u32[]{:S(2)}, u32[]{:S(2)}) collective-permute-start(f32[16,8,128]{2,1,0:T(8,128)S(1)} %shard_map.30.refs_0_), channel_id=1, source_target_pairs={{0,1},{1,0},{2,3},{3,2},{4,5},{5,4},{6,7},{7,6},{8,9},{9,8},{10,11... | collective-permute-start | bytes 196616 | tf_op jit(solution)/shard_map/ppermute | solution.py:643
  23.4 0.7 %collective-permute-done.9.refs_3_ = f32[16,8,128]{2,1,0:T(8,128)S(1)} collective-permute-done((f32[16,8,128]{2,1,0:T(8,128)S(1)}, f32[16,8,128]{2,1,0:T(8,128)S(1)}, u32[]{:S(2)}, u32[]{:S(2)}) %collective-permute-start.9) | collective-permute-done | bytes 65568 | tf_op jit(solution)/shard_map/ppermute | solution.py:640
  24.1 0.8 %collective-permute-start.13 = (f32[16,8,128]{2,1,0:T(8,128)S(1)}, f32[16,8,128]{2,1,0:T(8,128)S(1)}, u32[]{:S(2)}, u32[]{:S(2)}) collective-permute-start(f32[16,8,128]{2,1,0:T(8,128)S(1)} %collective-permute-done.9.refs_3_), channel_id=1, source_target_pairs={{0,1},{1,0},{2,3},{3,2},{4,5},{5,4},{6,7},{7,6},{8,9},{9,8},{10,11... | collective-permute-start | bytes 196616 | tf_op jit(solution)/shard_map/ppermute | solution.py:643
  24.9 1.1 %collective-permute-done.8.refs_2_ = f32[16,8,128]{2,1,0:T(8,128)S(1)} collective-permute-done((f32[16,8,128]{2,1,0:T(8,128)S(1)}, f32[16,8,128]{2,1,0:T(8,128)S(1)}, u32[]{:S(2)}, u32[]{:S(2)}) %collective-permute-start.8) | collective-permute-done | bytes 65568 | tf_op jit(solution)/shard_map/ppermute | solution.py:640
  26.0 0.3 %collective-permute-start.12 = (f32[16,8,128]{2,1,0:T(8,128)S(1)}, f32[16,8,128]{2,1,0:T(8,128)S(1)}, u32[]{:S(2)}, u32[]{:S(2)}) collective-permute-start(f32[16,8,128]{2,1,0:T(8,128)S(1)} %collective-permute-done.8.refs_2_), channel_id=1, source_target_pairs={{0,1},{1,0},{2,3},{3,2},{4,5},{5,4},{6,7},{7,6},{8,9},{9,8},{10,11... | collective-permute-start | bytes 196616 | tf_op jit(solution)/shard_map/ppermute | solution.py:643
  26.5 0.7 %collective-permute-done.12.refs_6_ = f32[16,8,128]{2,1,0:T(8,128)S(1)} collective-permute-done((f32[16,8,128]{2,1,0:T(8,128)S(1)}, f32[16,8,128]{2,1,0:T(8,128)S(1)}, u32[]{:S(2)}, u32[]{:S(2)}) %collective-permute-start.12) | collective-permute-done | bytes 65568 | tf_op jit(solution)/shard_map/ppermute | solution.py:643
  27.2 0.4 %collective-permute-done.11.refs_5_ = f32[16,8,128]{2,1,0:T(8,128)S(1)} collective-permute-done((f32[16,8,128]{2,1,0:T(8,128)S(1)}, f32[16,8,128]{2,1,0:T(8,128)S(1)}, u32[]{:S(2)}, u32[]{:S(2)}) %collective-permute-start.11) | collective-permute-done | bytes 65568 | tf_op jit(solution)/shard_map/ppermute | solution.py:643
  27.6 2.7 %shard_map.31 = f32[8,8,256]{2,1,0:T(8,128)} custom-call(f32[16,8,128]{2,1,0:T(8,128)S(1)} %shard_map.30.refs_0_, f32[16,8,128]{2,1,0:T(8,128)S(1)} %collective-permute-done.7.refs_1_, f32[16,8,128]{2,1,0:T(8,128)S(1)} %collective-permute-done.8.refs_2_, f32[16,8,128]{2,1,0:T(8,128)S(1)} %collective-permute-done.9.refs_3_, ...), custom_call_target="tpu_custom_call" | custom-call | tf_op jit(solution)/shard_map/pallas_call | solution.py:95
  (15 shorter events, 0.4 us)
Async XLA Ops:
  0.0 0.8 %copy-start = (f32[8,8,256]{2,1,0:T(8,128)S(1)}, f32[8,8,256]{2,1,0:T(8,128)}, u32[]{:S(2)}) copy-start(f32[8,8,256]{2,1,0:T(8,128)} %c_ref.3) | copy-start | bytes 196612
  0.8 7.4 %copy-start.1 = (f32[8,8,256]{2,1,0:T(8,128)S(1)}, f32[8,8,256]{2,1,0:T(8,128)}, u32[]{:S(2)}) copy-start(f32[8,8,256]{2,1,0:T(8,128)} %f_ref.3) | copy-start | bytes 196612
  0.9 4.5 %collective-permute-start.1 = (f32[7,8,256]{2,1,0:T(8,128)S(1)}, f32[7,8,256]{2,1,0:T(8,128)S(1)}, u32[]{:S(2)}, u32[]{:S(2)}) collective-permute-start(f32[7,8,256]{2,1,0:T(8,128)S(1)} %get-tuple-element.23), channel_id=1, source_target_pairs={{0,1},{1,0},{2,3},{3,2},{4,5},{5,4},{6,7},{7,6},{8,16},{9,17},{10,... | collective-permute-start | bytes 172040 | tf_op jit(solution)/shard_map/ppermute | solution.py:609
  1.4 6.8 %collective-permute-start = (f32[7,8,256]{2,1,0:T(8,128)S(1)}, f32[7,8,256]{2,1,0:T(8,128)S(1)}, u32[]{:S(2)}, u32[]{:S(2)}) collective-permute-start(f32[7,8,256]{2,1,0:T(8,128)S(1)} %get-tuple-element.24), channel_id=1, source_target_pairs={{0,8},{8,0},{16,24},{24,16},{1,9},{9,1},{17,25},{25,17},{2,10},{10... | collective-permute-start | bytes 172040 | tf_op jit(solution)/shard_map/ppermute | solution.py:608
  8.3 4.5 %collective-permute-start.2 = (f32[10,8,256]{2,1,0:T(8,128)S(1)}, f32[10,8,256]{2,1,0:T(8,128)S(1)}, u32[]{:S(2)}, u32[]{:S(2)}) collective-permute-start(f32[10,8,256]{2,1,0:T(8,128)S(1)} %get-tuple-element.14), channel_id=1, source_target_pairs={{0,8},{1,2},{2,1},{3,4},{4,3},{5,6},{6,5},{7,15},{8,0},{9,10},{10,... | collective-permute-start | bytes 245768 | tf_op jit(solution)/shard_map/ppermute | solution.py:620
  9.6 3.1 %collective-permute-start.3 = (f32[10,8,256]{2,1,0:T(8,128)S(1)}, f32[10,8,256]{2,1,0:T(8,128)S(1)}, u32[]{:S(2)}, u32[]{:S(2)}) collective-permute-start(f32[10,8,256]{2,1,0:T(8,128)S(1)} %get-tuple-element.15), channel_id=1, source_target_pairs={{0,1},{1,0},{2,3},{3,2},{4,5},{5,4},{6,7},{7,6},{8,9},{9,8},{10,11... | collective-permute-start | bytes 245768 | tf_op jit(solution)/shard_map/ppermute | solution.py:619
  13.5 5.1 %collective-permute-start.6 = (f32[4,8,128]{2,1,0:T(8,128)S(1)}, f32[4,8,128]{2,1,0:T(8,128)S(1)}, u32[]{:S(2)}, u32[]{:S(2)}) collective-permute-start(f32[4,8,128]{2,1,0:T(8,128)S(1)} %get-tuple-element.16.refs_0_), channel_id=1, source_target_pairs={{0,7},{1,6},{2,5},{3,4},{4,3},{5,2},{6,1},{7,0},{8,15},{9,14},{10,... | collective-permute-start | bytes 49160 | tf_op jit(solution)/shard_map/ppermute | solution.py:634
  14.2 4.4 %collective-permute-start.5 = (f32[4,8,128]{2,1,0:T(8,128)S(1)}, f32[4,8,128]{2,1,0:T(8,128)S(1)}, u32[]{:S(2)}, u32[]{:S(2)}) collective-permute-start(f32[4,8,128]{2,1,0:T(8,128)S(1)} %get-tuple-element.16.refs_0_), channel_id=1, source_target_pairs={{0,5},{1,4},{2,7},{3,6},{4,1},{5,0},{6,3},{7,2},{8,13},{9,12},{10,... | collective-permute-start | bytes 49160 | tf_op jit(solution)/shard_map/ppermute | solution.py:634
  15.7 3.2 %collective-permute-start.4 = (f32[4,8,128]{2,1,0:T(8,128)S(1)}, f32[4,8,128]{2,1,0:T(8,128)S(1)}, u32[]{:S(2)}, u32[]{:S(2)}) collective-permute-start(f32[4,8,128]{2,1,0:T(8,128)S(1)} %get-tuple-element.16.refs_0_), channel_id=1, source_target_pairs={{0,3},{1,2},{2,1},{3,0},{4,7},{5,6},{6,5},{7,4},{8,11},{9,10},{10,... | collective-permute-start | bytes 49160 | tf_op jit(solution)/shard_map/ppermute | solution.py:634
  18.9 5.2 %collective-permute-start.9 = (f32[16,8,128]{2,1,0:T(8,128)S(1)}, f32[16,8,128]{2,1,0:T(8,128)S(1)}, u32[]{:S(2)}, u32[]{:S(2)}) collective-permute-start(f32[16,8,128]{2,1,0:T(8,128)S(1)} %shard_map.30.refs_0_), channel_id=1, source_target_pairs={{0,24},{1,25},{2,26},{3,27},{4,28},{5,29},{6,30},{7,31},{8,16},{9,... | collective-permute-start | bytes 196616 | tf_op jit(solution)/shard_map/ppermute | solution.py:640
  20.5 5.5 %collective-permute-start.8 = (f32[16,8,128]{2,1,0:T(8,128)S(1)}, f32[16,8,128]{2,1,0:T(8,128)S(1)}, u32[]{:S(2)}, u32[]{:S(2)}) collective-permute-start(f32[16,8,128]{2,1,0:T(8,128)S(1)} %shard_map.30.refs_0_), channel_id=1, source_target_pairs={{0,16},{1,17},{2,18},{3,19},{4,20},{5,21},{6,22},{7,23},{8,24},{9,... | collective-permute-start | bytes 196616 | tf_op jit(solution)/shard_map/ppermute | solution.py:640
  21.7 4.6 %collective-permute-start.7 = (f32[16,8,128]{2,1,0:T(8,128)S(1)}, f32[16,8,128]{2,1,0:T(8,128)S(1)}, u32[]{:S(2)}, u32[]{:S(2)}) collective-permute-start(f32[16,8,128]{2,1,0:T(8,128)S(1)} %shard_map.30.refs_0_), channel_id=1, source_target_pairs={{0,8},{1,9},{2,10},{3,11},{4,12},{5,13},{6,14},{7,15},{8,0},{9,1},... | collective-permute-start | bytes 196616 | tf_op jit(solution)/shard_map/ppermute | solution.py:640
  22.4 4.1 %collective-permute-start.10 = (f32[16,8,128]{2,1,0:T(8,128)S(1)}, f32[16,8,128]{2,1,0:T(8,128)S(1)}, u32[]{:S(2)}, u32[]{:S(2)}) collective-permute-start(f32[16,8,128]{2,1,0:T(8,128)S(1)} %shard_map.30.refs_0_), channel_id=1, source_target_pairs={{0,1},{1,0},{2,3},{3,2},{4,5},{5,4},{6,7},{7,6},{8,9},{9,8},{10,11... | collective-permute-start | bytes 196616 | tf_op jit(solution)/shard_map/ppermute | solution.py:643
  24.1 2.4 %collective-permute-start.13 = (f32[16,8,128]{2,1,0:T(8,128)S(1)}, f32[16,8,128]{2,1,0:T(8,128)S(1)}, u32[]{:S(2)}, u32[]{:S(2)}) collective-permute-start(f32[16,8,128]{2,1,0:T(8,128)S(1)} %collective-permute-done.9.refs_3_), channel_id=1, source_target_pairs={{0,1},{1,0},{2,3},{3,2},{4,5},{5,4},{6,7},{7,6},{8,9},{9,8},{10,11... | collective-permute-start | bytes 196616 | tf_op jit(solution)/shard_map/ppermute | solution.py:643
  26.0 1.3 %collective-permute-start.12 = (f32[16,8,128]{2,1,0:T(8,128)S(1)}, f32[16,8,128]{2,1,0:T(8,128)S(1)}, u32[]{:S(2)}, u32[]{:S(2)}) collective-permute-start(f32[16,8,128]{2,1,0:T(8,128)S(1)} %collective-permute-done.8.refs_2_), channel_id=1, source_target_pairs={{0,1},{1,0},{2,3},{3,2},{4,5},{5,4},{6,7},{7,6},{8,9},{9,8},{10,11... | collective-permute-start | bytes 196616 | tf_op jit(solution)/shard_map/ppermute | solution.py:643
  26.4 1.3 %collective-permute-start.11 = (f32[16,8,128]{2,1,0:T(8,128)S(1)}, f32[16,8,128]{2,1,0:T(8,128)S(1)}, u32[]{:S(2)}, u32[]{:S(2)}) collective-permute-start(f32[16,8,128]{2,1,0:T(8,128)S(1)} %collective-permute-done.7.refs_1_), channel_id=1, source_target_pairs={{0,1},{1,0},{2,3},{3,2},{4,5},{5,4},{6,7},{7,6},{8,9},{9,8},{10,11... | collective-permute-start | bytes 196616 | tf_op jit(solution)/shard_map/ppermute | solution.py:643

commit v9 on v8

--- a/solution.py
+++ b/solution.py
@@ -229,8 +229,10 @@
         after = half + turn(half, -1, 0)
         deeper = jnp.where(lane == depth - 1, 0.0, half + turn(half, -1, 1))
         wx_ref[s + 1] = above
-        wy_ref[s] = after
-        wz_ref[s] = deeper
+        inner = 0 < s < tall - 1
+        if inner:
+            wy_ref[s] = after
+            wz_ref[s] = deeper
         diag = wx_ref[s] + above + after + turn(after, 1, 0) + deeper + turn(deeper, 1, 1)
         diag = diag + jnp.where((lane == 0) | (lane == depth - 1), half, 0.0)
         inside = col_inside
@@ -241,8 +243,10 @@
         inv = jnp.where(inside, 1.0 / diag, 0.0)
         if DEEP_F <= s < DEEP_F + rows:
             diag_ref[s - DEEP_F] = diag[:cols]
-        inv_ref[s] = inv
-        v_ref[s] = fx_ref[s] * inv * inv_mid
+        if inner:
+            inv_ref[s] = inv
+        span = wide[0] if inner else cols
+        v_ref[s, :span] = fx_ref[s, :span] * inv[:span] * inv_mid
 
     def pulled(x_ref, shift, s, span):
         at = s - shift
@@ -253,8 +257,9 @@
         return fx_ref[s, :span] + total
 
     for s in range(1, tall - 1):
-        total = pulled(v_ref, 0, s, wide[0])
-        u_ref[s - 1] = (1.0 + keep - push) * v_ref[s] + push * (inv_ref[s] * total)
+        span = wide[0] if 1 < s < tall - 2 else cols
+        total = pulled(v_ref, 0, s, span)
+        u_ref[s - 1, :span] = (1.0 + keep - push) * v_ref[s, :span] + push * (inv_ref[s, :span] * total)
 
     def residual(s):
         return pulled(u_ref, 1, s, cols) - diag_ref[s - DEEP_F] * u_ref[s - 1, :cols]
@@ -543,8 +548,9 @@
             inside = inside & (gx > 0)
         if row >= rows:
             inside = inside & (gx < along_x - 1)
-        total = u0_ref[s - 1] + (0.75 * carried[near] + 0.25 * carried[far])
-        v0_ref[s] = jnp.where(inside, total, 0.0)
+        span = wide[0] if 1 < s < rows + 2 * DEEP_F - 2 else cols
+        total = u0_ref[s - 1, :span] + (0.75 * carried[near][:span] + 0.25 * carried[far][:span])
+        v0_ref[s, :span] = jnp.where(inside[:span], total, 0.0)
 
     def pulled0(x_ref, s, span):
         return fx_ref[s, :span] + beside(
@@ -553,10 +559,11 @@
         )
 
     for s in range(2, rows + 2 * DEEP_F - 2):
-        v = v0_ref[s]
-        d = (inv0_ref[s] * pulled0(v0_ref, s, wide[0]) - v) * inv_mid
+        span = wide[0] if 2 < s < rows + 2 * DEEP_F - 3 else cols
+        v = v0_ref[s, :span]
+        d = (inv0_ref[s, :span] * pulled0(v0_ref, s, span) - v) * inv_mid
         d0_ref[s] = d[:cols]
-        x0_ref[s] = v + d
+        x0_ref[s, :span] = v + d
     for i in range(rows):
         s = i + DEEP_F
         total = inv0_ref[s, :cols] * pulled0(x0_ref, s, cols)

time: 30.5 us -> 30.5 us (level)
  no operation moved by 1% of the time
where the time goes in v9:
time: 30.5 us; the launch traced here: 30.3 us
  starting transfers between devices  15.5 us (51%)
  waiting for transfers between devices  10.5 us (34%)
  Pallas kernels  3.48 us (11%)
  local copies, waits for them, and re-layouts  0.85 us (3%)
    ppermute x1, starting transfers between devices, body(): a = lax.ppermute(a, 'gx', pairs_from(0, along_x))  3.98 us
    ppermute x3, starting transfers between devices, body(): lax.ppermute(line, ('gx', 'gy'), at_distance(along_x, along_y, 'gx', dist...  3.55 us
    pallas_call x4, Pallas kernels, call(): pl.pallas_call(kernel, out_shape=[jax.ShapeDtypeStruct(s, F32) for s in o...  3.48 us
    ppermute x3, starting transfers between devices, body(): lax.ppermute(send, ('gx', 'gy'), at_distance(along_x, along_y, 'gy', dist...  3.4 us
    ppermute x1, waiting for transfers between devices, body(): a = lax.ppermute(a, 'gx', pairs_from(0, along_x))  2.86 us
    ppermute x1, waiting for transfers between devices, body(): z = lax.ppermute(z, ('gx', 'gy'), swaps(along_x, along_y, 'gy', 1))  2.75 us
    ppermute x4, starting transfers between devices, body(): other = [lax.ppermute(line, 'gy', pairs_from(0, along_y)) for line in own]  2.29 us
    ppermute x3, waiting for transfers between devices, body(): lax.ppermute(send, ('gx', 'gy'), at_distance(along_x, along_y, 'gy', dist...  1.96 us
  transfers between devices with their start and end apart: 14, of which 8 were waited for; matrix products, arithmetic and copies ran while one was open for 0% of the time, Pallas kernels for 0%

profile of v9, /device:TPU:0, one launch (start us, length us, event | category | flops | bytes accessed | tf_op | source)
XLA Modules:
  0.0 30.3 jit_solution(14956006272836455077)
XLA Ops:
  0.0 0.8 %fusion.2 = (f32[3,8,256]{2,1,0:T(8,128)S(1)}, f32[3,8,256]{2,1,0:T(8,128)S(1)}) fusion(f32[8,8,256]{2,1,0:T(8,128)} %f_ref.3), kind=kLoop, calls=%fused_computation.4 | loop fusion | bytes 98304 | tf_op jit(solution)/shard_map/slice | solution.py:612
  0.9 0.5 %collective-permute-start.1 = (f32[7,8,256]{2,1,0:T(8,128)S(1)}, f32[7,8,256]{2,1,0:T(8,128)S(1)}, u32[]{:S(2)}, u32[]{:S(2)}) collective-permute-start(f32[7,8,256]{2,1,0:T(8,128)S(1)} %get-tuple-element.23), channel_id=1, source_target_pairs={{0,1},{1,0},{2,3},{3,2},{4,5},{5,4},{6,7},{7,6},{8,16},{9,17},{10,... | collective-permute-start | bytes 172040 | tf_op jit(solution)/shard_map/ppermute | solution.py:616
  1.4 4.0 %collective-permute-start = (f32[7,8,256]{2,1,0:T(8,128)S(1)}, f32[7,8,256]{2,1,0:T(8,128)S(1)}, u32[]{:S(2)}, u32[]{:S(2)}) collective-permute-start(f32[7,8,256]{2,1,0:T(8,128)S(1)} %get-tuple-element.24), channel_id=1, source_target_pairs={{0,8},{8,0},{16,24},{24,16},{1,9},{9,1},{17,25},{25,17},{2,10},{10... | collective-permute-start | bytes 172040 | tf_op jit(solution)/shard_map/ppermute | solution.py:615
  5.4 2.9 %collective-permute-done.a_ref = f32[7,8,256]{2,1,0:T(8,128)S(1)} collective-permute-done((f32[7,8,256]{2,1,0:T(8,128)S(1)}, f32[7,8,256]{2,1,0:T(8,128)S(1)}, u32[]{:S(2)}, u32[]{:S(2)}) %collective-permute-start) | collective-permute-done | bytes 57376 | tf_op jit(solution)/shard_map/ppermute | solution.py:615
  8.3 1.4 %collective-permute-start.2 = (f32[10,8,256]{2,1,0:T(8,128)S(1)}, f32[10,8,256]{2,1,0:T(8,128)S(1)}, u32[]{:S(2)}, u32[]{:S(2)}) collective-permute-start(f32[10,8,256]{2,1,0:T(8,128)S(1)} %get-tuple-element.14), channel_id=1, source_target_pairs={{0,8},{1,2},{2,1},{3,4},{4,3},{5,6},{6,5},{7,15},{8,0},{9,10},{10,... | collective-permute-start | bytes 245768 | tf_op jit(solution)/shard_map/ppermute | solution.py:627
  9.6 0.4 %collective-permute-start.3 = (f32[10,8,256]{2,1,0:T(8,128)S(1)}, f32[10,8,256]{2,1,0:T(8,128)S(1)}, u32[]{:S(2)}, u32[]{:S(2)}) collective-permute-start(f32[10,8,256]{2,1,0:T(8,128)S(1)} %get-tuple-element.15), channel_id=1, source_target_pairs={{0,1},{1,0},{2,3},{3,2},{4,5},{5,4},{6,7},{7,6},{8,9},{9,8},{10,11... | collective-permute-start | bytes 245768 | tf_op jit(solution)/shard_map/ppermute | solution.py:626
  10.0 2.7 %collective-permute-done.2.z_ref = f32[10,8,256]{2,1,0:T(8,128)S(1)} collective-permute-done((f32[10,8,256]{2,1,0:T(8,128)S(1)}, f32[10,8,256]{2,1,0:T(8,128)S(1)}, u32[]{:S(2)}, u32[]{:S(2)}) %collective-permute-start.2) | collective-permute-done | bytes 81952 | tf_op jit(solution)/shard_map/ppermute | solution.py:627
  12.8 0.7 %shard_map.29 = (f32[4,8,128]{2,1,0:T(8,128)S(1)}, f32[12,16,256]{2,1,0:T(8,128)S(1)}, f32[14,16,256]{2,1,0:T(8,128)S(1)}, f32[15,16,256]{2,1,0:T(8,128)S(1)}, f...) custom-call(f32[8,8,256]{2,1,0:T(8,128)S(1)} %copy-done.1, ...), custom_call_target="tpu_custom_call" | custom-call | tf_op jit(solution)/shard_map/pallas_call | solution.py:95
  13.5 0.7 %collective-permute-start.6 = (f32[4,8,128]{2,1,0:T(8,128)S(1)}, f32[4,8,128]{2,1,0:T(8,128)S(1)}, u32[]{:S(2)}, u32[]{:S(2)}) collective-permute-start(f32[4,8,128]{2,1,0:T(8,128)S(1)} %get-tuple-element.16.refs_0_), channel_id=1, source_target_pairs={{0,7},{1,6},{2,5},{3,4},{4,3},{5,2},{6,1},{7,0},{8,15},{9,14},{10,... | collective-permute-start | bytes 49160 | tf_op jit(solution)/shard_map/ppermute | solution.py:641
  14.2 1.5 %collective-permute-start.5 = (f32[4,8,128]{2,1,0:T(8,128)S(1)}, f32[4,8,128]{2,1,0:T(8,128)S(1)}, u32[]{:S(2)}, u32[]{:S(2)}) collective-permute-start(f32[4,8,128]{2,1,0:T(8,128)S(1)} %get-tuple-element.16.refs_0_), channel_id=1, source_target_pairs={{0,5},{1,4},{2,7},{3,6},{4,1},{5,0},{6,3},{7,2},{8,13},{9,12},{10,... | collective-permute-start | bytes 49160 | tf_op jit(solution)/shard_map/ppermute | solution.py:641
  15.7 1.2 %collective-permute-start.4 = (f32[4,8,128]{2,1,0:T(8,128)S(1)}, f32[4,8,128]{2,1,0:T(8,128)S(1)}, u32[]{:S(2)}, u32[]{:S(2)}) collective-permute-start(f32[4,8,128]{2,1,0:T(8,128)S(1)} %get-tuple-element.16.refs_0_), channel_id=1, source_target_pairs={{0,3},{1,2},{2,1},{3,0},{4,7},{5,6},{6,5},{7,4},{8,11},{9,10},{10,... | collective-permute-start | bytes 49160 | tf_op jit(solution)/shard_map/ppermute | solution.py:641
  16.9 1.7 %collective-permute-done.6.refs_3_ = f32[4,8,128]{2,1,0:T(8,128)S(1)} collective-permute-done((f32[4,8,128]{2,1,0:T(8,128)S(1)}, f32[4,8,128]{2,1,0:T(8,128)S(1)}, u32[]{:S(2)}, u32[]{:S(2)}) %collective-permute-start.6) | collective-permute-done | bytes 16416 | tf_op jit(solution)/shard_map/ppermute | solution.py:641
  18.6 0.2 collective-permute-done.4.refs_1_
  18.9 1.6 %collective-permute-start.9 = (f32[16,8,128]{2,1,0:T(8,128)S(1)}, f32[16,8,128]{2,1,0:T(8,128)S(1)}, u32[]{:S(2)}, u32[]{:S(2)}) collective-permute-start(f32[16,8,128]{2,1,0:T(8,128)S(1)} %shard_map.30.refs_0_), channel_id=1, source_target_pairs={{0,24},{1,25},{2,26},{3,27},{4,28},{5,29},{6,30},{7,31},{8,16},{9,... | collective-permute-start | bytes 196616 | tf_op jit(solution)/shard_map/ppermute | solution.py:647
  20.5 1.2 %collective-permute-start.8 = (f32[16,8,128]{2,1,0:T(8,128)S(1)}, f32[16,8,128]{2,1,0:T(8,128)S(1)}, u32[]{:S(2)}, u32[]{:S(2)}) collective-permute-start(f32[16,8,128]{2,1,0:T(8,128)S(1)} %shard_map.30.refs_0_), channel_id=1, source_target_pairs={{0,16},{1,17},{2,18},{3,19},{4,20},{5,21},{6,22},{7,23},{8,24},{9,... | collective-permute-start | bytes 196616 | tf_op jit(solution)/shard_map/ppermute | solution.py:647
  21.7 0.7 %collective-permute-start.7 = (f32[16,8,128]{2,1,0:T(8,128)S(1)}, f32[16,8,128]{2,1,0:T(8,128)S(1)}, u32[]{:S(2)}, u32[]{:S(2)}) collective-permute-start(f32[16,8,128]{2,1,0:T(8,128)S(1)} %shard_map.30.refs_0_), channel_id=1, source_target_pairs={{0,8},{1,9},{2,10},{3,11},{4,12},{5,13},{6,14},{7,15},{8,0},{9,1},... | collective-permute-start | bytes 196616 | tf_op jit(solution)/shard_map/ppermute | solution.py:647
  22.4 1.0 %collective-permute-start.10 = (f32[16,8,128]{2,1,0:T(8,128)S(1)}, f32[16,8,128]{2,1,0:T(8,128)S(1)}, u32[]{:S(2)}, u32[]{:S(2)}) collective-permute-start(f32[16,8,128]{2,1,0:T(8,128)S(1)} %shard_map.30.refs_0_), channel_id=1, source_target_pairs={{0,1},{1,0},{2,3},{3,2},{4,5},{5,4},{6,7},{7,6},{8,9},{9,8},{10,11... | collective-permute-start | bytes 196616 | tf_op jit(solution)/shard_map/ppermute | solution.py:650
  23.4 0.7 %collective-permute-done.9.refs_3_ = f32[16,8,128]{2,1,0:T(8,128)S(1)} collective-permute-done((f32[16,8,128]{2,1,0:T(8,128)S(1)}, f32[16,8,128]{2,1,0:T(8,128)S(1)}, u32[]{:S(2)}, u32[]{:S(2)}) %collective-permute-start.9) | collective-permute-done | bytes 65568 | tf_op jit(solution)/shard_map/ppermute | solution.py:647
  24.1 0.8 %collective-permute-start.13 = (f32[16,8,128]{2,1,0:T(8,128)S(1)}, f32[16,8,128]{2,1,0:T(8,128)S(1)}, u32[]{:S(2)}, u32[]{:S(2)}) collective-permute-start(f32[16,8,128]{2,1,0:T(8,128)S(1)} %collective-permute-done.9.refs_3_), channel_id=1, source_target_pairs={{0,1},{1,0},{2,3},{3,2},{4,5},{5,4},{6,7},{7,6},{8,9},{9,8},{10,11... | collective-permute-start | bytes 196616 | tf_op jit(solution)/shard_map/ppermute | solution.py:650
  24.9 1.1 %collective-permute-done.8.refs_2_ = f32[16,8,128]{2,1,0:T(8,128)S(1)} collective-permute-done((f32[16,8,128]{2,1,0:T(8,128)S(1)}, f32[16,8,128]{2,1,0:T(8,128)S(1)}, u32[]{:S(2)}, u32[]{:S(2)}) %collective-permute-start.8) | collective-permute-done | bytes 65568 | tf_op jit(solution)/shard_map/ppermute | solution.py:647
  26.0 0.3 %collective-permute-start.12 = (f32[16,8,128]{2,1,0:T(8,128)S(1)}, f32[16,8,128]{2,1,0:T(8,128)S(1)}, u32[]{:S(2)}, u32[]{:S(2)}) collective-permute-start(f32[16,8,128]{2,1,0:T(8,128)S(1)} %collective-permute-done.8.refs_2_), channel_id=1, source_target_pairs={{0,1},{1,0},{2,3},{3,2},{4,5},{5,4},{6,7},{7,6},{8,9},{9,8},{10,11... | collective-permute-start | bytes 196616 | tf_op jit(solution)/shard_map/ppermute | solution.py:650
  26.5 0.7 %collective-permute-done.12.refs_6_ = f32[16,8,128]{2,1,0:T(8,128)S(1)} collective-permute-done((f32[16,8,128]{2,1,0:T(8,128)S(1)}, f32[16,8,128]{2,1,0:T(8,128)S(1)}, u32[]{:S(2)}, u32[]{:S(2)}) %collective-permute-start.12) | collective-permute-done | bytes 65568 | tf_op jit(solution)/shard_map/ppermute | solution.py:650
  27.2 0.4 %collective-permute-done.11.refs_5_ = f32[16,8,128]{2,1,0:T(8,128)S(1)} collective-permute-done((f32[16,8,128]{2,1,0:T(8,128)S(1)}, f32[16,8,128]{2,1,0:T(8,128)S(1)}, u32[]{:S(2)}, u32[]{:S(2)}) %collective-permute-start.11) | collective-permute-done | bytes 65568 | tf_op jit(solution)/shard_map/ppermute | solution.py:650
  27.6 2.7 %shard_map.31 = f32[8,8,256]{2,1,0:T(8,128)} custom-call(f32[16,8,128]{2,1,0:T(8,128)S(1)} %shard_map.30.refs_0_, f32[16,8,128]{2,1,0:T(8,128)S(1)} %collective-permute-done.7.refs_1_, f32[16,8,128]{2,1,0:T(8,128)S(1)} %collective-permute-done.8.refs_2_, f32[16,8,128]{2,1,0:T(8,128)S(1)} %collective-permute-done.9.refs_3_, ...), custom_call_target="tpu_custom_call" | custom-call | tf_op jit(solution)/shard_map/pallas_call | solution.py:95
  (15 shorter events, 0.4 us)
Async XLA Ops:
  0.0 0.8 %copy-start = (f32[8,8,256]{2,1,0:T(8,128)S(1)}, f32[8,8,256]{2,1,0:T(8,128)}, u32[]{:S(2)}) copy-start(f32[8,8,256]{2,1,0:T(8,128)} %c_ref.3) | copy-start | bytes 196612
  0.8 7.4 %copy-start.1 = (f32[8,8,256]{2,1,0:T(8,128)S(1)}, f32[8,8,256]{2,1,0:T(8,128)}, u32[]{:S(2)}) copy-start(f32[8,8,256]{2,1,0:T(8,128)} %f_ref.3) | copy-start | bytes 196612
  0.9 4.5 %collective-permute-start.1 = (f32[7,8,256]{2,1,0:T(8,128)S(1)}, f32[7,8,256]{2,1,0:T(8,128)S(1)}, u32[]{:S(2)}, u32[]{:S(2)}) collective-permute-start(f32[7,8,256]{2,1,0:T(8,128)S(1)} %get-tuple-element.23), channel_id=1, source_target_pairs={{0,1},{1,0},{2,3},{3,2},{4,5},{5,4},{6,7},{7,6},{8,16},{9,17},{10,... | collective-permute-start | bytes 172040 | tf_op jit(solution)/shard_map/ppermute | solution.py:616
  1.4 6.8 %collective-permute-start = (f32[7,8,256]{2,1,0:T(8,128)S(1)}, f32[7,8,256]{2,1,0:T(8,128)S(1)}, u32[]{:S(2)}, u32[]{:S(2)}) collective-permute-start(f32[7,8,256]{2,1,0:T(8,128)S(1)} %get-tuple-element.24), channel_id=1, source_target_pairs={{0,8},{8,0},{16,24},{24,16},{1,9},{9,1},{17,25},{25,17},{2,10},{10... | collective-permute-start | bytes 172040 | tf_op jit(solution)/shard_map/ppermute | solution.py:615
  8.3 4.5 %collective-permute-start.2 = (f32[10,8,256]{2,1,0:T(8,128)S(1)}, f32[10,8,256]{2,1,0:T(8,128)S(1)}, u32[]{:S(2)}, u32[]{:S(2)}) collective-permute-start(f32[10,8,256]{2,1,0:T(8,128)S(1)} %get-tuple-element.14), channel_id=1, source_target_pairs={{0,8},{1,2},{2,1},{3,4},{4,3},{5,6},{6,5},{7,15},{8,0},{9,10},{10,... | collective-permute-start | bytes 245768 | tf_op jit(solution)/shard_map/ppermute | solution.py:627
  9.6 3.1 %collective-permute-start.3 = (f32[10,8,256]{2,1,0:T(8,128)S(1)}, f32[10,8,256]{2,1,0:T(8,128)S(1)}, u32[]{:S(2)}, u32[]{:S(2)}) collective-permute-start(f32[10,8,256]{2,1,0:T(8,128)S(1)} %get-tuple-element.15), channel_id=1, source_target_pairs={{0,1},{1,0},{2,3},{3,2},{4,5},{5,4},{6,7},{7,6},{8,9},{9,8},{10,11... | collective-permute-start | bytes 245768 | tf_op jit(solution)/shard_map/ppermute | solution.py:626
  13.5 5.1 %collective-permute-start.6 = (f32[4,8,128]{2,1,0:T(8,128)S(1)}, f32[4,8,128]{2,1,0:T(8,128)S(1)}, u32[]{:S(2)}, u32[]{:S(2)}) collective-permute-start(f32[4,8,128]{2,1,0:T(8,128)S(1)} %get-tuple-element.16.refs_0_), channel_id=1, source_target_pairs={{0,7},{1,6},{2,5},{3,4},{4,3},{5,2},{6,1},{7,0},{8,15},{9,14},{10,... | collective-permute-start | bytes 49160 | tf_op jit(solution)/shard_map/ppermute | solution.py:641
  14.2 4.4 %collective-permute-start.5 = (f32[4,8,128]{2,1,0:T(8,128)S(1)}, f32[4,8,128]{2,1,0:T(8,128)S(1)}, u32[]{:S(2)}, u32[]{:S(2)}) collective-permute-start(f32[4,8,128]{2,1,0:T(8,128)S(1)} %get-tuple-element.16.refs_0_), channel_id=1, source_target_pairs={{0,5},{1,4},{2,7},{3,6},{4,1},{5,0},{6,3},{7,2},{8,13},{9,12},{10,... | collective-permute-start | bytes 49160 | tf_op jit(solution)/shard_map/ppermute | solution.py:641
  15.7 3.2 %collective-permute-start.4 = (f32[4,8,128]{2,1,0:T(8,128)S(1)}, f32[4,8,128]{2,1,0:T(8,128)S(1)}, u32[]{:S(2)}, u32[]{:S(2)}) collective-permute-start(f32[4,8,128]{2,1,0:T(8,128)S(1)} %get-tuple-element.16.refs_0_), channel_id=1, source_target_pairs={{0,3},{1,2},{2,1},{3,0},{4,7},{5,6},{6,5},{7,4},{8,11},{9,10},{10,... | collective-permute-start | bytes 49160 | tf_op jit(solution)/shard_map/ppermute | solution.py:641
  18.9 5.2 %collective-permute-start.9 = (f32[16,8,128]{2,1,0:T(8,128)S(1)}, f32[16,8,128]{2,1,0:T(8,128)S(1)}, u32[]{:S(2)}, u32[]{:S(2)}) collective-permute-start(f32[16,8,128]{2,1,0:T(8,128)S(1)} %shard_map.30.refs_0_), channel_id=1, source_target_pairs={{0,24},{1,25},{2,26},{3,27},{4,28},{5,29},{6,30},{7,31},{8,16},{9,... | collective-permute-start | bytes 196616 | tf_op jit(solution)/shard_map/ppermute | solution.py:647
  20.5 5.5 %collective-permute-start.8 = (f32[16,8,128]{2,1,0:T(8,128)S(1)}, f32[16,8,128]{2,1,0:T(8,128)S(1)}, u32[]{:S(2)}, u32[]{:S(2)}) collective-permute-start(f32[16,8,128]{2,1,0:T(8,128)S(1)} %shard_map.30.refs_0_), channel_id=1, source_target_pairs={{0,16},{1,17},{2,18},{3,19},{4,20},{5,21},{6,22},{7,23},{8,24},{9,... | collective-permute-start | bytes 196616 | tf_op jit(solution)/shard_map/ppermute | solution.py:647
  21.7 4.6 %collective-permute-start.7 = (f32[16,8,128]{2,1,0:T(8,128)S(1)}, f32[16,8,128]{2,1,0:T(8,128)S(1)}, u32[]{:S(2)}, u32[]{:S(2)}) collective-permute-start(f32[16,8,128]{2,1,0:T(8,128)S(1)} %shard_map.30.refs_0_), channel_id=1, source_target_pairs={{0,8},{1,9},{2,10},{3,11},{4,12},{5,13},{6,14},{7,15},{8,0},{9,1},... | collective-permute-start | bytes 196616 | tf_op jit(solution)/shard_map/ppermute | solution.py:647
  22.4 4.1 %collective-permute-start.10 = (f32[16,8,128]{2,1,0:T(8,128)S(1)}, f32[16,8,128]{2,1,0:T(8,128)S(1)}, u32[]{:S(2)}, u32[]{:S(2)}) collective-permute-start(f32[16,8,128]{2,1,0:T(8,128)S(1)} %shard_map.30.refs_0_), channel_id=1, source_target_pairs={{0,1},{1,0},{2,3},{3,2},{4,5},{5,4},{6,7},{7,6},{8,9},{9,8},{10,11... | collective-permute-start | bytes 196616 | tf_op jit(solution)/shard_map/ppermute | solution.py:650
  24.1 2.4 %collective-permute-start.13 = (f32[16,8,128]{2,1,0:T(8,128)S(1)}, f32[16,8,128]{2,1,0:T(8,128)S(1)}, u32[]{:S(2)}, u32[]{:S(2)}) collective-permute-start(f32[16,8,128]{2,1,0:T(8,128)S(1)} %collective-permute-done.9.refs_3_), channel_id=1, source_target_pairs={{0,1},{1,0},{2,3},{3,2},{4,5},{5,4},{6,7},{7,6},{8,9},{9,8},{10,11... | collective-permute-start | bytes 196616 | tf_op jit(solution)/shard_map/ppermute | solution.py:650
  26.0 1.3 %collective-permute-start.12 = (f32[16,8,128]{2,1,0:T(8,128)S(1)}, f32[16,8,128]{2,1,0:T(8,128)S(1)}, u32[]{:S(2)}, u32[]{:S(2)}) collective-permute-start(f32[16,8,128]{2,1,0:T(8,128)S(1)} %collective-permute-done.8.refs_2_), channel_id=1, source_target_pairs={{0,1},{1,0},{2,3},{3,2},{4,5},{5,4},{6,7},{7,6},{8,9},{9,8},{10,11... | collective-permute-start | bytes 196616 | tf_op jit(solution)/shard_map/ppermute | solution.py:650
  26.3 1.3 %collective-permute-start.11 = (f32[16,8,128]{2,1,0:T(8,128)S(1)}, f32[16,8,128]{2,1,0:T(8,128)S(1)}, u32[]{:S(2)}, u32[]{:S(2)}) collective-permute-start(f32[16,8,128]{2,1,0:T(8,128)S(1)} %collective-permute-done.7.refs_1_), channel_id=1, source_target_pairs={{0,1},{1,0},{2,3},{3,2},{4,5},{5,4},{6,7},{7,6},{8,9},{9,8},{10,11... | collective-permute-start | bytes 196616 | tf_op jit(solution)/shard_map/ppermute | solution.py:650
